TPU v7x, 256 devices: a whole 4x4x8 slice. The times are simulated.
256 devices in a mesh: dp: 16 (over y, x_lo, core), seq: 16 (over x_hi, z).
Axes of the slice: x: 4 (x_hi: 2, x_lo: 2; x = x_hi * 2 + x_lo), y: 4, z: 8, core: 2. Of those that a mesh axis runs over, the one named last changes fastest.
Arguments:
- tokens: bfloat16 [16, 2048, 4096], P('dp', 'seq'), may hold values from -100 to 100
- query_weight: bfloat16 [4096, 4096], P('dp', 'seq'), may hold values from -0.09375 to 0.09375
- key_weight: bfloat16 [4096, 4096], P('dp', 'seq'), may hold values from -0.09375 to 0.09375
- value_weight: bfloat16 [4096, 4096], P('dp', 'seq'), may hold values from -0.09375 to 0.09375
- log_decay: float32 [16, 32, 2048], P('dp', 'seq'), may hold values from -0.75 to 0
Outputs:
- mixed: bfloat16 [16, 2048, 4096], P('dp', 'seq')
All inputs are finite; a program needn't handle non-finite values.
Results may differ from a plain program's by a relative error of at most 0.0073.
Values may be sent and summed in bfloat16 or wider, within the bound.
No kernel may reach another device: no remote copies, remote signals or barrier semaphores. Data moves between devices by JAX's collectives and lax.ppermute only.
A program may use at most 128 MiB of HBM per device.

v0:
```python
import jax
import jax.numpy as jnp
from jax import lax
from jax.sharding import PartitionSpec as P

BLOCK = 256


def lightning(query, keys_in, values_in, log_decay, block_rows):
    length, head_count, head_width = query.shape
    block_count = length // block_rows
    queries = query.reshape(block_count, block_rows, head_count, head_width)
    keys_all = keys_in.reshape(block_count, block_rows, head_count, head_width)
    values_all = values_in.reshape(block_count, block_rows, head_count, head_width)
    log_gates = log_decay.reshape(head_count, block_count, block_rows).transpose(1, 0, 2)
    within = jnp.cumsum(log_gates, axis=-1)
    positions = jnp.arange(block_rows)
    causal = positions[:, None] >= positions[None, :]

    def advance(memory, blocks):
        query_block, key_block, value_block, decay_block = blocks
        scores = jnp.einsum(
            "thd,shd->hts", query_block, key_block, preferred_element_type=jnp.float32
        )
        weights = jnp.where(
            causal[None], jnp.exp(decay_block[:, :, None] - decay_block[:, None, :]), 0.0
        )
        weighted = (scores * weights).astype(jnp.bfloat16)
        local_part = jnp.einsum(
            "hts,shd->thd", weighted, value_block, preferred_element_type=jnp.float32
        )
        scaled_query = (
            query_block.astype(jnp.float32) * jnp.exp(decay_block).T[:, :, None]
        ).astype(jnp.bfloat16)
        carried = jnp.einsum(
            "thd,hde->the",
            scaled_query,
            memory.astype(jnp.bfloat16),
            preferred_element_type=jnp.float32,
        )
        block_total = decay_block[:, -1]
        fading = jnp.exp(block_total[:, None] - decay_block).T[:, :, None]
        faded_keys = (key_block.astype(jnp.float32) * fading).astype(jnp.bfloat16)
        update = jnp.einsum(
            "shd,she->hde", faded_keys, value_block, preferred_element_type=jnp.float32
        )
        memory = jnp.exp(block_total)[:, None, None] * memory + update
        return (memory, local_part + carried)

    initial = jnp.zeros((head_count, head_width, head_width), jnp.float32)
    final_memory, blocks_out = lax.scan(advance, initial, (queries, keys_all, values_all, within))
    attended = blocks_out.reshape(length, head_count, head_width)
    inverse_rms = lax.rsqrt(jnp.mean(attended * attended, axis=-1, keepdims=True) + 1e-06)
    return (attended * inverse_rms).astype(jnp.bfloat16).reshape(length, head_count * head_width)


def normalize_rows(token_rows):
    values_f = token_rows.astype(jnp.float32)
    inverse_rms = lax.rsqrt(jnp.mean(values_f * values_f, axis=-1, keepdims=True) + 1e-05)
    return (values_f * inverse_rms).astype(jnp.bfloat16)


def shards(tokens, query_weight, key_weight, value_weight, log_decay):
    query_cols, key_cols, value_cols = (
        lax.all_gather(query_weight, "dp", axis=0, tiled=True),
        lax.all_gather(key_weight, "dp", axis=0, tiled=True),
        lax.all_gather(value_weight, "dp", axis=0, tiled=True),
    )
    columns = query_cols.shape[1]
    own_rows = tokens[0]
    gathered = lax.all_gather(own_rows, "seq", axis=0, tiled=True)
    shard_rows = gathered
    shard_rows = normalize_rows(shard_rows)
    queries = jax.nn.silu(
        jnp.dot(shard_rows, query_cols, preferred_element_type=jnp.float32)
    ).astype(jnp.bfloat16)
    keys_part = jax.nn.silu(
        jnp.dot(shard_rows, key_cols, preferred_element_type=jnp.float32)
    ).astype(jnp.bfloat16)
    values_part = jnp.dot(shard_rows, value_cols, preferred_element_type=jnp.float32).astype(
        jnp.bfloat16
    )
    packed = jnp.concatenate((queries, keys_part, values_part), axis=1)
    length = packed.shape[0]
    head_count = log_decay.shape[1]
    head_width = columns // head_count
    shaped = (length, head_count, head_width)
    query = packed[:, :columns].reshape(shaped)
    keys_rows = packed[:, columns : 2 * columns].reshape(shaped)
    values_rows = packed[:, 2 * columns :].reshape(shaped)
    mixed_heads = lightning(query, keys_rows, values_rows, log_decay[0], BLOCK)
    regrouped = lax.all_to_all(mixed_heads, "seq", split_axis=0, concat_axis=1, tiled=True)
    return regrouped[None]


def solution(mesh):
    placed = (
        P("dp", "seq", None),
        P("dp", "seq"),
        P("dp", "seq"),
        P("dp", "seq"),
        P("dp", "seq", None),
    )
    return jax.shard_map(
        shards, mesh=mesh, in_specs=placed, out_specs=P("dp", "seq", None), check_vma=False
    )
```

profile of v0, /device:TPU:1, one launch (start us, length us, event | category | flops | bytes accessed | tf_op | source)
XLA Modules:
  0.0 454.4 jit_solution(3681263972709339640)
XLA Ops:
  6.5 0.7 all-gather.12.cloned.1.call-update
  7.3 0.7 all-gather.8.cloned.1.call-update
  8.1 0.7 all-gather.10.cloned.1.call-update
  9.3 0.7 copy_bitcast_fusion.11
  10.1 1.1 reduce-window.6
  11.5 1.4 copy.71
  12.8 225.6 %all-gather.12.cloned.1.call-done = bf16[1,2048,4096]{2,1,0:T(8,128)(2,1)} async-done(((bf16[1,128,4096]{2,1,0:T(8,128)(2,1)}), bf16[1,2048,4096]{2,1,0:T(8,128)(2,1)}) %all-gather.12.cloned.1.call-update) | async-done | bytes 16777232 | tf_op jit(solution)/shard_map/all_gather | solution.py:71
  238.4 7.2 %fusion.22 = f32[2048]{0:T(1024)S(1)} fusion(bf16[1,2048,4096]{2,1,0:T(8,128)(2,1)} %all-gather.12.cloned.1.call-done), kind=kLoop, calls=%fused_computation.40 | loop fusion | flops 25163776 | bytes 16785408 | tf_op jit(solution)/shard_map/reduce_sum | solution.py:59
  245.6 28.8 %all-gather.8.cloned.1.call-done = bf16[4096,256]{1,0:T(8,128)(2,1)} async-done(((bf16[256,256]{1,0:T(8,128)(2,1)}), bf16[4096,256]{1,0:T(8,128)(2,1)}) %all-gather.8.cloned.1.call-update) | async-done | bytes 2097168 | tf_op jit(solution)/shard_map/all_gather | solution.py:67
  274.4 12.3 %convolution_convert_fusion = bf16[2048,256]{1,0:T(8,128)(2,1)} fusion(bf16[4096,256]{1,0:T(8,128)(2,1)} %all-gather.8.cloned.1.call-done, bf16[1,2048,4096]{2,1,0:T(8,128)(2,1)} %all-gather.12.cloned.1.call-done, f32[2048]{0:T(1024)S(1)} %add_rsqrt_fusion.1), kind=kOutput, calls=%fused_computation.42 | convolution fusion | flops 4320657408 | bytes 19931136 | tf_op jit(solution)/shard_map/dot_general | solution.py:80
  286.7 2.2 reshape_reshape.10
  288.9 24.0 %all-gather.10.cloned.1.call-done = bf16[4096,256]{1,0:T(8,128)(2,1)} async-done(((bf16[256,256]{1,0:T(8,128)(2,1)}), bf16[4096,256]{1,0:T(8,128)(2,1)}) %all-gather.10.cloned.1.call-update) | async-done | bytes 2097168 | tf_op jit(solution)/shard_map/all_gather | solution.py:65
  312.8 12.5 %multiply_convert_fusion.4 = bf16[2048,256]{1,0:T(8,128)(2,1)} fusion(bf16[4096,256]{1,0:T(8,128)(2,1)} %all-gather.10.cloned.1.call-done, bf16[1,2048,4096]{2,1,0:T(8,128)(2,1)} %all-gather.12.cloned.1.call-done, f32[2048]{0:T(1024)S(1)} %add_rsqrt_fusion.1), kind=kOutput, calls=%fused_computation.46 | convolution fusion | flops 4322754560 | bytes 19931136 | tf_op jit(solution)/shard_map/dot_general | solution.py:75
  325.4 2.2 reshape_reshape.11
  327.6 23.5 %all-gather.6.cloned.1.call-done = bf16[4096,256]{1,0:T(8,128)(2,1)} async-done(((bf16[256,256]{1,0:T(8,128)(2,1)}), bf16[4096,256]{1,0:T(8,128)(2,1)}) %all-gather.6.cloned.1.call-update) | async-done | bytes 2097168 | tf_op jit(solution)/shard_map/all_gather | solution.py:66
  351.1 12.6 %multiply_convert_fusion.5 = bf16[2048,256]{1,0:T(8,128)(2,1)} fusion(bf16[4096,256]{1,0:T(8,128)(2,1)} %all-gather.6.cloned.1.call-done, bf16[1,2048,4096]{2,1,0:T(8,128)(2,1)} %all-gather.12.cloned.1.call-done, f32[2048]{0:T(1024)S(1)} %add_rsqrt_fusion.1), kind=kOutput, calls=%fused_computation.47 | convolution fusion | flops 4322754560 | bytes 19931136 | tf_op jit(solution)/shard_map/dot_general | solution.py:78
  363.7 2.1 reshape_reshape.9
  365.8 36.4 %while.13 = (s32[]{:T(128)}, f32[2,128,128]{2,1,0:T(8,128)S(1)}, f32[8,256,2,128]{1,3,2,0:T(8,128)S(1)}, f32[8,2,256]{1,2,0:T(8,128)}, bf16[8,256,2,128]{3,2,1,0...) while((s32[]{:T(128)}, f32[2,128,128]{2,1,0:T(8,128)S(1)}, ...), condition=%wide.region_4.5_spmd.clone, body=%wide.region_3.4_spmd.clone.sunk | while | flops 101843456 | bytes 2914472 | solution.py:51
  365.8 1.1 constant_dynamic-slice_fusion.6
  367.0 0.9 exponential_bitcast_fusion.4
  368.4 1.0 constant_dynamic-slice_fusion.5
  370.4 1.2 constant_dynamic-slice_fusion.6
  371.5 0.9 exponential_bitcast_fusion.4
  372.9 1.0 constant_dynamic-slice_fusion.5
  374.9 1.2 constant_dynamic-slice_fusion.6
  376.1 0.9 exponential_bitcast_fusion.4
  377.5 1.0 constant_dynamic-slice_fusion.5
  379.5 1.2 constant_dynamic-slice_fusion.6
  380.6 0.9 exponential_bitcast_fusion.4
  382.0 1.0 constant_dynamic-slice_fusion.5
  384.0 1.2 constant_dynamic-slice_fusion.6
  385.2 0.9 exponential_bitcast_fusion.4
  386.6 1.0 constant_dynamic-slice_fusion.5
  388.6 1.2 constant_dynamic-slice_fusion.6
  389.7 0.9 exponential_bitcast_fusion.4
  391.1 1.0 constant_dynamic-slice_fusion.5
  393.1 1.2 constant_dynamic-slice_fusion.6
  394.3 0.9 exponential_bitcast_fusion.4
  395.7 1.0 constant_dynamic-slice_fusion.5
  397.7 1.2 constant_dynamic-slice_fusion.6
  398.8 0.9 exponential_bitcast_fusion.4
  400.2 1.0 constant_dynamic-slice_fusion.5
  402.4 2.5 copy.65
  405.2 1.7 copy.78
  407.3 1.4 reshape.61
  408.7 2.5 fusion.24
  411.5 35.1 %all_to_all.13 = bf16[16,128,256]{1,2,0:T(8,128)(2,1)S(1)} all-to-all(bf16[16,128,256]{1,2,0:T(8,128)(2,1)S(1)} %copy.66), channel_id=1, replica_groups=mesh['dp'=16,'seq'=16] {'seq'}, dimensions={0} | all-to-all | bytes 2097152 | tf_op jit(solution)/shard_map/all_to_all | solution.py:92
  446.6 1.3 copy.67
  (100 shorter events, 13.1 us)
Async XLA Ops:
  6.5 231.9 %all-gather.12.cloned.1.call-start = ((), (), s32[]{:S(2)}) async-start(), calls=%async_computation.4 | async-start | bytes 17825792 | tf_op jit(solution)/shard_map/all_gather | solution.py:71
  7.3 267.2 %all-gather.8.cloned.1.call-start = ((), (), s32[]{:S(2)}) async-start(), calls=%async_computation.2 | async-start | bytes 2228224 | tf_op jit(solution)/shard_map/all_gather | solution.py:67
  8.0 304.8 %all-gather.10.cloned.1.call-start = ((), (), s32[]{:S(2)}) async-start(), calls=%async_computation.3 | async-start | bytes 2228224 | tf_op jit(solution)/shard_map/all_gather | solution.py:65
  8.7 342.4 %all-gather.6.cloned.1.call-start = ((), (), s32[]{:S(2)}) async-start(), calls=%async_computation.1 | async-start | bytes 2228224 | tf_op jit(solution)/shard_map/all_gather | solution.py:66
  405.2 2.2 copy-start
Sparse Core Ops, SparseCore 0:
  9.9 228.4 all-gather.11
  240.3 34.0 all-gather.7
  276.3 36.5 all-gather.9
  314.6 36.5 all-gather.5
where the time goes:
time: 456 us; the launch traced here: 454 us
  waiting for transfers between devices  304 us (67%)
  matrix products  46.1 us (10%)
  local copies, waits for them, and re-layouts  43.3 us (9%)
  blocking collectives  35.1 us (8%)
  between operations  13.2 us (3%)
  other arithmetic  11.6 us (3%)
    all_gather x1, waiting for transfers between devices, shards(): gathered = lax.all_gather(own_rows, 'seq', axis=0, tiled=True)  226 us
    all_to_all x1, blocking collectives, shards(): lax.all_to_all(mixed_heads, 'seq', split_axis=0, concat_axis=1, tiled=True)  35.1 us
    all_gather x1, waiting for transfers between devices, shards(): lax.all_gather(value_weight, 'dp', axis=0, tiled=True)  28.8 us
    all_gather x1, waiting for transfers between devices, shards(): lax.all_gather(query_weight, 'dp', axis=0, tiled=True)  24 us
    all_gather x1, waiting for transfers between devices, shards(): lax.all_gather(key_weight, 'dp', axis=0, tiled=True)  23.5 us
    dynamic_slice x16, local copies, waits for them, and re-layouts, lightning(): lax.scan(advance, initial, (queries, keys_all, values_all, within))  17.3 us
    dot_general x1, matrix products, shards(): jnp.dot(shard_rows, key_cols, preferred_element_type=jnp.float32)  12.6 us
    dot_general x1, matrix products, shards(): jnp.dot(shard_rows, query_cols, preferred_element_type=jnp.float32)  12.5 us
  transfers between devices with their start and end apart: 4, of which 4 were waited for; matrix products, arithmetic and copies ran while one was open for 9% of the time, Pallas kernels for 0%

commit v1 on v0

v1 whole, which is shorter than its diff:
```python
import jax
import jax.numpy as jnp
from jax import lax
from jax.experimental import pallas as pl
from jax.experimental.pallas import tpu as pltpu
from jax.sharding import Mesh, PartitionSpec as P

BLOCK = 256
DH = 128
SHAPE = (4, 2, 2, 2, 8)
NAMES = ("y", "xl", "c", "xh", "z")
X_INDEX = (0, 2, 1, 3)


def ring_y(value, step):
    return lax.ppermute(value, "y", [(i, (i + step) % 4) for i in range(4)])


def ring_x(value, step):
    return lax.ppermute(
        value, ("xl", "xh"), [(X_INDEX[i], X_INDEX[(i + step) % 4]) for i in range(4)]
    )


def swap_core(value):
    return lax.ppermute(value, "c", [(0, 1), (1, 0)])


def swap_half(value):
    return lax.ppermute(value, "xh", [(0, 1), (1, 0)])


def swap_roles(value):
    return lax.ppermute(value, ("c", "xh"), [(0, 0), (1, 2), (2, 1), (3, 3)])


def normalize_rows(token_rows):
    values_f = token_rows.astype(jnp.float32)
    inverse_rms = lax.rsqrt(jnp.mean(values_f * values_f, axis=-1, keepdims=True) + 1e-05)
    return (values_f * inverse_rms).astype(jnp.bfloat16)


def around(value, ring, axis):
    one, three = ring(value, 1), ring(value, -1)
    half = value.shape[axis] // 2
    first = lax.slice_in_dim(one, 0, half, axis=axis)
    second = lax.slice_in_dim(three, half, 2 * half, axis=axis)
    two = jnp.concatenate((ring(first, 1), ring(second, -1)), axis=axis)
    return jnp.stack((value, one, two, three))


def project_kernel(place_ref, rows_ref, weight_ref, *rest):
    out_ref = rest[-1]
    rows = rows_ref[0].reshape(rows_ref.shape[1] * rows_ref.shape[2], rows_ref.shape[3])
    for part in range(3):
        product = jnp.dot(
            rows, weight_ref[:, part * 256 : (part + 1) * 256], preferred_element_type=jnp.float32
        )
        if part < 2:
            product = product / (1.0 + jnp.exp(-product))
        out_ref[0, 0, :, :, part * 256 : (part + 1) * 256] = product.astype(jnp.bfloat16).reshape(
            out_ref.shape[2], out_ref.shape[3], 256
        )


def project(place, rows, weight, previous=None):
    group, width = 4, weight.shape[1]
    in_specs = [
        pl.BlockSpec((1, group, 64, rows.shape[3]), lambda i, j, place: (i, j, 0, 0)),
        pl.BlockSpec(weight.shape, lambda i, j, place: (0, 0)),
    ]
    operands = [rows, weight]
    aliases = {}
    if previous is not None:
        in_specs.append(pl.BlockSpec(memory_space=pl.ANY))
        operands.append(previous)
        aliases = {3: 0}
    return pl.pallas_call(
        project_kernel,
        out_shape=jax.ShapeDtypeStruct((2, 2, 8, 64, width), jnp.bfloat16),
        grid_spec=pltpu.PrefetchScalarGridSpec(
            num_scalar_prefetch=1,
            grid=(2, 8 // group),
            in_specs=in_specs,
            out_specs=pl.BlockSpec(
                (1, 1, group, 64, width), lambda i, j, place: (place[0], i, j, 0, 0)
            ),
        ),
        input_output_aliases=aliases,
        compiler_params=pltpu.CompilerParams(vmem_limit_bytes=48 << 20),
        cost_estimate=pl.CostEstimate(
            flops=2 * 1024 * 4096 * 768, bytes_accessed=16 << 20, transcendentals=0
        ),
        name="project",
    )(place, *operands)


def attend_kernel(qkv_ref, row_ref, column_ref, out_ref, state_ref):
    @pl.when(pl.program_id(0) == 0)
    def _():
        state_ref[...] = jnp.zeros_like(state_ref)

    def rows_of(start):
        part = qkv_ref[0, :, :, :, start : start + DH]
        return jnp.concatenate(
            [part[core, chunk] for chunk in range(2) for core in range(2)], axis=0
        )

    later = lax.broadcasted_iota(jnp.int32, (BLOCK, BLOCK), 0)
    earlier = lax.broadcasted_iota(jnp.int32, (BLOCK, BLOCK), 1)
    causal = later >= earlier
    for head in range(2):
        query = rows_of(head * DH)
        keys = rows_of(256 + head * DH)
        values = rows_of(512 + head * DH)
        g_row = row_ref[0, head : head + 1, :]
        g_column = column_ref[0, :, head : head + 1]
        total = g_row[:, BLOCK - 1 :]
        scores = lax.dot_general(
            query, keys, (((1,), (1,)), ((), ())), preferred_element_type=jnp.float32
        )
        weights = jnp.exp(jnp.where(causal, g_column - g_row, -jnp.inf))
        weighted = (scores * weights).astype(jnp.bfloat16)
        scaled_query = (query.astype(jnp.float32) * jnp.exp(g_column)).astype(jnp.bfloat16)
        state = state_ref[head]
        attended = jnp.dot(weighted, values, preferred_element_type=jnp.float32) + jnp.dot(
            scaled_query, state.astype(jnp.bfloat16), preferred_element_type=jnp.float32
        )
        faded_keys = (keys.astype(jnp.float32) * jnp.exp(total - g_column)).astype(jnp.bfloat16)
        update = lax.dot_general(
            faded_keys, values, (((0,), (0,)), ((), ())), preferred_element_type=jnp.float32
        )
        state_ref[head] = jnp.exp(total) * state + update
        inverse_rms = lax.rsqrt(jnp.mean(attended * attended, axis=-1, keepdims=True) + 1e-06)
        mixed = (attended * inverse_rms).astype(jnp.bfloat16)
        out_ref[:, :, head * DH : (head + 1) * DH] = mixed.reshape(2, BLOCK // 2, DH)


def attend(qkv, row, column):
    return pl.pallas_call(
        attend_kernel,
        out_shape=jax.ShapeDtypeStruct((16, 128, 256), jnp.bfloat16),
        grid_spec=pltpu.PrefetchScalarGridSpec(
            num_scalar_prefetch=0,
            grid=(8,),
            in_specs=[
                pl.BlockSpec((1, 2, 2, 64, 768), lambda i: (i // 4, 0, i % 4, 0, 0)),
                pl.BlockSpec((1, 2, BLOCK), lambda i: (i, 0, 0)),
                pl.BlockSpec((1, BLOCK, 2), lambda i: (i, 0, 0)),
            ],
            out_specs=pl.BlockSpec((2, 128, 256), lambda i: (i, 0, 0)),
            scratch_shapes=[pltpu.VMEM((2, DH, DH), jnp.float32)],
        ),
        compiler_params=pltpu.CompilerParams(vmem_limit_bytes=48 << 20),
        cost_estimate=pl.CostEstimate(
            flops=16 * 50_331_648, bytes_accessed=4 << 20, transcendentals=0
        ),
        name="attend",
    )(qkv, row, column)


def gather_weight(weight):
    y, half = lax.axis_index("y"), lax.axis_index("xh")
    x = half * 2 + lax.axis_index("xl")
    own = swap_roles(weight)
    by_row = own.reshape(2, 128, own.shape[1])
    first = around(around(by_row[0], ring_y, 0), ring_x, 1)
    second = around(around(by_row[1], ring_x, 0), ring_y, 1)
    both = jnp.stack((first.transpose(1, 0, 2, 3), second))
    order_y = jnp.mod(y - jnp.arange(4), 4)
    order_x = jnp.mod(x - jnp.arange(4), 4)
    both = jnp.take(jnp.take(both, order_y, axis=1), order_x, axis=2)
    both = both.reshape(2, 4, 2, 2, 128, weight.shape[1]).transpose(1, 3, 2, 0, 4, 5)
    return both.reshape(4096, weight.shape[1])


def shards(tokens, query_weight, key_weight, value_weight, log_decay):
    core, half = lax.axis_index("c"), lax.axis_index("xh")
    on_place = core == half
    normed = normalize_rows(tokens[0]).reshape(2, 64, 4096)
    kept = lax.dynamic_index_in_dim(normed, core, 0, keepdims=False)
    given = lax.dynamic_index_in_dim(normed, 1 - core, 0, keepdims=False)
    got = swap_core(given)
    staying = jnp.where(on_place, kept, got)
    leaving = jnp.where(on_place, got, kept)
    arrived = swap_half(leaving)
    near = lax.all_gather(staying, ("c", "z"), axis=0, tiled=False).reshape(2, 8, 64, 4096)
    far = lax.all_gather(arrived, ("c", "z"), axis=0, tiled=False).reshape(2, 8, 64, 4096)

    weight = gather_weight(jnp.concatenate((query_weight, key_weight, value_weight), axis=1))
    decay = swap_roles(log_decay[0])
    g = jnp.cumsum(decay.reshape(2, 8, BLOCK), axis=-1)
    row, column = g.transpose(1, 0, 2), g.transpose(1, 2, 0)

    place = half.astype(jnp.int32).reshape(1)
    qkv = project(place, near, weight)
    qkv = project(1 - place, far, weight, qkv)
    mixed = attend(qkv, row, column)
    spread = lax.all_to_all(mixed, ("c", "z"), split_axis=0, concat_axis=0, tiled=True)
    spread = swap_roles(spread)
    return spread.transpose(1, 0, 2).reshape(1, 128, 4096)


def solution(mesh):
    inner = Mesh(mesh.devices.reshape(SHAPE), NAMES)
    rows, lanes = ("y", "xl", "c"), ("xh", "z")
    placed = (
        P(rows, lanes, None),
        P(rows, lanes),
        P(rows, lanes),
        P(rows, lanes),
        P(rows, lanes, None),
    )
    return jax.shard_map(
        shards, mesh=inner, in_specs=placed, out_specs=P(rows, lanes, None), check_vma=False
    )
```

time: 456 us -> 225 us (0.49)
  waiting for transfers between devices: 304 us -> 51.5 us
  matrix products: 46.1 us -> 0 us
  starting transfers between devices: 0.12 us -> 38.1 us
  Pallas kernels: 0 us -> 31.1 us
  local copies, waits for them, and re-layouts: 43.3 us -> 25.7 us
  other arithmetic: 11.6 us -> 27.4 us
    all_gather x4 -> x2, waiting for transfers between devices: 302 us -> 0.01 us  [the longest x1 0.01 us: shards(): lax.all_gather(staying, ('c', 'z'), axis=0, tiled=False)]
    ppermute x0 -> x21, waiting for transfers between devices: none -> 51.4 us  [the longest x3 23.2 us: swap_roles(): return lax.ppermute(value, ('c', 'xh'), [(0, 0), (1, 2), (2, 1), (3, 3)])]
    dot_general x27 -> x0, matrix products: 46.1 us -> none  [the longest x1 12.6 us: shards(): jnp.dot(shard_rows, key_cols, preferred_element_type=jnp.float32)]
    ppermute x0 -> x21, starting transfers between devices: none -> 38.1 us  [the longest x3 14.3 us: swap_roles(): return lax.ppermute(value, ('c', 'xh'), [(0, 0), (1, 2), (2, 1), (3, 3)])]
    pallas_call x0 -> x3, Pallas kernels: none -> 31.1 us  [the longest x2 21.6 us: project(): pl.pallas_call(project_kernel, out_shape=jax.ShapeDtypeStruct((2, 2, 8, 6...]
    dynamic_slice x16 -> x0, local copies, waits for them, and re-layouts: 17.3 us -> none  [lightning(): lax.scan(advance, initial, (queries, keys_all, values_all, within))]
    select_n x0 -> x5, other arithmetic: none -> 13.3 us  [the longest x4 12.4 us: gather_weight(): both = jnp.take(jnp.take(both, order_y, axis=1), order_x, axis=2)]
    gather x0 -> x2, local copies, waits for them, and re-layouts: none -> 13.1 us  [gather_weight(): both = jnp.take(jnp.take(both, order_y, axis=1), order_x, axis=2)]
  transfers between devices with their start and end apart: 4 -> 23, of which waited for: 4 -> 9; matrix products, arithmetic and copies ran while one was open for 9% -> 19% of each run, Pallas kernels for 0% -> 5%
where the time goes in v1:
time: 225 us; the launch traced here: 224 us
  waiting for transfers between devices  51.5 us (23%)
  starting transfers between devices  38.1 us (17%)
  blocking collectives  36.7 us (16%)
  Pallas kernels  31.1 us (14%)
  other arithmetic  27.4 us (12%)
  local copies, waits for them, and re-layouts  25.7 us (11%)
  between operations  13.7 us (6%)
    all_to_all x1, blocking collectives, shards(): lax.all_to_all(mixed, ('c', 'z'), split_axis=0, concat_axis=0, tiled=True)  36.7 us
    ppermute x3, waiting for transfers between devices, swap_roles(): return lax.ppermute(value, ('c', 'xh'), [(0, 0), (1, 2), (2, 1), (3, 3)])  23.2 us
    pallas_call x2, Pallas kernels, project(): pl.pallas_call(project_kernel, out_shape=jax.ShapeDtypeStruct((2, 2, 8, 6...  21.6 us
    ppermute x3, starting transfers between devices, swap_roles(): return lax.ppermute(value, ('c', 'xh'), [(0, 0), (1, 2), (2, 1), (3, 3)])  14.3 us
    ppermute x1, waiting for transfers between devices, swap_half(): return lax.ppermute(value, 'xh', [(0, 1), (1, 0)])  13.6 us
    gather x2, local copies, waits for them, and re-layouts, gather_weight(): both = jnp.take(jnp.take(both, order_y, axis=1), order_x, axis=2)  13.1 us
    select_n x4, other arithmetic, gather_weight(): both = jnp.take(jnp.take(both, order_y, axis=1), order_x, axis=2)  12.4 us
    ppermute x8, starting transfers between devices, ring_y(): return lax.ppermute(value, 'y', [(i, (i + step) % 4) for i in range(4)])  10.9 us
  transfers between devices with their start and end apart: 23, of which 9 were waited for; matrix products, arithmetic and copies ran while one was open for 19% of the time, Pallas kernels for 5%

profile of v1, /device:TPU:1, one launch (start us, length us, event | category | flops | bytes accessed | tf_op | source)
XLA Modules:
  0.0 224.2 jit_solution(1511634529509839221)
XLA Ops:
  6.5 1.5 multiply_reduce_fusion
  8.2 1.5 multiply_convert_fusion
  9.7 3.3 %collective-permute-start = (bf16[64,4096]{1,0:T(8,128)(2,1)S(1)}, bf16[64,4096]{1,0:T(8,128)(2,1)S(1)}, u32[]{:S(2)}, u32[]{:S(2)}) collective-permute-start(bf16[64,4096]{1,0:T(8,128)(2,1)S(1)} %dynamic-slice_bitcast_fusion), channel_id=1, source_target_pairs={{0,16},{16,0},{1,17},{17,1},{2,18},{18,2},{3,19},{19,3},{4,20},{20... | collective-permute-start | bytes 1572872 | tf_op jit(solution)/shard_map/ppermute | solution.py:26
  13.1 1.5 collective-permute-done
  14.6 0.9 bitcast_select_fusion
  15.6 1.1 collective-permute-start.1
  16.7 13.6 %collective-permute-done.1 = bf16[64,4096]{1,0:T(8,128)(2,1)S(1)} collective-permute-done((bf16[64,4096]{1,0:T(8,128)(2,1)S(1)}, bf16[64,4096]{1,0:T(8,128)(2,1)S(1)}, u32[]{:S(2)}, u32[]{:S(2)}) %collective-permute-start.1) | collective-permute-done | bytes 524320 | tf_op jit(solution)/shard_map/ppermute | solution.py:30
  30.3 0.9 copy-done.4
  31.3 4.0 %collective-permute-start.2 = (bf16[256,768]{1,0:T(8,128)(2,1)S(1)}, bf16[256,768]{1,0:T(8,128)(2,1)S(1)}, u32[]{:S(2)}, u32[]{:S(2)}) collective-permute-start(bf16[256,768]{1,0:T(8,128)(2,1)S(1)} %pad_maximum_fusion.3), channel_id=1, source_target_pairs={{0,0},{8,16},{16,8},{24,24},{1,1},{9,17},{17,9},{25,25},{2,2},{10,... | collective-permute-start | bytes 1179656 | tf_op jit(solution)/shard_map/ppermute | solution.py:34
  35.3 8.7 %collective-permute-done.2 = bf16[256,768]{1,0:T(8,128)(2,1)S(1)} collective-permute-done((bf16[256,768]{1,0:T(8,128)(2,1)S(1)}, bf16[256,768]{1,0:T(8,128)(2,1)S(1)}, u32[]{:S(2)}, u32[]{:S(2)}) %collective-permute-start.2) | collective-permute-done | bytes 393248 | tf_op jit(solution)/shard_map/ppermute | solution.py:34
  44.2 2.6 %collective-permute-start.5 = (bf16[128,768]{1,0:T(8,128)(2,1)S(1)}, bf16[128,768]{1,0:T(8,128)(2,1)S(1)}, u32[]{:S(2)}, u32[]{:S(2)}) collective-permute-start(bf16[128,768]{1,0:T(8,128)(2,1)S(1)} %get-tuple-element.14), channel_id=1, source_target_pairs={{0,192},{64,0},{128,64},{192,128},{1,193},{65,1},{129,65},{193,129... | collective-permute-start | bytes 589832 | tf_op jit(solution)/shard_map/ppermute | solution.py:16
  46.8 2.7 %collective-permute-start.13 = (bf16[128,768]{1,0:T(8,128)(2,1)S(1)}, bf16[128,768]{1,0:T(8,128)(2,1)S(1)}, u32[]{:S(2)}, u32[]{:S(2)}) collective-permute-start(bf16[128,768]{1,0:T(8,128)(2,1)S(1)} %get-tuple-element.13), channel_id=1, source_target_pairs={{0,40},{32,0},{8,32},{40,8},{1,41},{33,1},{9,33},{41,9},{2,42},{34... | collective-permute-start | bytes 589832 | tf_op jit(solution)/shard_map/ppermute | solution.py:20
  49.5 0.8 collective-permute-done.3
  50.4 2.7 %collective-permute-start.6 = (bf16[64,768]{1,0:T(8,128)(2,1)S(1)}, bf16[64,768]{1,0:T(8,128)(2,1)S(1)}, u32[]{:S(2)}, u32[]{:S(2)}) collective-permute-start(bf16[64,768]{1,0:T(8,128)(2,1)S(1)} %slice.62), channel_id=1, source_target_pairs={{0,192},{64,0},{128,64},{192,128},{1,193},{65,1},{129,65},{193,129... | collective-permute-start | bytes 294920 | tf_op jit(solution)/shard_map/ppermute | solution.py:16
  53.3 2.7 %collective-permute-start.14 = (bf16[64,768]{1,0:T(8,128)(2,1)S(1)}, bf16[64,768]{1,0:T(8,128)(2,1)S(1)}, u32[]{:S(2)}, u32[]{:S(2)}) collective-permute-start(bf16[64,768]{1,0:T(8,128)(2,1)S(1)} %slice.67), channel_id=1, source_target_pairs={{0,40},{32,0},{8,32},{40,8},{1,41},{33,1},{9,33},{41,9},{2,42},{34... | collective-permute-start | bytes 294920 | tf_op jit(solution)/shard_map/ppermute | solution.py:20
  56.0 1.0 fusion.7
  57.1 1.4 collective-permute-start.7
  58.5 1.0 fusion.6
  60.1 2.1 collective-permute-start.17
  62.2 7.2 %collective-permute-start.19 = (f32[2,2048]{1,0:T(2,128)S(1)}, f32[2,2048]{1,0:T(2,128)S(1)}, u32[]{:S(2)}, u32[]{:S(2)}) collective-permute-start(f32[2,2048]{1,0:T(2,128)S(1)} %bitcast.82), channel_id=1, source_target_pairs={{0,0},{8,16},{16,8},{24,24},{1,1},{9,17},{17,9},{25,25},{2,2},{10,... | collective-permute-start | bytes 49160 | tf_op jit(solution)/shard_map/ppermute | solution.py:34
  69.5 7.3 %collective-permute-done.9 = bf16[4,128,768]{2,1,0:T(8,128)(2,1)S(1)} collective-permute-done((bf16[4,128,768]{2,1,0:T(8,128)(2,1)}, bf16[4,128,768]{2,1,0:T(8,128)(2,1)S(1)}, u32[]{:S(2)}, u32[]{:S(2)}) %collective-permute-start.9) | collective-permute-done | bytes 786464 | tf_op jit(solution)/shard_map/ppermute | solution.py:20
  76.8 0.8 slice.64
  77.6 0.8 slice.63
  78.4 1.5 collective-permute-start.8
  80.0 1.2 reduce-window.6
  81.1 1.8 slice.68
  82.9 1.8 slice.69
  84.7 2.7 %collective-permute-start.18 = (bf16[4,64,768]{2,1,0:T(8,128)(2,1)}, bf16[4,64,768]{2,1,0:T(8,128)(2,1)}, u32[]{:S(2)}, u32[]{:S(2)}) collective-permute-start(bf16[4,64,768]{2,1,0:T(8,128)(2,1)} %slice.69), channel_id=1, source_target_pairs={{0,192},{64,0},{128,64},{192,128},{1,193},{65,1},{129,65},{193,129... | collective-permute-start | bytes 1179656 | tf_op jit(solution)/shard_map/ppermute | solution.py:16
  88.7 1.2 maximum_bitcast_fusion.2
  89.8 3.9 %collective-permute-done.16 = bf16[4,64,768]{2,1,0:T(8,128)(2,1)} collective-permute-done((bf16[4,64,768]{2,1,0:T(8,128)(2,1)}, bf16[4,64,768]{2,1,0:T(8,128)(2,1)}, u32[]{:S(2)}, u32[]{:S(2)}) %collective-permute-start.16) | collective-permute-done | bytes 393248 | tf_op jit(solution)/shard_map/ppermute | solution.py:16
  93.8 0.7 collective-permute-done.18
  94.5 1.2 maximum_bitcast_fusion.3
  96.1 1.6 maximum_bitcast_fusion.1
  97.7 3.3 %pad_maximum_fusion = bf16[2,4,4,128,768]{4,3,2,1,0:T(8,128)(2,1)} fusion(bf16[1,4,4,128,768]{4,3,2,1,0:T(8,128)(2,1)S(1)} %maximum_bitcast_fusion.1, bf16[1,4,4,128,768]{4,3,2,1,0:T(8,128)(2,1)S(1)} %maximum_bitcast_fusion), kind=kLoop, calls=%fused_computation.2 | loop fusion | flops 3145728 | bytes 12582912 | tf_op jit(solution)/shard_map/stack | solution.py:169
  101.0 6.5 %gather_fusion = bf16[4,2,4,128,768]{4,3,2,1,0:T(8,128)(2,1)} fusion(bf16[2,4,4,128,768]{4,3,2,1,0:T(8,128)(2,1)} %pad_maximum_fusion, s32[1024]{0:T(1024)S(1)} %pad_clamp_fusion.1), kind=kCustom, calls=%fused_computation | custom fusion | bytes 12582928 | tf_op jit(solution)/shard_map/jit(_take)/gather | solution.py:172
  107.5 6.2 %select_bitcast_fusion = bf16[2,4,4,128,768]{4,3,2,0,1:T(8,128)(2,1)} fusion(bf16[4,2,4,128,768]{4,3,2,1,0:T(8,128)(2,1)} %gather_fusion, pred[4]{0:T(512)(128)(4,1)S(1)} %compare_and_fusion), kind=kLoop, calls=%fused_computation.4 | loop fusion | flops 3145728 | bytes 12582916 | tf_op jit(solution)/shard_map/jit(_take)/select_n | solution.py:172
  113.6 6.6 %gather_fusion.1 = bf16[4,2,4,128,768]{4,3,1,2,0:T(8,128)(2,1)} fusion(bf16[2,4,4,128,768]{4,3,2,0,1:T(8,128)(2,1)} %select_bitcast_fusion, s32[1024]{0:T(1024)S(1)} %pad_clamp_fusion), kind=kCustom, calls=%fused_computation.1 | custom fusion | bytes 12582928 | tf_op jit(solution)/shard_map/jit(_take)/gather | solution.py:172
  120.2 6.2 %copy_select_fusion = bf16[2,4,2,2,128,768]{5,4,0,2,3,1:T(8,128)(2,1)} fusion(bf16[2,4,2,2,128,768]{5,4,0,1,3,2:T(8,128)(2,1)} %bitcast.68, pred[2,2]{0,1:T(4,128)(4,1)S(1)} %compare_and_fusion.1), kind=kLoop, calls=%fused_computation.3 | loop fusion | flops 3145728 | bytes 12582916 | tf_op jit(solution)/shard_map/jit(_take)/select_n | solution.py:172
  126.4 10.8 %project.2.rest_0_ = bf16[2,2,8,64,768]{4,3,2,1,0:T(8,128)(2,1)S(1)} custom-call(s32[1]{0:T(128)} %bitcast.place_ref, bf16[2,8,64,4096]{3,2,1,0:T(8,128)(2,1)} %bitcast.80, bf16[4096,768]{1,0:T(8,128)(2,1)} %bitcast.69), custom_call_target="tpu_custom_call" | custom-call | flops 6442450944 | bytes 16777216 | tf_op jit(solution)/shard_map/project/pallas_call | solution.py:78
  137.2 1.6 copy-done
  138.9 1.9 copy-done.1
  140.7 10.8 %project.3.qkv_ref = bf16[2,2,8,64,768]{4,3,2,1,0:T(8,128)(2,1)S(1)} custom-call(s32[1]{0:T(128)S(6)} %sub.45.place_ref, bf16[2,8,64,4096]{3,2,1,0:T(8,128)(2,1)} %bitcast.81, bf16[4096,768]{1,0:T(8,128)(2,1)} %bitcast.70, bf16[2,2,8,64,768]{4,3,2,1,0:T(8,128)(2,1)S(1)} %copy-done.1), custom_call_target="tpu_custom_call", output_to_operand_aliasing={{}: (3, {})} | custom-call | flops 6442450944 | bytes 16777216 | tf_op jit(solution)/shard_map/project/pallas_call | solution.py:78
  151.5 9.5 %attend.1 = bf16[16,128,256]{2,1,0:T(8,128)(2,1)S(1)} custom-call(bf16[2,2,8,64,768]{4,3,2,1,0:T(8,128)(2,1)S(1)} %project.3.qkv_ref, f32[8,2,256]{2,1,0:T(2,128)S(1)} %copy.20.row_ref, f32[8,256,2]{2,1,0:T(8,128)S(1)} %bitcast.67), custom_call_target="tpu_custom_call" | custom-call | flops 805306368 | bytes 4194304 | tf_op jit(solution)/shard_map/attend/pallas_call | solution.py:140
  161.0 36.7 %all_to_all.5 = bf16[16,128,256]{2,1,0:T(8,128)(2,1)S(1)} all-to-all(bf16[16,128,256]{2,1,0:T(8,128)(2,1)S(1)} %attend.1), channel_id=1, replica_groups=mesh['y'=4,'xl'=2,'c'=2,'xh'=2,'z'=8] {'c','z'}, dimensions={0} | all-to-all | bytes 2097152 | tf_op jit(solution)/shard_map/all_to_all | solution.py:199
  197.8 3.1 %collective-permute-start.20 = (bf16[16,128,256]{2,1,0:T(8,128)(2,1)S(1)}, bf16[16,128,256]{2,1,0:T(8,128)(2,1)S(1)}, u32[]{:S(2)}, u32[]{:S(2)}) collective-permute-start(bf16[16,128,256]{2,1,0:T(8,128)(2,1)S(1)} %all_to_all.5), channel_id=1, source_target_pairs={{0,0},{8,16},{16,8},{24,24},{1,1},{9,17},{17,9},{25,25},{2,2},{10,... | collective-permute-start | bytes 3145736 | tf_op jit(solution)/shard_map/ppermute | solution.py:34
  200.9 14.5 %collective-permute-done.20 = bf16[16,128,256]{2,1,0:T(8,128)(2,1)S(1)} collective-permute-done((bf16[16,128,256]{2,1,0:T(8,128)(2,1)S(1)}, bf16[16,128,256]{2,1,0:T(8,128)(2,1)S(1)}, u32[]{:S(2)}, u32[]{:S(2)}) %collective-permute-start.20) | collective-permute-done | bytes 1048608 | tf_op jit(solution)/shard_map/ppermute | solution.py:34
  215.4 0.7 copy.21
  216.1 1.3 copy.22
  (68 shorter events, 3.2 us)
Async XLA Ops:
  6.5 119.9 %all-gather.7.cloned.1.call-start = ((), (), s32[]{:S(2)}) async-start(), calls=%async_computation.2 | async-start | bytes 8912896 | tf_op jit(solution)/shard_map/all_gather | solution.py:187
  8.1 23.1 %copy-start.5 = (bf16[256,256]{1,0:T(8,128)(2,1)S(1)}, bf16[256,256]{1,0:T(8,128)(2,1)}, u32[]{:S(2)}) copy-start(bf16[256,256]{1,0:T(8,128)(2,1)} %param.8) | copy-start | bytes 393220
  8.2 23.1 %copy-start.6 = (bf16[256,256]{1,0:T(8,128)(2,1)S(1)}, bf16[256,256]{1,0:T(8,128)(2,1)}, u32[]{:S(2)}) copy-start(bf16[256,256]{1,0:T(8,128)(2,1)} %param.7) | copy-start | bytes 393220
  8.2 23.1 %copy-start.7 = (bf16[256,256]{1,0:T(8,128)(2,1)S(1)}, bf16[256,256]{1,0:T(8,128)(2,1)}, u32[]{:S(2)}) copy-start(bf16[256,256]{1,0:T(8,128)(2,1)} %param.6) | copy-start | bytes 393220
  9.7 4.9 %collective-permute-start = (bf16[64,4096]{1,0:T(8,128)(2,1)S(1)}, bf16[64,4096]{1,0:T(8,128)(2,1)S(1)}, u32[]{:S(2)}, u32[]{:S(2)}) collective-permute-start(bf16[64,4096]{1,0:T(8,128)(2,1)S(1)} %dynamic-slice_bitcast_fusion), channel_id=1, source_target_pairs={{0,16},{16,0},{1,17},{17,1},{2,18},{18,2},{3,19},{19,3},{4,20},{20... | collective-permute-start | bytes 1572872 | tf_op jit(solution)/shard_map/ppermute | solution.py:26
  15.5 123.3 %all-gather.5.cloned.1.call-start = ((), (), s32[]{:S(2)}) async-start(), calls=%async_computation.1 | async-start | bytes 8912896 | tf_op jit(solution)/shard_map/all_gather | solution.py:188
  15.6 14.7 %collective-permute-start.1 = (bf16[64,4096]{1,0:T(8,128)(2,1)S(1)}, bf16[64,4096]{1,0:T(8,128)(2,1)S(1)}, u32[]{:S(2)}, u32[]{:S(2)}) collective-permute-start(bf16[64,4096]{1,0:T(8,128)(2,1)S(1)} %get-tuple-element.6), channel_id=1, source_target_pairs={{0,8},{8,0},{1,9},{9,1},{2,10},{10,2},{3,11},{11,3},{4,12},{12,4},... | collective-permute-start | bytes 1572872 | tf_op jit(solution)/shard_map/ppermute | solution.py:30
  30.3 0.9 copy-start.4
  31.3 12.8 %collective-permute-start.2 = (bf16[256,768]{1,0:T(8,128)(2,1)S(1)}, bf16[256,768]{1,0:T(8,128)(2,1)S(1)}, u32[]{:S(2)}, u32[]{:S(2)}) collective-permute-start(bf16[256,768]{1,0:T(8,128)(2,1)S(1)} %pad_maximum_fusion.3), channel_id=1, source_target_pairs={{0,0},{8,16},{16,8},{24,24},{1,1},{9,17},{17,9},{25,25},{2,2},{10,... | collective-permute-start | bytes 1179656 | tf_op jit(solution)/shard_map/ppermute | solution.py:34
  44.1 6.2 %collective-permute-start.3 = (bf16[128,768]{1,0:T(8,128)(2,1)S(1)}, bf16[128,768]{1,0:T(8,128)(2,1)S(1)}, u32[]{:S(2)}, u32[]{:S(2)}) collective-permute-start(bf16[128,768]{1,0:T(8,128)(2,1)S(1)} %get-tuple-element.14), channel_id=1, source_target_pairs={{0,64},{64,128},{128,192},{192,0},{1,65},{65,129},{129,193},{193,1... | collective-permute-start | bytes 589832 | tf_op jit(solution)/shard_map/ppermute | solution.py:16
  44.2 6.1 %collective-permute-start.5 = (bf16[128,768]{1,0:T(8,128)(2,1)S(1)}, bf16[128,768]{1,0:T(8,128)(2,1)S(1)}, u32[]{:S(2)}, u32[]{:S(2)}) collective-permute-start(bf16[128,768]{1,0:T(8,128)(2,1)S(1)} %get-tuple-element.14), channel_id=1, source_target_pairs={{0,192},{64,0},{128,64},{192,128},{1,193},{65,1},{129,65},{193,129... | collective-permute-start | bytes 589832 | tf_op jit(solution)/shard_map/ppermute | solution.py:16
  46.8 15.4 %copy-start.8 = (f32[1,2,2048]{2,1,0:T(2,128)S(1)}, f32[1,2,2048]{2,1,0:T(2,128)}, u32[]{:S(2)}) copy-start(f32[1,2,2048]{2,1,0:T(2,128)} %param.9) | copy-start | bytes 49156
  46.8 6.3 %collective-permute-start.11 = (bf16[128,768]{1,0:T(8,128)(2,1)S(1)}, bf16[128,768]{1,0:T(8,128)(2,1)S(1)}, u32[]{:S(2)}, u32[]{:S(2)}) collective-permute-start(bf16[128,768]{1,0:T(8,128)(2,1)S(1)} %get-tuple-element.13), channel_id=1, source_target_pairs={{0,32},{32,8},{8,40},{40,0},{1,33},{33,9},{9,41},{41,1},{2,34},{34... | collective-permute-start | bytes 589832 | tf_op jit(solution)/shard_map/ppermute | solution.py:20
  46.8 6.4 %collective-permute-start.13 = (bf16[128,768]{1,0:T(8,128)(2,1)S(1)}, bf16[128,768]{1,0:T(8,128)(2,1)S(1)}, u32[]{:S(2)}, u32[]{:S(2)}) collective-permute-start(bf16[128,768]{1,0:T(8,128)(2,1)S(1)} %get-tuple-element.13), channel_id=1, source_target_pairs={{0,40},{32,0},{8,32},{40,8},{1,41},{33,1},{9,33},{41,9},{2,42},{34... | collective-permute-start | bytes 589832 | tf_op jit(solution)/shard_map/ppermute | solution.py:20
  50.3 5.7 %collective-permute-start.4 = (bf16[64,768]{1,0:T(8,128)(2,1)S(1)}, bf16[64,768]{1,0:T(8,128)(2,1)S(1)}, u32[]{:S(2)}, u32[]{:S(2)}) collective-permute-start(bf16[64,768]{1,0:T(8,128)(2,1)S(1)} %slice.61), channel_id=1, source_target_pairs={{0,64},{64,128},{128,192},{192,0},{1,65},{65,129},{129,193},{193,1... | collective-permute-start | bytes 294920 | tf_op jit(solution)/shard_map/ppermute | solution.py:16
  50.4 5.6 %collective-permute-start.6 = (bf16[64,768]{1,0:T(8,128)(2,1)S(1)}, bf16[64,768]{1,0:T(8,128)(2,1)S(1)}, u32[]{:S(2)}, u32[]{:S(2)}) collective-permute-start(bf16[64,768]{1,0:T(8,128)(2,1)S(1)} %slice.62), channel_id=1, source_target_pairs={{0,192},{64,0},{128,64},{192,128},{1,193},{65,1},{129,65},{193,129... | collective-permute-start | bytes 294920 | tf_op jit(solution)/shard_map/ppermute | solution.py:16
  53.2 5.4 %collective-permute-start.12 = (bf16[64,768]{1,0:T(8,128)(2,1)S(1)}, bf16[64,768]{1,0:T(8,128)(2,1)S(1)}, u32[]{:S(2)}, u32[]{:S(2)}) collective-permute-start(bf16[64,768]{1,0:T(8,128)(2,1)S(1)} %slice.66), channel_id=1, source_target_pairs={{0,32},{32,8},{8,40},{40,0},{1,33},{33,9},{9,41},{41,1},{2,34},{34... | collective-permute-start | bytes 294920 | tf_op jit(solution)/shard_map/ppermute | solution.py:20
  53.3 5.2 %collective-permute-start.14 = (bf16[64,768]{1,0:T(8,128)(2,1)S(1)}, bf16[64,768]{1,0:T(8,128)(2,1)S(1)}, u32[]{:S(2)}, u32[]{:S(2)}) collective-permute-start(bf16[64,768]{1,0:T(8,128)(2,1)S(1)} %slice.67), channel_id=1, source_target_pairs={{0,40},{32,0},{8,32},{40,8},{1,41},{33,1},{9,33},{41,9},{2,42},{34... | collective-permute-start | bytes 294920 | tf_op jit(solution)/shard_map/ppermute | solution.py:20
  57.0 19.8 %collective-permute-start.9 = (bf16[4,128,768]{2,1,0:T(8,128)(2,1)}, bf16[4,128,768]{2,1,0:T(8,128)(2,1)S(1)}, u32[]{:S(2)}, u32[]{:S(2)}) collective-permute-start(bf16[4,128,768]{2,1,0:T(8,128)(2,1)} %get-tuple-element.8), channel_id=1, source_target_pairs={{0,40},{32,0},{8,32},{40,8},{1,41},{33,1},{9,33},{41,9},{2,42},{34... | collective-permute-start | bytes 2359304 | tf_op jit(solution)/shard_map/ppermute | solution.py:20
  57.1 20.5 %collective-permute-start.7 = (bf16[4,128,768]{2,1,0:T(8,128)(2,1)}, bf16[4,128,768]{2,1,0:T(8,128)(2,1)S(1)}, u32[]{:S(2)}, u32[]{:S(2)}) collective-permute-start(bf16[4,128,768]{2,1,0:T(8,128)(2,1)} %get-tuple-element.8), channel_id=1, source_target_pairs={{0,32},{32,8},{8,40},{40,0},{1,33},{33,9},{9,41},{41,1},{2,34},{34... | collective-permute-start | bytes 2359304 | tf_op jit(solution)/shard_map/ppermute | solution.py:20
  59.5 21.6 %collective-permute-start.15 = (bf16[4,128,768]{2,1,0:T(8,128)(2,1)}, bf16[4,128,768]{2,1,0:T(8,128)(2,1)}, u32[]{:S(2)}, u32[]{:S(2)}) collective-permute-start(bf16[4,128,768]{2,1,0:T(8,128)(2,1)} %get-tuple-element.10), channel_id=1, source_target_pairs={{0,64},{64,128},{128,192},{192,0},{1,65},{65,129},{129,193},{193,1... | collective-permute-start | bytes 2359304 | tf_op jit(solution)/shard_map/ppermute | solution.py:16
  60.1 22.8 %collective-permute-start.17 = (bf16[4,128,768]{2,1,0:T(8,128)(2,1)}, bf16[4,128,768]{2,1,0:T(8,128)(2,1)}, u32[]{:S(2)}, u32[]{:S(2)}) collective-permute-start(bf16[4,128,768]{2,1,0:T(8,128)(2,1)} %get-tuple-element.10), channel_id=1, source_target_pairs={{0,192},{64,0},{128,64},{192,128},{1,193},{65,1},{129,65},{193,129... | collective-permute-start | bytes 2359304 | tf_op jit(solution)/shard_map/ppermute | solution.py:16
  62.2 17.7 %collective-permute-start.19 = (f32[2,2048]{1,0:T(2,128)S(1)}, f32[2,2048]{1,0:T(2,128)S(1)}, u32[]{:S(2)}, u32[]{:S(2)}) collective-permute-start(f32[2,2048]{1,0:T(2,128)S(1)} %bitcast.82), channel_id=1, source_target_pairs={{0,0},{8,16},{16,8},{24,24},{1,1},{9,17},{17,9},{25,25},{2,2},{10,... | collective-permute-start | bytes 49160 | tf_op jit(solution)/shard_map/ppermute | solution.py:34
  77.6 10.7 %collective-permute-start.10 = (bf16[4,64,768]{2,1,0:T(8,128)(2,1)}, bf16[4,64,768]{2,1,0:T(8,128)(2,1)}, u32[]{:S(2)}, u32[]{:S(2)}) collective-permute-start(bf16[4,64,768]{2,1,0:T(8,128)(2,1)} %slice.64), channel_id=1, source_target_pairs={{0,40},{32,0},{8,32},{40,8},{1,41},{33,1},{9,33},{41,9},{2,42},{34... | collective-permute-start | bytes 1179656 | tf_op jit(solution)/shard_map/ppermute | solution.py:20
  77.6 10.0 %copy-start.2 = (bf16[4,128,768]{2,1,0:T(8,128)(2,1)}, bf16[4,128,768]{2,1,0:T(8,128)(2,1)S(1)}, u32[]{:S(2)}) copy-start(bf16[4,128,768]{2,1,0:T(8,128)(2,1)S(1)} %collective-permute-done.7) | copy-start | bytes 2359300
  78.4 10.2 %collective-permute-start.8 = (bf16[4,64,768]{2,1,0:T(8,128)(2,1)}, bf16[4,64,768]{2,1,0:T(8,128)(2,1)}, u32[]{:S(2)}, u32[]{:S(2)}) collective-permute-start(bf16[4,64,768]{2,1,0:T(8,128)(2,1)} %slice.63), channel_id=1, source_target_pairs={{0,32},{32,8},{8,40},{40,0},{1,33},{33,9},{9,41},{41,1},{2,34},{34... | collective-permute-start | bytes 1179656 | tf_op jit(solution)/shard_map/ppermute | solution.py:20
  82.9 10.9 %collective-permute-start.16 = (bf16[4,64,768]{2,1,0:T(8,128)(2,1)}, bf16[4,64,768]{2,1,0:T(8,128)(2,1)}, u32[]{:S(2)}, u32[]{:S(2)}) collective-permute-start(bf16[4,64,768]{2,1,0:T(8,128)(2,1)} %slice.68), channel_id=1, source_target_pairs={{0,64},{64,128},{128,192},{192,0},{1,65},{65,129},{129,193},{193,1... | collective-permute-start | bytes 1179656 | tf_op jit(solution)/shard_map/ppermute | solution.py:16
  84.7 9.8 %collective-permute-start.18 = (bf16[4,64,768]{2,1,0:T(8,128)(2,1)}, bf16[4,64,768]{2,1,0:T(8,128)(2,1)}, u32[]{:S(2)}, u32[]{:S(2)}) collective-permute-start(bf16[4,64,768]{2,1,0:T(8,128)(2,1)} %slice.69), channel_id=1, source_target_pairs={{0,192},{64,0},{128,64},{192,128},{1,193},{65,1},{129,65},{193,129... | collective-permute-start | bytes 1179656 | tf_op jit(solution)/shard_map/ppermute | solution.py:16
  88.3 7.3 %copy-start.3 = (bf16[4,128,768]{2,1,0:T(8,128)(2,1)S(1)}, bf16[4,128,768]{2,1,0:T(8,128)(2,1)}, u32[]{:S(2)}) copy-start(bf16[4,128,768]{2,1,0:T(8,128)(2,1)} %copy-done.2) | copy-start | bytes 2359300
  137.2 1.6 copy-start
  138.9 1.9 copy-start.1
  197.8 17.6 %collective-permute-start.20 = (bf16[16,128,256]{2,1,0:T(8,128)(2,1)S(1)}, bf16[16,128,256]{2,1,0:T(8,128)(2,1)S(1)}, u32[]{:S(2)}, u32[]{:S(2)}) collective-permute-start(bf16[16,128,256]{2,1,0:T(8,128)(2,1)S(1)} %all_to_all.5), channel_id=1, source_target_pairs={{0,0},{8,16},{16,8},{24,24},{1,1},{9,17},{17,9},{25,25},{2,2},{10,... | collective-permute-start | bytes 3145736 | tf_op jit(solution)/shard_map/ppermute | solution.py:34
Sparse Core Ops, SparseCore 0:
  15.6 57.2 all-gather.6
  74.8 54.4 all-gather.4

commit v2 on v1

v2 whole, which is shorter than its diff:
```python
import functools

import jax
import jax.numpy as jnp
from jax import lax
from jax.experimental import pallas as pl
from jax.experimental.pallas import tpu as pltpu
from jax.sharding import Mesh, PartitionSpec as P

BLOCK = 256
DH = 128
SHAPE = (4, 2, 2, 2, 8)
NAMES = ("y", "xl", "c", "xh", "z")


def swap_core(value):
    return lax.ppermute(value, "c", [(0, 1), (1, 0)])


def swap_half(value):
    return lax.ppermute(value, "xh", [(0, 1), (1, 0)])


def swap_roles(value):
    return lax.ppermute(value, ("c", "xh"), [(0, 0), (1, 2), (2, 1), (3, 3)])


def normalize_rows(token_rows):
    values_f = token_rows.astype(jnp.float32)
    inverse_rms = lax.rsqrt(jnp.mean(values_f * values_f, axis=-1, keepdims=True) + 1e-05)
    return (values_f * inverse_rms).astype(jnp.bfloat16)


def ring_z(value, step):
    return lax.ppermute(value, "z", [(i, (i + step) % 8) for i in range(8)])


def gather_weight(weight):
    order = [
        ((y * 2 + xl) * 2 + core) * 2 + xh
        for y in range(4)
        for xh in range(2)
        for xl in range(2)
        for core in range(2)
    ]
    whole = lax.all_gather(
        weight, ("y", "xl", "c", "xh"), axis=0, tiled=False, axis_index_groups=[order]
    )
    return whole.reshape(4, 2, 1024, weight.shape[1])


SLOTS = (
    [(0, 0), (1, 0), (0, 1), (0, 7), (0, 2), (0, 6), (1, 1), (1, 7)]
    + [(0, 3), (0, 5), (1, 2), (1, 6), (0, 4), (1, 3), (1, 5), (1, 4)]
)
BATCHES = ((0, 13), (13, 16))


def project_kernel(count, last_group, core_ref, *refs):
    pieces, weight_ref = refs[:count], refs[count]
    outs = refs[count + 1 :]
    group, part = pl.program_id(0), pl.program_id(1)
    rows = jnp.concatenate([piece[...] for piece in pieces], axis=0)
    weight = weight_ref[:, 0].reshape(4096, 256)
    product = jnp.dot(rows, weight, preferred_element_type=jnp.float32)
    gated = product / (1.0 + jnp.exp(-product))
    result = jnp.where(part < 2, gated, product).astype(jnp.bfloat16).reshape(-1, 64, 256)
    if last_group == 0:
        slots = outs[0].shape[0]
        outs[0][...] = result[:slots]
        outs[1][...] = result[slots:]
        return

    @pl.when(group == 0)
    def _():
        outs[0][...] = result

    @pl.when(group == 1)
    def _():
        outs[1][...] = result


def project(core, pieces, weight, both):
    rows = sum(piece.shape[0] for piece in pieces)
    width = weight.shape[3]
    groups = 2 if both else 1
    slots = rows // 64 if both else rows // 128
    out = jax.ShapeDtypeStruct((slots, 64, width), jnp.bfloat16)

    def columns(g, p, core):
        mine = 1 if not both else g
        return 0, mine * core[0] + (1 - mine) * (1 - core[0]), 0, p

    last = pl.BlockSpec((slots, 64, 256), lambda g, p, core: (0, 0, g * p))
    first = pl.BlockSpec((slots, 64, 256), lambda g, p, core: (0, 0, (1 - g) * p + g * 2))
    return pl.pallas_call(
        functools.partial(project_kernel, len(pieces), groups - 1),
        out_shape=(out, out),
        grid_spec=pltpu.PrefetchScalarGridSpec(
            num_scalar_prefetch=1,
            grid=(groups, 3),
            in_specs=[pl.BlockSpec(piece.shape, lambda g, p, core: (0, 0)) for piece in pieces]
            + [pl.BlockSpec((4, 1, 1024, 256), columns)],
            out_specs=[first, last if both else first],
        ),
        compiler_params=pltpu.CompilerParams(vmem_limit_bytes=58 << 20),
        cost_estimate=pl.CostEstimate(
            flops=groups * 2 * rows * 4096 * width,
            bytes_accessed=2 * rows * 8192 + groups * (6 << 20),
            transcendentals=0,
        ),
        name="project",
    )(core, *pieces, weight)


def attend_kernel(chunk_ref, core_ref, *refs):
    batches = len(BATCHES)
    kept, got = refs[:batches], refs[batches : 2 * batches]
    row_ref, column_ref, out_ref, all_ref = refs[2 * batches :]
    core = core_ref[0]
    for batch, (first, last) in enumerate(BATCHES):
        for slot in range(first, last):
            chunk = chunk_ref[slot]
            all_ref[chunk, core] = kept[batch][slot - first]
            all_ref[chunk, 1 - core] = got[batch][slot - first]
    later = lax.broadcasted_iota(jnp.int32, (BLOCK, BLOCK), 0)
    earlier = lax.broadcasted_iota(jnp.int32, (BLOCK, BLOCK), 1)
    causal = later >= earlier
    states = [jnp.zeros((DH, DH), jnp.float32)] * 2
    for step in range(8):
        rows = all_ref[2 * step : 2 * step + 2].reshape(BLOCK, 768)
        results = []
        for head in range(2):
            query = rows[:, head * DH : (head + 1) * DH]
            keys = rows[:, 256 + head * DH : 256 + (head + 1) * DH]
            values = rows[:, 512 + head * DH : 512 + (head + 1) * DH]
            g_row = row_ref[step, head : head + 1, :]
            g_column = column_ref[step, :, head : head + 1]
            total = g_row[:, BLOCK - 1 :]
            scores = lax.dot_general(
                query, keys, (((1,), (1,)), ((), ())), preferred_element_type=jnp.float32
            )
            weights = jnp.exp(jnp.where(causal, g_column - g_row, -jnp.inf))
            weighted = (scores * weights).astype(jnp.bfloat16)
            scaled_query = (query.astype(jnp.float32) * jnp.exp(g_column)).astype(jnp.bfloat16)
            state = states[head]
            attended = jnp.dot(weighted, values, preferred_element_type=jnp.float32) + jnp.dot(
                scaled_query, state.astype(jnp.bfloat16), preferred_element_type=jnp.float32
            )
            faded_keys = (keys.astype(jnp.float32) * jnp.exp(total - g_column)).astype(jnp.bfloat16)
            update = lax.dot_general(
                faded_keys, values, (((0,), (0,)), ((), ())), preferred_element_type=jnp.float32
            )
            states[head] = jnp.exp(total) * state + update
            inverse_rms = lax.rsqrt(jnp.mean(attended * attended, axis=-1, keepdims=True) + 1e-06)
            results.append((attended * inverse_rms).astype(jnp.bfloat16))
        mixed = jnp.concatenate(results, axis=1).reshape(2, BLOCK // 2, 2 * DH)
        out_ref[2 * step : 2 * step + 2] = mixed


def attend(chunks, core, kept, got, row, column):
    vmem = pl.BlockSpec(memory_space=pltpu.VMEM)
    smem = pl.BlockSpec(memory_space=pltpu.SMEM)
    return pl.pallas_call(
        attend_kernel,
        out_shape=jax.ShapeDtypeStruct((16, 128, 256), jnp.bfloat16),
        in_specs=[smem, smem] + [vmem] * (2 * len(BATCHES) + 2),
        out_specs=vmem,
        scratch_shapes=[pltpu.VMEM((16, 2, 64, 768), jnp.bfloat16)],
        compiler_params=pltpu.CompilerParams(vmem_limit_bytes=24 << 20),
        cost_estimate=pl.CostEstimate(
            flops=16 * 50_331_648, bytes_accessed=4 << 20, transcendentals=0
        ),
        name="attend",
    )(chunks, core, *kept, *got, row, column)


def shards(tokens, query_weight, key_weight, value_weight, log_decay):
    core, half, z = lax.axis_index("c"), lax.axis_index("xh"), lax.axis_index("z")
    on_place = core == half
    weight = gather_weight(jnp.concatenate((query_weight, key_weight, value_weight), axis=1))
    normed = normalize_rows(tokens[0]).reshape(2, 64, 4096)
    kept = lax.dynamic_index_in_dim(normed, core, 0, keepdims=False)
    given = lax.dynamic_index_in_dim(normed, 1 - core, 0, keepdims=False)
    got = swap_core(given)
    near = jnp.where(on_place, kept, got)
    far = swap_half(jnp.where(on_place, got, kept))

    decay = swap_roles(log_decay[0])
    g = jnp.cumsum(decay.reshape(2, 8, BLOCK), axis=-1)
    row, column = g.transpose(1, 0, 2), g.transpose(1, 2, 0)

    held = {}
    for kind, mine in enumerate((near, far)):
        held[kind, 0] = (mine,)
        up = down = mine
        for distance in range(1, 4):
            up, down = ring_z(up, 1), ring_z(down, -1)
            held[kind, distance], held[kind, 8 - distance] = (up,), (down,)
        held[kind, 4] = (ring_z(up[:32], 1), ring_z(down[32:], -1))
    place = core.astype(jnp.int32).reshape(1)
    early, late = ([p for at in SLOTS[i:j] for p in held[at]] for i, j in BATCHES)
    for_other, for_me = project(place, early, weight, True)
    late_mine, late_other = project(
        place, late + [swap_core(piece) for piece in late], weight, False
    )
    mine, others = (for_me, late_mine), (swap_core(for_other), late_other)

    chunks = jnp.stack(
        [(half + kind) % 2 * 8 + jnp.mod(z - step, 8) for kind, step in SLOTS]
    ).astype(jnp.int32)
    mixed = attend(chunks, place, mine, others, row, column)

    spread = lax.all_to_all(mixed, ("xh", "z"), split_axis=0, concat_axis=0, tiled=True)
    spread = spread.reshape(2, 8, 128, 256)
    kept = lax.dynamic_index_in_dim(spread, core, 0, keepdims=False)
    got = swap_core(lax.dynamic_index_in_dim(spread, 1 - core, 0, keepdims=False))
    first = jnp.where(core == 0, kept, got)
    second = jnp.where(core == 0, got, kept)
    out = jnp.concatenate((first, second)).transpose(1, 0, 2)
    return out.reshape(1, 128, 4096)


def solution(mesh):
    inner = Mesh(mesh.devices.reshape(SHAPE), NAMES)
    rows, lanes = ("y", "xl", "c"), ("xh", "z")
    placed = (
        P(rows, lanes, None),
        P(rows, lanes),
        P(rows, lanes),
        P(rows, lanes),
        P(rows, lanes, None),
    )
    return jax.shard_map(
        shards, mesh=inner, in_specs=placed, out_specs=P(rows, lanes, None), check_vma=False
    )
```

time: 225 us -> 184 us (0.82)
  other arithmetic: 27.4 us -> 5.22 us
  local copies, waits for them, and re-layouts: 25.7 us -> 5.86 us
  starting transfers between devices: 38.1 us -> 40.8 us
    ppermute x16, waiting for transfers between devices: 13.1 us -> 43.4 us  [ring_z(): return lax.ppermute(value, 'z', [(i, (i + step) % 8) for i in range(8)])]
    ppermute x3 -> x1, waiting for transfers between devices: 23.2 us -> 1.33 us  [swap_roles(): return lax.ppermute(value, ('c', 'xh'), [(0, 0), (1, 2), (2, 1), (3, 3)])]
    select_n x5 -> x2, other arithmetic: 13.3 us -> 0.15 us  [the longest x1 0.07 us: shards(): far = swap_half(jnp.where(on_place, got, kept))]
    gather x2 -> x0, local copies, waits for them, and re-layouts: 13.1 us -> none  [gather_weight(): both = jnp.take(jnp.take(both, order_y, axis=1), order_x, axis=2)]
    ppermute x1, waiting for transfers between devices: 13.6 us -> 2.74 us  [swap_half(): return lax.ppermute(value, 'xh', [(0, 1), (1, 0)])]
    another operation x12 -> x3, other arithmetic: 10.9 us -> 1.26 us  [the longest x3 5.28 us: gather_weight(): both = jnp.stack((first.transpose(1, 0, 2, 3), second))]
    ppermute x3 -> x1, starting transfers between devices: 14.3 us -> 5.11 us  [swap_roles(): return lax.ppermute(value, ('c', 'xh'), [(0, 0), (1, 2), (2, 1), (3, 3)])]
    ppermute x1 -> x7, starting transfers between devices: 3.33 us -> 9.94 us  [swap_core(): return lax.ppermute(value, 'c', [(0, 1), (1, 0)])]
  transfers between devices with their start and end apart: 23 -> 26, of which waited for: 9 -> 12; matrix products, arithmetic and copies ran while one was open for 19% -> 2% of each run, Pallas kernels for 5% -> 13%
where the time goes in v2:
time: 184 us
  waiting for transfers between devices  51.2 us (28%)
  starting transfers between devices  40.8 us (22%)
  blocking collectives  34.7 us (19%)
  Pallas kernels  32.3 us (18%)
  between operations  13.7 us (7%)
  local copies, waits for them, and re-layouts  5.86 us (3%)
  other arithmetic  5.22 us (3%)
    ppermute x16, waiting for transfers between devices, ring_z(): return lax.ppermute(value, 'z', [(i, (i + step) % 8) for i in range(8)])  43.4 us
    all_to_all x1, blocking collectives, shards(): lax.all_to_all(mixed, ('xh', 'z'), split_axis=0, concat_axis=0, tiled=True)  34.7 us
    pallas_call x2, Pallas kernels, project(): pl.pallas_call(functools.partial(project_kernel, len(pieces), groups - 1)...  23.9 us
    ppermute x16, starting transfers between devices, ring_z(): return lax.ppermute(value, 'z', [(i, (i + step) % 8) for i in range(8)])  23 us
    ppermute x7, starting transfers between devices, swap_core(): return lax.ppermute(value, 'c', [(0, 1), (1, 0)])  9.94 us
    pallas_call x1, Pallas kernels, attend(): pl.pallas_call(attend_kernel, out_shape=jax.ShapeDtypeStruct((16, 128, 25...  8.36 us
    ppermute x1, starting transfers between devices, swap_roles(): return lax.ppermute(value, ('c', 'xh'), [(0, 0), (1, 2), (2, 1), (3, 3)])  5.11 us
  transfers between devices with their start and end apart: 26, of which 12 were waited for; matrix products, arithmetic and copies ran while one was open for 2% of the time, Pallas kernels for 13%

profile of v2, /device:TPU:1, one launch (start us, length us, event | category | flops | bytes accessed | tf_op | source)
XLA Modules:
  0.0 183.6 jit_solution(17965979800221266532)
XLA Ops:
  6.5 1.9 %pad_maximum_fusion = bf16[256,768]{1,0:T(8,128)(2,1)} fusion(bf16[256,256]{1,0:T(8,128)(2,1)} %param.8, bf16[256,256]{1,0:T(8,128)(2,1)} %param.7, bf16[256,256]{1,0:T(8,128)(2,1)} %param.6), kind=kLoop, calls=%fused_computation.9 | loop fusion | flops 1179648 | bytes 786432 | tf_op jit(solution)/shard_map/concatenate | solution.py:181
  8.5 1.5 multiply_reduce_fusion
  10.0 0.1 rsqrt.12
  10.1 0.3 multiply_convert_fusion
  10.4 3.3 %collective-permute-start = (bf16[64,4096]{1,0:T(8,128)(2,1)S(1)}, bf16[64,4096]{1,0:T(8,128)(2,1)S(1)}, u32[]{:S(2)}, u32[]{:S(2)}) collective-permute-start(bf16[64,4096]{1,0:T(8,128)(2,1)S(1)} %dynamic-slice_bitcast_fusion.1), channel_id=1, source_target_pairs={{0,16},{16,0},{1,17},{17,1},{2,18},{18,2},{3,19},{19,3},{4,20},{20... | collective-permute-start | bytes 1572872 | tf_op jit(solution)/shard_map/ppermute | solution.py:17
  13.8 1.5 collective-permute-done
  15.5 3.9 %collective-permute-start.3 = (bf16[64,4096]{1,0:T(8,128)(2,1)S(1)}, bf16[64,4096]{1,0:T(8,128)(2,1)S(1)}, u32[]{:S(2)}, u32[]{:S(2)}) collective-permute-start(bf16[64,4096]{1,0:T(8,128)(2,1)S(1)} %get-tuple-element.16.refs_0_), channel_id=1, source_target_pairs={{0,7},{1,0},{2,1},{3,2},{4,3},{5,4},{6,5},{7,6},{8,15},{9,8},{10,9... | collective-permute-start | bytes 1572872 | tf_op jit(solution)/shard_map/ppermute | solution.py:35
  19.4 2.7 %collective-permute-start.1 = (bf16[64,4096]{1,0:T(8,128)(2,1)S(1)}, bf16[64,4096]{1,0:T(8,128)(2,1)S(1)}, u32[]{:S(2)}, u32[]{:S(2)}) collective-permute-start(bf16[64,4096]{1,0:T(8,128)(2,1)S(1)} %get-tuple-element.15), channel_id=1, source_target_pairs={{0,8},{8,0},{1,9},{9,1},{2,10},{10,2},{3,11},{11,3},{4,12},{12,4},... | collective-permute-start | bytes 1572872 | tf_op jit(solution)/shard_map/ppermute | solution.py:21
  22.1 9.3 %collective-permute-done.2.refs_2_ = bf16[64,4096]{1,0:T(8,128)(2,1)S(1)} collective-permute-done((bf16[64,4096]{1,0:T(8,128)(2,1)S(1)}, bf16[64,4096]{1,0:T(8,128)(2,1)S(1)}, u32[]{:S(2)}, u32[]{:S(2)}) %collective-permute-start.2) | collective-permute-done | bytes 524320 | tf_op jit(solution)/shard_map/ppermute | solution.py:35
  31.4 2.7 %collective-permute-start.5 = (bf16[64,4096]{1,0:T(8,128)(2,1)S(1)}, bf16[64,4096]{1,0:T(8,128)(2,1)S(1)}, u32[]{:S(2)}, u32[]{:S(2)}) collective-permute-start(bf16[64,4096]{1,0:T(8,128)(2,1)S(1)} %collective-permute-done.3.refs_3_), channel_id=1, source_target_pairs={{0,7},{1,0},{2,1},{3,2},{4,3},{5,4},{6,5},{7,6},{8,15},{9,8},{10,9... | collective-permute-start | bytes 1572872 | tf_op jit(solution)/shard_map/ppermute | solution.py:35
  34.1 2.7 %collective-permute-done.1.refs_1_ = bf16[64,4096]{1,0:T(8,128)(2,1)S(1)} collective-permute-done((bf16[64,4096]{1,0:T(8,128)(2,1)S(1)}, bf16[64,4096]{1,0:T(8,128)(2,1)S(1)}, u32[]{:S(2)}, u32[]{:S(2)}) %collective-permute-start.1) | collective-permute-done | bytes 524320 | tf_op jit(solution)/shard_map/ppermute | solution.py:21
  36.8 2.7 %collective-permute-start.7 = (bf16[64,4096]{1,0:T(8,128)(2,1)S(1)}, bf16[64,4096]{1,0:T(8,128)(2,1)S(1)}, u32[]{:S(2)}, u32[]{:S(2)}) collective-permute-start(bf16[64,4096]{1,0:T(8,128)(2,1)S(1)} %collective-permute-done.1.refs_1_), channel_id=1, source_target_pairs={{0,7},{1,0},{2,1},{3,2},{4,3},{5,4},{6,5},{7,6},{8,15},{9,8},{10,9... | collective-permute-start | bytes 1572872 | tf_op jit(solution)/shard_map/ppermute | solution.py:35
  39.5 5.8 %collective-permute-done.4.refs_4_ = bf16[64,4096]{1,0:T(8,128)(2,1)S(1)} collective-permute-done((bf16[64,4096]{1,0:T(8,128)(2,1)S(1)}, bf16[64,4096]{1,0:T(8,128)(2,1)S(1)}, u32[]{:S(2)}, u32[]{:S(2)}) %collective-permute-start.4) | collective-permute-done | bytes 524320 | tf_op jit(solution)/shard_map/ppermute | solution.py:35
  45.3 2.7 %collective-permute-start.9 = (bf16[64,4096]{1,0:T(8,128)(2,1)S(1)}, bf16[64,4096]{1,0:T(8,128)(2,1)S(1)}, u32[]{:S(2)}, u32[]{:S(2)}) collective-permute-start(bf16[64,4096]{1,0:T(8,128)(2,1)S(1)} %collective-permute-done.5.refs_5_), channel_id=1, source_target_pairs={{0,7},{1,0},{2,1},{3,2},{4,3},{5,4},{6,5},{7,6},{8,15},{9,8},{10,9... | collective-permute-start | bytes 1572872 | tf_op jit(solution)/shard_map/ppermute | solution.py:35
  48.0 8.6 %collective-permute-done.6.refs_6_ = bf16[64,4096]{1,0:T(8,128)(2,1)S(1)} collective-permute-done((bf16[64,4096]{1,0:T(8,128)(2,1)S(1)}, bf16[64,4096]{1,0:T(8,128)(2,1)S(1)}, u32[]{:S(2)}, u32[]{:S(2)}) %collective-permute-start.6) | collective-permute-done | bytes 524320 | tf_op jit(solution)/shard_map/ppermute | solution.py:35
  56.5 2.7 %collective-permute-start.11 = (bf16[64,4096]{1,0:T(8,128)(2,1)S(1)}, bf16[64,4096]{1,0:T(8,128)(2,1)}, u32[]{:S(2)}, u32[]{:S(2)}) collective-permute-start(bf16[64,4096]{1,0:T(8,128)(2,1)S(1)} %collective-permute-done.7.refs_7_), channel_id=1, source_target_pairs={{0,7},{1,0},{2,1},{3,2},{4,3},{5,4},{6,5},{7,6},{8,15},{9,8},{10,9... | collective-permute-start | bytes 1572872 | tf_op jit(solution)/shard_map/ppermute | solution.py:35
  59.2 8.6 %collective-permute-done.8.refs_8_ = bf16[64,4096]{1,0:T(8,128)(2,1)S(1)} collective-permute-done((bf16[64,4096]{1,0:T(8,128)(2,1)S(1)}, bf16[64,4096]{1,0:T(8,128)(2,1)S(1)}, u32[]{:S(2)}, u32[]{:S(2)}) %collective-permute-start.8) | collective-permute-done | bytes 524320 | tf_op jit(solution)/shard_map/ppermute | solution.py:35
  68.0 2.7 %collective-permute-start.13 = (bf16[32,4096]{1,0:T(8,128)(2,1)S(1)}, bf16[32,4096]{1,0:T(8,128)(2,1)}, u32[]{:S(2)}, u32[]{:S(2)}) collective-permute-start(bf16[32,4096]{1,0:T(8,128)(2,1)S(1)} %slice.25), channel_id=1, source_target_pairs={{0,7},{1,0},{2,1},{3,2},{4,3},{5,4},{6,5},{7,6},{8,15},{9,8},{10,9... | collective-permute-start | bytes 786440 | tf_op jit(solution)/shard_map/ppermute | solution.py:35
  70.7 8.4 %collective-permute-done.10.refs_10_ = bf16[64,4096]{1,0:T(8,128)(2,1)} collective-permute-done((bf16[64,4096]{1,0:T(8,128)(2,1)S(1)}, bf16[64,4096]{1,0:T(8,128)(2,1)}, u32[]{:S(2)}, u32[]{:S(2)}) %collective-permute-start.10) | collective-permute-done | bytes 524320 | tf_op jit(solution)/shard_map/ppermute | solution.py:35
  79.1 2.7 %collective-permute-start.15 = (bf16[64,4096]{1,0:T(8,128)(2,1)}, bf16[64,4096]{1,0:T(8,128)(2,1)S(1)}, u32[]{:S(2)}, u32[]{:S(2)}) collective-permute-start(bf16[64,4096]{1,0:T(8,128)(2,1)} %collective-permute-done.11.refs_11_), channel_id=1, source_target_pairs={{0,7},{1,0},{2,1},{3,2},{4,3},{5,4},{6,5},{7,6},{8,15},{9,8},{10,9... | collective-permute-start | bytes 1572872 | tf_op jit(solution)/shard_map/ppermute | solution.py:35
  81.8 2.8 %collective-permute-done.12.refs_12_ = bf16[32,4096]{1,0:T(8,128)(2,1)S(1)} collective-permute-done((bf16[32,4096]{1,0:T(8,128)(2,1)S(1)}, bf16[32,4096]{1,0:T(8,128)(2,1)S(1)}, u32[]{:S(2)}, u32[]{:S(2)}) %collective-permute-start.12) | collective-permute-done | bytes 262176 | tf_op jit(solution)/shard_map/ppermute | solution.py:35
  84.6 0.7 copy-done.16
  85.4 17.0 %project.2 = (bf16[13,64,768]{2,1,0:T(8,128)(2,1)}, bf16[13,64,768]{2,1,0:T(8,128)(2,1)}) custom-call(s32[1]{0:T(128)} %bitcast.16.core_ref, bf16[64,4096]{1,0:T(8,128)(2,1)} %copy-done.6, bf16[64,4096]{1,0:T(8,128)(2,1)} %copy-done.11, bf16[64,4096]{1,0:T(8,128)(2,1)} %copy-done.9, bf16[64,4096]{1,0:T(8,128)(2,1)} %copy-done.10, ...), custom_call_target="tpu_custom_call" | custom-call | flops 10468982784 | bytes 26214400 | tf_op jit(solution)/shard_map/project/pallas_call | solution.py:96
  102.4 3.0 %collective-permute-start.22 = (bf16[13,64,768]{2,1,0:T(8,128)(2,1)}, bf16[13,64,768]{2,1,0:T(8,128)(2,1)S(1)}, u32[]{:S(2)}, u32[]{:S(2)}) collective-permute-start(bf16[13,64,768]{2,1,0:T(8,128)(2,1)} %get-tuple-element.11), channel_id=1, source_target_pairs={{0,16},{16,0},{1,17},{17,1},{2,18},{18,2},{3,19},{19,3},{4,20},{20... | collective-permute-start | bytes 3833864 | tf_op jit(solution)/shard_map/ppermute | solution.py:17
  105.4 0.1 collective-permute-start.16
  105.5 2.7 %collective-permute-start.17 = (bf16[32,4096]{1,0:T(8,128)(2,1)S(1)}, bf16[32,4096]{1,0:T(8,128)(2,1)}, u32[]{:S(2)}, u32[]{:S(2)}) collective-permute-start(bf16[32,4096]{1,0:T(8,128)(2,1)S(1)} %slice.27), channel_id=1, source_target_pairs={{0,7},{1,0},{2,1},{3,2},{4,3},{5,4},{6,5},{7,6},{8,15},{9,8},{10,9... | collective-permute-start | bytes 786440 | tf_op jit(solution)/shard_map/ppermute | solution.py:35
  108.2 5.1 %collective-permute-start.23 = (f32[2,2048]{1,0:T(2,128)S(1)}, f32[2,2048]{1,0:T(2,128)S(1)}, u32[]{:S(2)}, u32[]{:S(2)}) collective-permute-start(f32[2,2048]{1,0:T(2,128)S(1)} %bitcast.48), channel_id=1, source_target_pairs={{0,0},{8,16},{16,8},{24,24},{1,1},{9,17},{17,9},{25,25},{2,2},{10,... | collective-permute-start | bytes 49160 | tf_op jit(solution)/shard_map/ppermute | solution.py:25
  113.3 0.1 collective-permute-start.18
  113.4 1.3 collective-permute-done.23
  114.8 0.1 stack.67.chunk_ref
  114.9 1.2 reduce-window.6
  116.1 0.6 collective-permute-start.20
  116.7 0.3 collective-permute-start.21
  117.0 0.2 slice_reduce_fusion
  117.3 0.4 copy.13
  117.6 0.3 copy.14.refs_4_
  118.0 0.2 collective-permute-done.20.refs_6_
  118.2 0.4 collective-permute-done.21.refs_7_
  118.6 6.9 %project.3 = (bf16[3,64,768]{2,1,0:T(8,128)(2,1)}, bf16[3,64,768]{2,1,0:T(8,128)(2,1)}) custom-call(s32[1]{0:T(128)} %bitcast.16.core_ref, bf16[64,4096]{1,0:T(8,128)(2,1)} %copy-done.4, bf16[64,4096]{1,0:T(8,128)(2,1)} %copy-done.5, bf16[32,4096]{1,0:T(8,128)(2,1)} %collective-permute-done.16.refs_2_, bf16[32,4096]{1,0:T(8,128)(2,1)} %collective-permute-done.17.refs_3_, ...), custom_call_target="tpu_custom_call" | custom-call | flops 2415919104 | bytes 12582912 | tf_op jit(solution)/shard_map/project/pallas_call | solution.py:96
  125.4 1.0 copy-done.1
  126.4 1.0 copy-done.2
  127.4 8.4 %attend.1 = bf16[16,128,256]{2,1,0:T(8,128)(2,1)S(1)} custom-call(s32[16]{0:T(128)S(1)} %stack.67.chunk_ref, s32[1]{0:T(128)} %bitcast.16.core_ref, bf16[13,64,768]{2,1,0:T(8,128)(2,1)S(1)} %copy-done, bf16[3,64,768]{2,1,0:T(8,128)(2,1)S(1)} %copy-done.1, bf16[13,64,768]{2,1,0:T(8,128)(2,1)S(1)} %collective-permute-done.22.refs_2_, ...), custom_call_target="tpu_custom_call" | custom-call | flops 805306368 | bytes 4194304 | tf_op jit(solution)/shard_map/attend/pallas_call | solution.py:164
  135.7 34.7 %all_to_all.5 = bf16[16,128,256]{2,1,0:T(8,128)(2,1)S(1)} all-to-all(bf16[16,128,256]{2,1,0:T(8,128)(2,1)S(1)} %attend.1), channel_id=1, replica_groups=mesh['y'=4,'xl'=2,'c'=2,'xh'=2,'z'=8] {'xh','z'}, dimensions={0} | all-to-all | bytes 2097152 | tf_op jit(solution)/shard_map/all_to_all | solution.py:214
  170.4 2.7 %collective-permute-start.24 = (bf16[8,128,256]{2,1,0:T(8,128)(2,1)S(1)}, bf16[8,128,256]{2,1,0:T(8,128)(2,1)S(1)}, u32[]{:S(2)}, u32[]{:S(2)}) collective-permute-start(bf16[8,128,256]{2,1,0:T(8,128)(2,1)S(1)} %dynamic-slice_bitcast_fusion), channel_id=1, source_target_pairs={{0,16},{16,0},{1,17},{17,1},{2,18},{18,2},{3,19},{19,3},{4,20},{20... | collective-permute-start | bytes 1572872 | tf_op jit(solution)/shard_map/ppermute | solution.py:17
  173.1 1.5 collective-permute-done.24
  174.7 0.1 maximum_bitcast_fusion
  174.8 0.7 copy.15
  175.5 1.3 copy.16
  (71 shorter events, 0.8 us)
Async XLA Ops:
  6.5 3.6 %copy-start.3 = (bf16[1,128,4096]{2,1,0:T(8,128)(2,1)S(1)}, bf16[1,128,4096]{2,1,0:T(8,128)(2,1)}, u32[]{:S(2)}) copy-start(bf16[1,128,4096]{2,1,0:T(8,128)(2,1)} %param.5) | copy-start | bytes 3145732
  6.5 78.8 %all-gather.3.cloned.1.call-start = ((), (), s32[]{:S(2)}) async-start(), calls=%async_computation.1 | async-start | bytes 12976128 | tf_op jit(solution)/shard_map/all_gather | solution.py:46
  10.4 4.9 %collective-permute-start = (bf16[64,4096]{1,0:T(8,128)(2,1)S(1)}, bf16[64,4096]{1,0:T(8,128)(2,1)S(1)}, u32[]{:S(2)}, u32[]{:S(2)}) collective-permute-start(bf16[64,4096]{1,0:T(8,128)(2,1)S(1)} %dynamic-slice_bitcast_fusion.1), channel_id=1, source_target_pairs={{0,16},{16,0},{1,17},{17,1},{2,18},{18,2},{3,19},{19,3},{4,20},{20... | collective-permute-start | bytes 1572872 | tf_op jit(solution)/shard_map/ppermute | solution.py:17
  15.4 70.0 %copy-start.6 = (bf16[64,4096]{1,0:T(8,128)(2,1)}, bf16[64,4096]{1,0:T(8,128)(2,1)S(1)}, u32[]{:S(2)}) copy-start(bf16[64,4096]{1,0:T(8,128)(2,1)S(1)} %get-tuple-element.16.refs_0_) | copy-start | bytes 1572868
  15.4 16.0 %collective-permute-start.2 = (bf16[64,4096]{1,0:T(8,128)(2,1)S(1)}, bf16[64,4096]{1,0:T(8,128)(2,1)S(1)}, u32[]{:S(2)}, u32[]{:S(2)}) collective-permute-start(bf16[64,4096]{1,0:T(8,128)(2,1)S(1)} %get-tuple-element.16.refs_0_), channel_id=1, source_target_pairs={{0,1},{1,2},{2,3},{3,4},{4,5},{5,6},{6,7},{7,0},{8,9},{9,10},{10,1... | collective-permute-start | bytes 1572872 | tf_op jit(solution)/shard_map/ppermute | solution.py:35
  15.5 15.9 %collective-permute-start.3 = (bf16[64,4096]{1,0:T(8,128)(2,1)S(1)}, bf16[64,4096]{1,0:T(8,128)(2,1)S(1)}, u32[]{:S(2)}, u32[]{:S(2)}) collective-permute-start(bf16[64,4096]{1,0:T(8,128)(2,1)S(1)} %get-tuple-element.16.refs_0_), channel_id=1, source_target_pairs={{0,7},{1,0},{2,1},{3,2},{4,3},{5,4},{6,5},{7,6},{8,15},{9,8},{10,9... | collective-permute-start | bytes 1572872 | tf_op jit(solution)/shard_map/ppermute | solution.py:35
  19.4 17.4 %collective-permute-start.1 = (bf16[64,4096]{1,0:T(8,128)(2,1)S(1)}, bf16[64,4096]{1,0:T(8,128)(2,1)S(1)}, u32[]{:S(2)}, u32[]{:S(2)}) collective-permute-start(bf16[64,4096]{1,0:T(8,128)(2,1)S(1)} %get-tuple-element.15), channel_id=1, source_target_pairs={{0,8},{8,0},{1,9},{9,1},{2,10},{10,2},{3,11},{11,3},{4,12},{12,4},... | collective-permute-start | bytes 1572872 | tf_op jit(solution)/shard_map/ppermute | solution.py:21
  31.4 27.8 %copy-start.9 = (bf16[64,4096]{1,0:T(8,128)(2,1)}, bf16[64,4096]{1,0:T(8,128)(2,1)S(1)}, u32[]{:S(2)}) copy-start(bf16[64,4096]{1,0:T(8,128)(2,1)S(1)} %collective-permute-done.2.refs_2_) | copy-start | bytes 1572868
  31.4 13.9 %collective-permute-start.4 = (bf16[64,4096]{1,0:T(8,128)(2,1)S(1)}, bf16[64,4096]{1,0:T(8,128)(2,1)S(1)}, u32[]{:S(2)}, u32[]{:S(2)}) collective-permute-start(bf16[64,4096]{1,0:T(8,128)(2,1)S(1)} %collective-permute-done.2.refs_2_), channel_id=1, source_target_pairs={{0,1},{1,2},{2,3},{3,4},{4,5},{5,6},{6,7},{7,0},{8,9},{9,10},{10,1... | collective-permute-start | bytes 1572872 | tf_op jit(solution)/shard_map/ppermute | solution.py:35
  31.4 27.8 %copy-start.10 = (bf16[64,4096]{1,0:T(8,128)(2,1)}, bf16[64,4096]{1,0:T(8,128)(2,1)S(1)}, u32[]{:S(2)}) copy-start(bf16[64,4096]{1,0:T(8,128)(2,1)S(1)} %collective-permute-done.3.refs_3_) | copy-start | bytes 1572868
  31.4 13.9 %collective-permute-start.5 = (bf16[64,4096]{1,0:T(8,128)(2,1)S(1)}, bf16[64,4096]{1,0:T(8,128)(2,1)S(1)}, u32[]{:S(2)}, u32[]{:S(2)}) collective-permute-start(bf16[64,4096]{1,0:T(8,128)(2,1)S(1)} %collective-permute-done.3.refs_3_), channel_id=1, source_target_pairs={{0,7},{1,0},{2,1},{3,2},{4,3},{5,4},{6,5},{7,6},{8,15},{9,8},{10,9... | collective-permute-start | bytes 1572872 | tf_op jit(solution)/shard_map/ppermute | solution.py:35
  36.8 22.4 %copy-start.11 = (bf16[64,4096]{1,0:T(8,128)(2,1)}, bf16[64,4096]{1,0:T(8,128)(2,1)S(1)}, u32[]{:S(2)}) copy-start(bf16[64,4096]{1,0:T(8,128)(2,1)S(1)} %collective-permute-done.1.refs_1_) | copy-start | bytes 1572868
  36.8 19.7 %collective-permute-start.6 = (bf16[64,4096]{1,0:T(8,128)(2,1)S(1)}, bf16[64,4096]{1,0:T(8,128)(2,1)S(1)}, u32[]{:S(2)}, u32[]{:S(2)}) collective-permute-start(bf16[64,4096]{1,0:T(8,128)(2,1)S(1)} %collective-permute-done.1.refs_1_), channel_id=1, source_target_pairs={{0,1},{1,2},{2,3},{3,4},{4,5},{5,6},{6,7},{7,0},{8,9},{9,10},{10,1... | collective-permute-start | bytes 1572872 | tf_op jit(solution)/shard_map/ppermute | solution.py:35
  36.8 19.7 %collective-permute-start.7 = (bf16[64,4096]{1,0:T(8,128)(2,1)S(1)}, bf16[64,4096]{1,0:T(8,128)(2,1)S(1)}, u32[]{:S(2)}, u32[]{:S(2)}) collective-permute-start(bf16[64,4096]{1,0:T(8,128)(2,1)S(1)} %collective-permute-done.1.refs_1_), channel_id=1, source_target_pairs={{0,7},{1,0},{2,1},{3,2},{4,3},{5,4},{6,5},{7,6},{8,15},{9,8},{10,9... | collective-permute-start | bytes 1572872 | tf_op jit(solution)/shard_map/ppermute | solution.py:35
  45.3 13.9 %copy-start.12 = (bf16[64,4096]{1,0:T(8,128)(2,1)}, bf16[64,4096]{1,0:T(8,128)(2,1)S(1)}, u32[]{:S(2)}) copy-start(bf16[64,4096]{1,0:T(8,128)(2,1)S(1)} %collective-permute-done.4.refs_4_) | copy-start | bytes 1572868
  45.3 22.6 %collective-permute-start.8 = (bf16[64,4096]{1,0:T(8,128)(2,1)S(1)}, bf16[64,4096]{1,0:T(8,128)(2,1)S(1)}, u32[]{:S(2)}, u32[]{:S(2)}) collective-permute-start(bf16[64,4096]{1,0:T(8,128)(2,1)S(1)} %collective-permute-done.4.refs_4_), channel_id=1, source_target_pairs={{0,1},{1,2},{2,3},{3,4},{4,5},{5,6},{6,7},{7,0},{8,9},{9,10},{10,1... | collective-permute-start | bytes 1572872 | tf_op jit(solution)/shard_map/ppermute | solution.py:35
  45.3 39.3 %copy-start.13 = (bf16[64,4096]{1,0:T(8,128)(2,1)}, bf16[64,4096]{1,0:T(8,128)(2,1)S(1)}, u32[]{:S(2)}) copy-start(bf16[64,4096]{1,0:T(8,128)(2,1)S(1)} %collective-permute-done.5.refs_5_) | copy-start | bytes 1572868
  45.3 22.7 %collective-permute-start.9 = (bf16[64,4096]{1,0:T(8,128)(2,1)S(1)}, bf16[64,4096]{1,0:T(8,128)(2,1)S(1)}, u32[]{:S(2)}, u32[]{:S(2)}) collective-permute-start(bf16[64,4096]{1,0:T(8,128)(2,1)S(1)} %collective-permute-done.5.refs_5_), channel_id=1, source_target_pairs={{0,7},{1,0},{2,1},{3,2},{4,3},{5,4},{6,5},{7,6},{8,15},{9,8},{10,9... | collective-permute-start | bytes 1572872 | tf_op jit(solution)/shard_map/ppermute | solution.py:35
  56.5 28.1 %copy-start.14 = (bf16[64,4096]{1,0:T(8,128)(2,1)}, bf16[64,4096]{1,0:T(8,128)(2,1)S(1)}, u32[]{:S(2)}) copy-start(bf16[64,4096]{1,0:T(8,128)(2,1)S(1)} %collective-permute-done.6.refs_6_) | copy-start | bytes 1572868
  56.5 22.6 %collective-permute-start.10 = (bf16[64,4096]{1,0:T(8,128)(2,1)S(1)}, bf16[64,4096]{1,0:T(8,128)(2,1)}, u32[]{:S(2)}, u32[]{:S(2)}) collective-permute-start(bf16[64,4096]{1,0:T(8,128)(2,1)S(1)} %collective-permute-done.6.refs_6_), channel_id=1, source_target_pairs={{0,1},{1,2},{2,3},{3,4},{4,5},{5,6},{6,7},{7,0},{8,9},{9,10},{10,1... | collective-permute-start | bytes 1572872 | tf_op jit(solution)/shard_map/ppermute | solution.py:35
  56.5 28.1 %copy-start.15 = (bf16[64,4096]{1,0:T(8,128)(2,1)}, bf16[64,4096]{1,0:T(8,128)(2,1)S(1)}, u32[]{:S(2)}) copy-start(bf16[64,4096]{1,0:T(8,128)(2,1)S(1)} %collective-permute-done.7.refs_7_) | copy-start | bytes 1572868
  56.5 22.6 %collective-permute-start.11 = (bf16[64,4096]{1,0:T(8,128)(2,1)S(1)}, bf16[64,4096]{1,0:T(8,128)(2,1)}, u32[]{:S(2)}, u32[]{:S(2)}) collective-permute-start(bf16[64,4096]{1,0:T(8,128)(2,1)S(1)} %collective-permute-done.7.refs_7_), channel_id=1, source_target_pairs={{0,7},{1,0},{2,1},{3,2},{4,3},{5,4},{6,5},{7,6},{8,15},{9,8},{10,9... | collective-permute-start | bytes 1572872 | tf_op jit(solution)/shard_map/ppermute | solution.py:35
  67.9 17.5 %copy-start.7 = (bf16[64,4096]{1,0:T(8,128)(2,1)}, bf16[64,4096]{1,0:T(8,128)(2,1)S(1)}, u32[]{:S(2)}) copy-start(bf16[64,4096]{1,0:T(8,128)(2,1)S(1)} %collective-permute-done.8.refs_8_) | copy-start | bytes 1572868
  67.9 16.7 %collective-permute-start.12 = (bf16[32,4096]{1,0:T(8,128)(2,1)S(1)}, bf16[32,4096]{1,0:T(8,128)(2,1)S(1)}, u32[]{:S(2)}, u32[]{:S(2)}) collective-permute-start(bf16[32,4096]{1,0:T(8,128)(2,1)S(1)} %slice.24), channel_id=1, source_target_pairs={{0,1},{1,2},{2,3},{3,4},{4,5},{5,6},{6,7},{7,0},{8,9},{9,10},{10,1... | collective-permute-start | bytes 786440 | tf_op jit(solution)/shard_map/ppermute | solution.py:35
  68.0 17.3 %copy-start.8 = (bf16[64,4096]{1,0:T(8,128)(2,1)}, bf16[64,4096]{1,0:T(8,128)(2,1)S(1)}, u32[]{:S(2)}) copy-start(bf16[64,4096]{1,0:T(8,128)(2,1)S(1)} %collective-permute-done.9.refs_9_) | copy-start | bytes 1572868
  68.0 17.3 %collective-permute-start.13 = (bf16[32,4096]{1,0:T(8,128)(2,1)S(1)}, bf16[32,4096]{1,0:T(8,128)(2,1)}, u32[]{:S(2)}, u32[]{:S(2)}) collective-permute-start(bf16[32,4096]{1,0:T(8,128)(2,1)S(1)} %slice.25), channel_id=1, source_target_pairs={{0,7},{1,0},{2,1},{3,2},{4,3},{5,4},{6,5},{7,6},{8,15},{9,8},{10,9... | collective-permute-start | bytes 786440 | tf_op jit(solution)/shard_map/ppermute | solution.py:35
  79.1 26.2 %collective-permute-start.14 = (bf16[64,4096]{1,0:T(8,128)(2,1)}, bf16[64,4096]{1,0:T(8,128)(2,1)S(1)}, u32[]{:S(2)}, u32[]{:S(2)}) collective-permute-start(bf16[64,4096]{1,0:T(8,128)(2,1)} %collective-permute-done.10.refs_10_), channel_id=1, source_target_pairs={{0,1},{1,2},{2,3},{3,4},{4,5},{5,6},{6,7},{7,0},{8,9},{9,10},{10,1... | collective-permute-start | bytes 1572872 | tf_op jit(solution)/shard_map/ppermute | solution.py:35
  79.1 26.4 %collective-permute-start.15 = (bf16[64,4096]{1,0:T(8,128)(2,1)}, bf16[64,4096]{1,0:T(8,128)(2,1)S(1)}, u32[]{:S(2)}, u32[]{:S(2)}) collective-permute-start(bf16[64,4096]{1,0:T(8,128)(2,1)} %collective-permute-done.11.refs_11_), channel_id=1, source_target_pairs={{0,7},{1,0},{2,1},{3,2},{4,3},{5,4},{6,5},{7,6},{8,15},{9,8},{10,9... | collective-permute-start | bytes 1572872 | tf_op jit(solution)/shard_map/ppermute | solution.py:35
  84.6 0.7 copy-start.16
  85.3 22.9 %copy-start.17 = (f32[1,2,2048]{2,1,0:T(2,128)S(1)}, f32[1,2,2048]{2,1,0:T(2,128)}, u32[]{:S(2)}) copy-start(f32[1,2,2048]{2,1,0:T(2,128)} %param.9) | copy-start | bytes 49156
  102.4 23.0 %collective-permute-start.22 = (bf16[13,64,768]{2,1,0:T(8,128)(2,1)}, bf16[13,64,768]{2,1,0:T(8,128)(2,1)S(1)}, u32[]{:S(2)}, u32[]{:S(2)}) collective-permute-start(bf16[13,64,768]{2,1,0:T(8,128)(2,1)} %get-tuple-element.11), channel_id=1, source_target_pairs={{0,16},{16,0},{1,17},{17,1},{2,18},{18,2},{3,19},{19,3},{4,20},{20... | collective-permute-start | bytes 3833864 | tf_op jit(solution)/shard_map/ppermute | solution.py:17
  105.3 13.2 %copy-start.4 = (bf16[64,4096]{1,0:T(8,128)(2,1)}, bf16[64,4096]{1,0:T(8,128)(2,1)S(1)}, u32[]{:S(2)}) copy-start(bf16[64,4096]{1,0:T(8,128)(2,1)S(1)} %collective-permute-done.14.refs_0_) | copy-start | bytes 1572868
  105.4 10.7 %collective-permute-start.16 = (bf16[32,4096]{1,0:T(8,128)(2,1)S(1)}, bf16[32,4096]{1,0:T(8,128)(2,1)}, u32[]{:S(2)}, u32[]{:S(2)}) collective-permute-start(bf16[32,4096]{1,0:T(8,128)(2,1)S(1)} %slice.26), channel_id=1, source_target_pairs={{0,1},{1,2},{2,3},{3,4},{4,5},{5,6},{6,7},{7,0},{8,9},{9,10},{10,1... | collective-permute-start | bytes 786440 | tf_op jit(solution)/shard_map/ppermute | solution.py:35
  105.5 13.1 %copy-start.5 = (bf16[64,4096]{1,0:T(8,128)(2,1)}, bf16[64,4096]{1,0:T(8,128)(2,1)S(1)}, u32[]{:S(2)}) copy-start(bf16[64,4096]{1,0:T(8,128)(2,1)S(1)} %collective-permute-done.15.refs_1_) | copy-start | bytes 1572868
  105.5 11.2 %collective-permute-start.17 = (bf16[32,4096]{1,0:T(8,128)(2,1)S(1)}, bf16[32,4096]{1,0:T(8,128)(2,1)}, u32[]{:S(2)}, u32[]{:S(2)}) collective-permute-start(bf16[32,4096]{1,0:T(8,128)(2,1)S(1)} %slice.27), channel_id=1, source_target_pairs={{0,7},{1,0},{2,1},{3,2},{4,3},{5,4},{6,5},{7,6},{8,15},{9,8},{10,9... | collective-permute-start | bytes 786440 | tf_op jit(solution)/shard_map/ppermute | solution.py:35
  108.2 6.6 %collective-permute-start.23 = (f32[2,2048]{1,0:T(2,128)S(1)}, f32[2,2048]{1,0:T(2,128)S(1)}, u32[]{:S(2)}, u32[]{:S(2)}) collective-permute-start(f32[2,2048]{1,0:T(2,128)S(1)} %bitcast.48), channel_id=1, source_target_pairs={{0,0},{8,16},{16,8},{24,24},{1,1},{9,17},{17,9},{25,25},{2,2},{10,... | collective-permute-start | bytes 49160 | tf_op jit(solution)/shard_map/ppermute | solution.py:25
  113.3 5.2 %collective-permute-start.18 = (bf16[64,4096]{1,0:T(8,128)(2,1)S(1)}, bf16[64,4096]{1,0:T(8,128)(2,1)}, u32[]{:S(2)}, u32[]{:S(2)}) collective-permute-start(bf16[64,4096]{1,0:T(8,128)(2,1)S(1)} %collective-permute-done.14.refs_0_), channel_id=1, source_target_pairs={{0,16},{16,0},{1,17},{17,1},{2,18},{18,2},{3,19},{19,3},{4,20},{20... | collective-permute-start | bytes 1572872 | tf_op jit(solution)/shard_map/ppermute | solution.py:17
  114.8 3.8 %collective-permute-start.19 = (bf16[64,4096]{1,0:T(8,128)(2,1)S(1)}, bf16[64,4096]{1,0:T(8,128)(2,1)}, u32[]{:S(2)}, u32[]{:S(2)}) collective-permute-start(bf16[64,4096]{1,0:T(8,128)(2,1)S(1)} %collective-permute-done.15.refs_1_), channel_id=1, source_target_pairs={{0,16},{16,0},{1,17},{17,1},{2,18},{18,2},{3,19},{19,3},{4,20},{20... | collective-permute-start | bytes 1572872 | tf_op jit(solution)/shard_map/ppermute | solution.py:17
  116.1 2.1 %collective-permute-start.20 = (bf16[32,4096]{1,0:T(8,128)(2,1)}, bf16[32,4096]{1,0:T(8,128)(2,1)}, u32[]{:S(2)}, u32[]{:S(2)}) collective-permute-start(bf16[32,4096]{1,0:T(8,128)(2,1)} %collective-permute-done.16.refs_2_), channel_id=1, source_target_pairs={{0,16},{16,0},{1,17},{17,1},{2,18},{18,2},{3,19},{19,3},{4,20},{20... | collective-permute-start | bytes 786440 | tf_op jit(solution)/shard_map/ppermute | solution.py:17
  116.7 1.9 %collective-permute-start.21 = (bf16[32,4096]{1,0:T(8,128)(2,1)}, bf16[32,4096]{1,0:T(8,128)(2,1)}, u32[]{:S(2)}, u32[]{:S(2)}) collective-permute-start(bf16[32,4096]{1,0:T(8,128)(2,1)} %collective-permute-done.17.refs_3_), channel_id=1, source_target_pairs={{0,16},{16,0},{1,17},{17,1},{2,18},{18,2},{3,19},{19,3},{4,20},{20... | collective-permute-start | bytes 786440 | tf_op jit(solution)/shard_map/ppermute | solution.py:17
  118.0 7.5 %copy-start = (bf16[13,64,768]{2,1,0:T(8,128)(2,1)S(1)}, bf16[13,64,768]{2,1,0:T(8,128)(2,1)}, u32[]{:S(2)}) copy-start(bf16[13,64,768]{2,1,0:T(8,128)(2,1)} %get-tuple-element.9.refs_0_) | copy-start | bytes 3833860
  125.4 1.0 copy-start.1
  126.4 1.0 copy-start.2
  170.4 4.2 %collective-permute-start.24 = (bf16[8,128,256]{2,1,0:T(8,128)(2,1)S(1)}, bf16[8,128,256]{2,1,0:T(8,128)(2,1)S(1)}, u32[]{:S(2)}, u32[]{:S(2)}) collective-permute-start(bf16[8,128,256]{2,1,0:T(8,128)(2,1)S(1)} %dynamic-slice_bitcast_fusion), channel_id=1, source_target_pairs={{0,16},{16,0},{1,17},{17,1},{2,18},{18,2},{3,19},{19,3},{4,20},{20... | collective-permute-start | bytes 1572872 | tf_op jit(solution)/shard_map/ppermute | solution.py:17
Sparse Core Ops, SparseCore 0:
  9.9 74.3 all-gather.2

commit v3 on v2

--- a/solution.py
+++ b/solution.py
@@ -33,6 +33,18 @@
 
 def ring_z(value, step):
     return lax.ppermute(value, "z", [(i, (i + step) % 8) for i in range(8)])
+
+
+def after(value, *others):
+    anywhere = pl.BlockSpec(memory_space=pl.ANY)
+    return pl.pallas_call(
+        lambda *refs: None,
+        out_shape=jax.ShapeDtypeStruct(value.shape, value.dtype),
+        in_specs=[anywhere] * (1 + len(others)),
+        out_specs=anywhere,
+        input_output_aliases={0: 0},
+        name="after",
+    )(value, *others)
 
 
 def gather_weight(weight):
@@ -51,78 +63,106 @@
 
 SLOTS = (
     [(0, 0), (1, 0), (0, 1), (0, 7), (0, 2), (0, 6), (1, 1), (1, 7)]
-    + [(0, 3), (0, 5), (1, 2), (1, 6), (0, 4), (1, 3), (1, 5), (1, 4)]
+    + [(0, 3), (0, 5), (1, 2), (1, 6), (1, 3), (1, 5)]
+    + [(0, 4), (1, 4)]
 )
-BATCHES = ((0, 13), (13, 16))
-
-
-def project_kernel(count, last_group, core_ref, *refs):
+BATCHES = ((0, 8), (8, 14), (14, 16))
+
+
+def project_kernel(count, core_ref, *refs):
     pieces, weight_ref = refs[:count], refs[count]
-    outs = refs[count + 1 :]
+    given_ref, kept_ref = refs[count + 1 :]
     group, part = pl.program_id(0), pl.program_id(1)
     rows = jnp.concatenate([piece[...] for piece in pieces], axis=0)
     weight = weight_ref[:, 0].reshape(4096, 256)
     product = jnp.dot(rows, weight, preferred_element_type=jnp.float32)
     gated = product / (1.0 + jnp.exp(-product))
-    result = jnp.where(part < 2, gated, product).astype(jnp.bfloat16).reshape(-1, 64, 256)
-    if last_group == 0:
-        slots = outs[0].shape[0]
-        outs[0][...] = result[:slots]
-        outs[1][...] = result[slots:]
-        return
+    result = jnp.where(part < 2, gated, product).astype(jnp.bfloat16).reshape(kept_ref.shape)
 
     @pl.when(group == 0)
     def _():
-        outs[0][...] = result
+        given_ref[...] = result
 
     @pl.when(group == 1)
     def _():
-        outs[1][...] = result
-
-
-def project(core, pieces, weight, both):
+        kept_ref[...] = result
+
+
+def project(core, pieces, weight):
     rows = sum(piece.shape[0] for piece in pieces)
     width = weight.shape[3]
-    groups = 2 if both else 1
-    slots = rows // 64 if both else rows // 128
+    slots = rows // 64
     out = jax.ShapeDtypeStruct((slots, 64, width), jnp.bfloat16)
 
     def columns(g, p, core):
-        mine = 1 if not both else g
-        return 0, mine * core[0] + (1 - mine) * (1 - core[0]), 0, p
-
-    last = pl.BlockSpec((slots, 64, 256), lambda g, p, core: (0, 0, g * p))
-    first = pl.BlockSpec((slots, 64, 256), lambda g, p, core: (0, 0, (1 - g) * p + g * 2))
+        return 0, g * core[0] + (1 - g) * (1 - core[0]), 0, p
+
     return pl.pallas_call(
-        functools.partial(project_kernel, len(pieces), groups - 1),
+        functools.partial(project_kernel, len(pieces)),
         out_shape=(out, out),
         grid_spec=pltpu.PrefetchScalarGridSpec(
             num_scalar_prefetch=1,
-            grid=(groups, 3),
+            grid=(2, 3),
             in_specs=[pl.BlockSpec(piece.shape, lambda g, p, core: (0, 0)) for piece in pieces]
             + [pl.BlockSpec((4, 1, 1024, 256), columns)],
-            out_specs=[first, last if both else first],
+            out_specs=[
+                pl.BlockSpec((slots, 64, 256), lambda g, p, core: (0, 0, (1 - g) * p + g * 2)),
+                pl.BlockSpec((slots, 64, 256), lambda g, p, core: (0, 0, g * p)),
+            ],
         ),
         compiler_params=pltpu.CompilerParams(vmem_limit_bytes=58 << 20),
         cost_estimate=pl.CostEstimate(
-            flops=groups * 2 * rows * 4096 * width,
-            bytes_accessed=2 * rows * 8192 + groups * (6 << 20),
+            flops=4 * rows * 4096 * width,
+            bytes_accessed=2 * rows * 8192 + (12 << 20),
             transcendentals=0,
         ),
         name="project",
     )(core, *pieces, weight)
 
 
-def attend_kernel(chunk_ref, core_ref, *refs):
-    batches = len(BATCHES)
-    kept, got = refs[:batches], refs[batches : 2 * batches]
-    row_ref, column_ref, out_ref, all_ref = refs[2 * batches :]
+def finish_kernel(chunk_ref, core_ref, one, two, three, four, weight_ref, *refs):
+    count = len(BATCHES) - 1
+    kept, got = refs[:count], refs[count : 2 * count]
+    row_ref, column_ref, out_ref, new_ref, all_ref, sems = refs[2 * count :]
+    part = pl.program_id(0)
     core = core_ref[0]
-    for batch, (first, last) in enumerate(BATCHES):
+    copies = []
+    for batch, (first, last) in enumerate(BATCHES[:count]):
         for slot in range(first, last):
-            chunk = chunk_ref[slot]
-            all_ref[chunk, core] = kept[batch][slot - first]
-            all_ref[chunk, 1 - core] = got[batch][slot - first]
+            for place, source in enumerate((kept, got)):
+                half = core if place == 0 else 1 - core
+                copies.append(
+                    pltpu.make_async_copy(
+                        source[batch].at[slot - first],
+                        all_ref.at[chunk_ref[slot], half],
+                        sems.at[2 * slot + place],
+                    )
+                )
+
+    @pl.when(part == 0)
+    def _():
+        for copy in copies:
+            copy.start()
+
+    rows = jnp.concatenate([piece[...] for piece in (one, two, three, four)], axis=0)
+    weight = weight_ref[:, 0].reshape(4096, 256)
+    product = jnp.dot(rows, weight, preferred_element_type=jnp.float32)
+    gated = product / (1.0 + jnp.exp(-product))
+    result = jnp.where(part < 2, gated, product).astype(jnp.bfloat16)
+    new_ref[:, :, pl.ds(pl.multiple_of(part * 256, 256), 256)] = result.reshape(-1, 64, 256)
+
+    @pl.when(part == 2)
+    def _():
+        for copy in copies:
+            copy.wait()
+        first, last = BATCHES[-1]
+        for i in range(last - first):
+            all_ref[chunk_ref[first + i], core] = new_ref[i]
+            all_ref[chunk_ref[first + i], 1 - core] = new_ref[last - first + i]
+        attend(row_ref, column_ref, out_ref, all_ref)
+
+
+def attend(row_ref, column_ref, out_ref, all_ref):
     later = lax.broadcasted_iota(jnp.int32, (BLOCK, BLOCK), 0)
     earlier = lax.broadcasted_iota(jnp.int32, (BLOCK, BLOCK), 1)
     causal = later >= earlier
@@ -158,21 +198,38 @@
         out_ref[2 * step : 2 * step + 2] = mixed
 
 
-def attend(chunks, core, kept, got, row, column):
-    vmem = pl.BlockSpec(memory_space=pltpu.VMEM)
-    smem = pl.BlockSpec(memory_space=pltpu.SMEM)
+def finish(chunks, core, pieces, weight, kept, got, row, column):
+    width = weight.shape[3]
+    anywhere = pl.BlockSpec(memory_space=pl.ANY)
+
+    def whole(array):
+        return pl.BlockSpec(array.shape, lambda p, chunks, core: (0,) * array.ndim)
+
     return pl.pallas_call(
-        attend_kernel,
+        finish_kernel,
         out_shape=jax.ShapeDtypeStruct((16, 128, 256), jnp.bfloat16),
-        in_specs=[smem, smem] + [vmem] * (2 * len(BATCHES) + 2),
-        out_specs=vmem,
-        scratch_shapes=[pltpu.VMEM((16, 2, 64, 768), jnp.bfloat16)],
-        compiler_params=pltpu.CompilerParams(vmem_limit_bytes=24 << 20),
+        grid_spec=pltpu.PrefetchScalarGridSpec(
+            num_scalar_prefetch=2,
+            grid=(3,),
+            in_specs=[whole(piece) for piece in pieces]
+            + [pl.BlockSpec((4, 1, 1024, 256), lambda p, chunks, core: (0, core[0], 0, p))]
+            + [anywhere] * (len(kept) + len(got))
+            + [whole(row), whole(column)],
+            out_specs=pl.BlockSpec((16, 128, 256), lambda p, chunks, core: (0, 0, 0)),
+            scratch_shapes=[
+                pltpu.VMEM((4, 64, width), jnp.bfloat16),
+                pltpu.VMEM((16, 2, 64, width), jnp.bfloat16),
+                pltpu.SemaphoreType.DMA((2 * BATCHES[-1][0],)),
+            ],
+        ),
+        compiler_params=pltpu.CompilerParams(vmem_limit_bytes=58 << 20),
         cost_estimate=pl.CostEstimate(
-            flops=16 * 50_331_648, bytes_accessed=4 << 20, transcendentals=0
-        ),
-        name="attend",
-    )(chunks, core, *kept, *got, row, column)
+            flops=2 * 256 * 4096 * width + 16 * 50_331_648,
+            bytes_accessed=12 << 20,
+            transcendentals=0,
+        ),
+        name="finish",
+    )(chunks, core, *pieces, weight, *kept, *got, row, column)
 
 
 def shards(tokens, query_weight, key_weight, value_weight, log_decay):
@@ -190,6 +247,10 @@
     g = jnp.cumsum(decay.reshape(2, 8, BLOCK), axis=-1)
     row, column = g.transpose(1, 0, 2), g.transpose(1, 2, 0)
 
+    chunks = jnp.stack(
+        [(half + kind) % 2 * 8 + jnp.mod(z - step, 8) for kind, step in SLOTS]
+    ).astype(jnp.int32)
+    place = after(core.astype(jnp.int32).reshape(1), chunks, row, column)
     held = {}
     for kind, mine in enumerate((near, far)):
         held[kind, 0] = (mine,)
@@ -197,19 +258,19 @@
         for distance in range(1, 4):
             up, down = ring_z(up, 1), ring_z(down, -1)
             held[kind, distance], held[kind, 8 - distance] = (up,), (down,)
-        held[kind, 4] = (ring_z(up[:32], 1), ring_z(down[32:], -1))
-    place = core.astype(jnp.int32).reshape(1)
-    early, late = ([p for at in SLOTS[i:j] for p in held[at]] for i, j in BATCHES)
-    for_other, for_me = project(place, early, weight, True)
-    late_mine, late_other = project(
-        place, late + [swap_core(piece) for piece in late], weight, False
-    )
-    mine, others = (for_me, late_mine), (swap_core(for_other), late_other)
-
-    chunks = jnp.stack(
-        [(half + kind) % 2 * 8 + jnp.mod(z - step, 8) for kind, step in SLOTS]
-    ).astype(jnp.int32)
-    mixed = attend(chunks, place, mine, others, row, column)
+    first = [p for at in SLOTS[slice(*BATCHES[0])] for p in held[at]]
+    first_other, first_me = project(place, first, weight)
+    ends = [after(*held[0, 3], first_other), after(*held[1, 5], first_other)]
+    held[0, 3], held[1, 5] = ends[:1], ends[1:]
+    last = [ring_z(ends[0], 1), ring_z(ends[1], -1)]
+    second = [p for at in SLOTS[slice(*BATCHES[1])] for p in held[at]]
+    second_other, second_me = project(place, second, weight)
+    swapped = [swap_core(piece) for piece in last]
+    first_other = swap_core(after(first_other, second_me))
+    others = (first_other, swap_core(second_other))
+    mixed = finish(
+        chunks, place, last + swapped, weight, (first_me, second_me), others, row, column
+    )
 
     spread = lax.all_to_all(mixed, ("xh", "z"), split_axis=0, concat_axis=0, tiled=True)
     spread = spread.reshape(2, 8, 128, 256)

time: 184 us -> 183 us (level)
  waiting for transfers between devices: 51.2 us -> 33.9 us
  Pallas kernels: 32.3 us -> 41.4 us
  starting transfers between devices: 40.8 us -> 47 us
    ppermute x16 -> x14, waiting for transfers between devices: 43.4 us -> 7.92 us  [ring_z(): return lax.ppermute(value, 'z', [(i, (i + step) % 8) for i in range(8)])]
    all_gather x1, waiting for transfers between devices: 0.01 us -> 12.3 us  [gather_weight(): lax.all_gather(weight, ('y', 'xl', 'c', 'xh'), axis=0, tiled=False, axis_...]
    pallas_call x3 -> x7, Pallas kernels: 32.3 us -> 41.4 us  [the longest x2 24.8 us: project(): pl.pallas_call(functools.partial(project_kernel, len(pieces)), out_shape=...]
    ppermute x1, starting transfers between devices: 5.11 us -> 10.6 us  [swap_roles(): return lax.ppermute(value, ('c', 'xh'), [(0, 0), (1, 2), (2, 1), (3, 3)])]
    ppermute x1, waiting for transfers between devices: 2.74 us -> 8.05 us  [swap_half(): return lax.ppermute(value, 'xh', [(0, 1), (1, 0)])]
    ppermute x16 -> x14, starting transfers between devices: 23 us -> 26.4 us  [ring_z(): return lax.ppermute(value, 'z', [(i, (i + step) % 8) for i in range(8)])]
    ppermute x7 -> x6, starting transfers between devices: 9.94 us -> 8.9 us  [swap_core(): return lax.ppermute(value, 'c', [(0, 1), (1, 0)])]
    ppermute x7 -> x6, waiting for transfers between devices: 3.64 us -> 4.59 us  [swap_core(): return lax.ppermute(value, 'c', [(0, 1), (1, 0)])]
  transfers between devices with their start and end apart: 26 -> 23, of which waited for: 12 -> 9; matrix products, arithmetic and copies ran while one was open for 2% -> 3% of each run, Pallas kernels for 13% -> 14%
where the time goes in v3:
time: 183 us; the launch traced here: 182 us
  starting transfers between devices  47 us (26%)
  Pallas kernels  41.4 us (23%)
  waiting for transfers between devices  33.9 us (19%)
  blocking collectives  33.5 us (18%)
  between operations  13.8 us (8%)
  local copies, waits for them, and re-layouts  7.14 us (4%)
  other arithmetic  5.2 us (3%)
    all_to_all x1, blocking collectives, shards(): lax.all_to_all(mixed, ('xh', 'z'), split_axis=0, concat_axis=0, tiled=True)  33.5 us
    ppermute x14, starting transfers between devices, ring_z(): return lax.ppermute(value, 'z', [(i, (i + step) % 8) for i in range(8)])  26.4 us
    pallas_call x2, Pallas kernels, project(): pl.pallas_call(functools.partial(project_kernel, len(pieces)), out_shape=...  24.8 us
    pallas_call x1, Pallas kernels, finish(): pl.pallas_call(finish_kernel, out_shape=jax.ShapeDtypeStruct((16, 128, 25...  16.1 us
    all_gather x1, waiting for transfers between devices, gather_weight(): lax.all_gather(weight, ('y', 'xl', 'c', 'xh'), axis=0, tiled=False, axis_...  12.3 us
    ppermute x1, starting transfers between devices, swap_roles(): return lax.ppermute(value, ('c', 'xh'), [(0, 0), (1, 2), (2, 1), (3, 3)])  10.6 us
    ppermute x6, starting transfers between devices, swap_core(): return lax.ppermute(value, 'c', [(0, 1), (1, 0)])  8.9 us
    ppermute x1, waiting for transfers between devices, swap_half(): return lax.ppermute(value, 'xh', [(0, 1), (1, 0)])  8.05 us
  transfers between devices with their start and end apart: 23, of which 9 were waited for; matrix products, arithmetic and copies ran while one was open for 3% of the time, Pallas kernels for 14%

profile of v3, /device:TPU:1, one launch (start us, length us, event | category | flops | bytes accessed | tf_op | source)
XLA Modules:
  0.0 181.9 jit_solution(3830681421158602252)
XLA Ops:
  6.5 1.9 %pad_maximum_fusion = bf16[256,768]{1,0:T(8,128)(2,1)} fusion(bf16[256,256]{1,0:T(8,128)(2,1)} %param.8, bf16[256,256]{1,0:T(8,128)(2,1)} %param.7, bf16[256,256]{1,0:T(8,128)(2,1)} %param.6), kind=kLoop, calls=%fused_computation.9 | loop fusion | flops 1179648 | bytes 786432 | tf_op jit(solution)/shard_map/concatenate | solution.py:238
  8.5 1.5 multiply_reduce_fusion
  10.0 0.1 rsqrt.12
  10.1 0.3 multiply_convert_fusion
  10.4 3.3 %collective-permute-start.1 = (bf16[64,4096]{1,0:T(8,128)(2,1)S(1)}, bf16[64,4096]{1,0:T(8,128)(2,1)S(1)}, u32[]{:S(2)}, u32[]{:S(2)}) collective-permute-start(bf16[64,4096]{1,0:T(8,128)(2,1)S(1)} %dynamic-slice_bitcast_fusion.1), channel_id=1, source_target_pairs={{0,16},{16,0},{1,17},{17,1},{2,18},{18,2},{3,19},{19,3},{4,20},{20... | collective-permute-start | bytes 1572872 | tf_op jit(solution)/shard_map/ppermute | solution.py:17
  13.8 1.5 collective-permute-done.1
  15.4 1.1 collective-permute-start.5
  16.5 1.6 collective-permute-start.2
  18.1 3.9 %collective-permute-start.6 = (bf16[64,4096]{1,0:T(8,128)(2,1)S(1)}, bf16[64,4096]{1,0:T(8,128)(2,1)}, u32[]{:S(2)}, u32[]{:S(2)}) collective-permute-start(bf16[64,4096]{1,0:T(8,128)(2,1)S(1)} %get-tuple-element.16.refs_0_), channel_id=1, source_target_pairs={{0,7},{1,0},{2,1},{3,2},{4,3},{5,4},{6,5},{7,6},{8,15},{9,8},{10,9... | collective-permute-start | bytes 1572872 | tf_op jit(solution)/shard_map/ppermute | solution.py:35
  22.1 8.1 %collective-permute-done.5.refs_1_ = bf16[64,4096]{1,0:T(8,128)(2,1)S(1)} collective-permute-done((bf16[64,4096]{1,0:T(8,128)(2,1)S(1)}, bf16[64,4096]{1,0:T(8,128)(2,1)S(1)}, u32[]{:S(2)}, u32[]{:S(2)}) %collective-permute-start.5) | collective-permute-done | bytes 524320 | tf_op jit(solution)/shard_map/ppermute | solution.py:21
  30.1 5.0 %collective-permute-start.9 = (bf16[64,4096]{1,0:T(8,128)(2,1)S(1)}, bf16[64,4096]{1,0:T(8,128)(2,1)}, u32[]{:S(2)}, u32[]{:S(2)}) collective-permute-start(bf16[64,4096]{1,0:T(8,128)(2,1)S(1)} %collective-permute-done.5.refs_1_), channel_id=1, source_target_pairs={{0,7},{1,0},{2,1},{3,2},{4,3},{5,4},{6,5},{7,6},{8,15},{9,8},{10,9... | collective-permute-start | bytes 1572872 | tf_op jit(solution)/shard_map/ppermute | solution.py:35
  35.1 0.1 collective-permute-start.3
  35.2 2.7 %collective-permute-start.7 = (bf16[64,4096]{1,0:T(8,128)(2,1)}, bf16[64,4096]{1,0:T(8,128)(2,1)}, u32[]{:S(2)}, u32[]{:S(2)}) collective-permute-start(bf16[64,4096]{1,0:T(8,128)(2,1)} %collective-permute-done.6.refs_3_), channel_id=1, source_target_pairs={{0,7},{1,0},{2,1},{3,2},{4,3},{5,4},{6,5},{7,6},{8,15},{9,8},{10,9... | collective-permute-start | bytes 1572872 | tf_op jit(solution)/shard_map/ppermute | solution.py:35
  37.9 6.7 %collective-permute-done.9.refs_7_ = bf16[64,4096]{1,0:T(8,128)(2,1)} collective-permute-done((bf16[64,4096]{1,0:T(8,128)(2,1)S(1)}, bf16[64,4096]{1,0:T(8,128)(2,1)}, u32[]{:S(2)}, u32[]{:S(2)}) %collective-permute-start.9) | collective-permute-done | bytes 524320 | tf_op jit(solution)/shard_map/ppermute | solution.py:35
  44.6 3.5 %collective-permute-start.11 = (bf16[64,4096]{1,0:T(8,128)(2,1)}, bf16[64,4096]{1,0:T(8,128)(2,1)}, u32[]{:S(2)}, u32[]{:S(2)}) collective-permute-start(bf16[64,4096]{1,0:T(8,128)(2,1)} %collective-permute-done.9.refs_7_), channel_id=1, source_target_pairs={{0,7},{1,0},{2,1},{3,2},{4,3},{5,4},{6,5},{7,6},{8,15},{9,8},{10,9... | collective-permute-start | bytes 1572872 | tf_op jit(solution)/shard_map/ppermute | solution.py:35
  48.1 10.6 %collective-permute-start = (f32[2,2048]{1,0:T(2,128)S(1)}, f32[2,2048]{1,0:T(2,128)S(1)}, u32[]{:S(2)}, u32[]{:S(2)}) collective-permute-start(f32[2,2048]{1,0:T(2,128)S(1)} %bitcast.50), channel_id=1, source_target_pairs={{0,0},{8,16},{16,8},{24,24},{1,1},{9,17},{17,9},{25,25},{2,2},{10,... | collective-permute-start | bytes 49160 | tf_op jit(solution)/shard_map/ppermute | solution.py:25
  58.9 0.6 stack.67.refs_1_.chunk_ref
  59.5 1.0 collective-permute-done
  60.6 1.2 reduce-window.6
  61.7 0.2 slice_reduce_fusion
  62.0 0.4 copy.19
  62.4 0.9 copy.20.refs_2_.refs_4_
  63.3 0.5 after.4.core_ref
  63.9 0.1 collective-permute-start.4
  64.0 3.0 %collective-permute-start.16 = (bf16[64,4096]{1,0:T(8,128)(2,1)}, bf16[64,4096]{1,0:T(8,128)(2,1)}, u32[]{:S(2)}, u32[]{:S(2)}) collective-permute-start(bf16[64,4096]{1,0:T(8,128)(2,1)} %collective-permute-done.7.refs_5_), channel_id=1, source_target_pairs={{0,7},{1,0},{2,1},{3,2},{4,3},{5,4},{6,5},{7,6},{8,15},{9,8},{10,9... | collective-permute-start | bytes 1572872 | tf_op jit(solution)/shard_map/ppermute | solution.py:35
  67.0 0.2 collective-permute-done.11.refs_3_
  67.2 3.4 %collective-permute-start.12 = (bf16[64,4096]{1,0:T(8,128)(2,1)}, bf16[64,4096]{1,0:T(8,128)(2,1)S(1)}, u32[]{:S(2)}, u32[]{:S(2)}) collective-permute-start(bf16[64,4096]{1,0:T(8,128)(2,1)} %collective-permute-done.11.refs_3_), channel_id=1, source_target_pairs={{0,7},{1,0},{2,1},{3,2},{4,3},{5,4},{6,5},{7,6},{8,15},{9,8},{10,9... | collective-permute-start | bytes 1572872 | tf_op jit(solution)/shard_map/ppermute | solution.py:35
  70.6 12.3 %all-gather.3.cloned.1.call-done = bf16[8192,768]{1,0:T(8,128)(2,1)} async-done(((bf16[256,768]{1,0:T(8,128)(2,1)}), bf16[8192,768]{1,0:T(8,128)(2,1)}) %all-gather.3.cloned.1.call-update) | async-done | bytes 12582928 | tf_op jit(solution)/shard_map/all_gather | solution.py:58
  82.9 13.1 %project.2 = (bf16[8,64,768]{2,1,0:T(8,128)(2,1)}, bf16[8,64,768]{2,1,0:T(8,128)(2,1)}) custom-call(s32[1]{0:T(128)} %after.4.core_ref, bf16[64,4096]{1,0:T(8,128)(2,1)} %copy-done.10, bf16[64,4096]{1,0:T(8,128)(2,1)} %copy-done.12, bf16[64,4096]{1,0:T(8,128)(2,1)} %copy-done.13, bf16[64,4096]{1,0:T(8,128)(2,1)} %collective-permute-done.6.refs_3_, ...), custom_call_target="tpu_custom_call" | custom-call | flops 6442450944 | bytes 20971520 | tf_op jit(solution)/shard_map/project/pallas_call | solution.py:100
  96.0 0.8 copy-done.9
  96.8 3.0 %collective-permute-start.13 = (bf16[64,4096]{1,0:T(8,128)(2,1)}, bf16[64,4096]{1,0:T(8,128)(2,1)S(1)}, u32[]{:S(2)}, u32[]{:S(2)}) collective-permute-start(bf16[64,4096]{1,0:T(8,128)(2,1)} %after.6.refs_5_), channel_id=1, source_target_pairs={{0,7},{1,0},{2,1},{3,2},{4,3},{5,4},{6,5},{7,6},{8,15},{9,8},{10,9... | collective-permute-start | bytes 1572872 | tf_op jit(solution)/shard_map/ppermute | solution.py:35
  99.9 0.8 copy-done.6
  100.7 11.7 %project.3 = (bf16[6,64,768]{2,1,0:T(8,128)(2,1)}, bf16[6,64,768]{2,1,0:T(8,128)(2,1)}) custom-call(s32[1]{0:T(128)} %after.4.core_ref, bf16[64,4096]{1,0:T(8,128)(2,1)} %after.5.refs_0_, bf16[64,4096]{1,0:T(8,128)(2,1)} %collective-permute-done.16.refs_1_, bf16[64,4096]{1,0:T(8,128)(2,1)} %collective-permute-done.17.refs_2_, ...), custom_call_target="tpu_custom_call" | custom-call | flops 4831838208 | bytes 18874368 | tf_op jit(solution)/shard_map/project/pallas_call | solution.py:100
  112.4 0.6 collective-permute-start.19
  113.0 0.4 copy-done.11
  113.4 0.5 collective-permute-start.20
  114.0 0.1 collective-permute-start.15
  114.1 1.0 collective-permute-done.10.one
  115.0 1.4 collective-permute-start.14
  116.5 1.5 collective-permute-done.14.three
  118.0 0.8 copy-done.8
  118.8 16.1 %finish.1 = bf16[16,128,256]{2,1,0:T(8,128)(2,1)} custom-call(s32[16]{0:T(128)} %stack.67.refs_1_.chunk_ref, s32[1]{0:T(128)} %after.4.core_ref, bf16[64,4096]{1,0:T(8,128)(2,1)} %copy-done.5, bf16[64,4096]{1,0:T(8,128)(2,1)} %copy-done.4, bf16[64,4096]{1,0:T(8,128)(2,1)} %copy-done.8, bf16[64,4096]{1,0:T(8,128)(2,1)} %copy-done.7, ...), custom_call_target="tpu_custom_call" | custom-call | flops 2415919104 | bytes 12582912 | tf_op jit(solution)/shard_map/finish/pallas_call | solution.py:208
  134.9 33.5 %all_to_all.5 = bf16[16,128,256]{2,1,0:T(8,128)(2,1)S(1)} all-to-all(bf16[16,128,256]{2,1,0:T(8,128)(2,1)} %finish.1), channel_id=1, replica_groups=mesh['y'=4,'xl'=2,'c'=2,'xh'=2,'z'=8] {'xh','z'}, dimensions={0} | all-to-all | bytes 2097152 | tf_op jit(solution)/shard_map/all_to_all | solution.py:275
  168.4 2.9 %collective-permute-start.21 = (bf16[8,128,256]{2,1,0:T(8,128)(2,1)S(1)}, bf16[8,128,256]{2,1,0:T(8,128)(2,1)S(1)}, u32[]{:S(2)}, u32[]{:S(2)}) collective-permute-start(bf16[8,128,256]{2,1,0:T(8,128)(2,1)S(1)} %dynamic-slice_bitcast_fusion), channel_id=1, source_target_pairs={{0,16},{16,0},{1,17},{17,1},{2,18},{18,2},{3,19},{19,3},{4,20},{20... | collective-permute-start | bytes 1572872 | tf_op jit(solution)/shard_map/ppermute | solution.py:17
  171.4 1.5 collective-permute-done.21
  173.0 0.1 maximum_bitcast_fusion
  173.1 0.7 copy.22
  173.8 1.3 copy.23
  (59 shorter events, 0.6 us)
Async XLA Ops:
  6.5 3.6 %copy-start.1 = (bf16[1,128,4096]{2,1,0:T(8,128)(2,1)S(1)}, bf16[1,128,4096]{2,1,0:T(8,128)(2,1)}, u32[]{:S(2)}) copy-start(bf16[1,128,4096]{2,1,0:T(8,128)(2,1)} %param.5) | copy-start | bytes 3145732
  6.5 76.3 %all-gather.3.cloned.1.call-start = ((), (), s32[]{:S(2)}) async-start(), calls=%async_computation.1 | async-start | bytes 12976128 | tf_op jit(solution)/shard_map/all_gather | solution.py:58
  10.4 37.8 %copy-start.14 = (f32[1,2,2048]{2,1,0:T(2,128)S(1)}, f32[1,2,2048]{2,1,0:T(2,128)}, u32[]{:S(2)}) copy-start(f32[1,2,2048]{2,1,0:T(2,128)} %param.9) | copy-start | bytes 49156
  10.4 4.9 %collective-permute-start.1 = (bf16[64,4096]{1,0:T(8,128)(2,1)S(1)}, bf16[64,4096]{1,0:T(8,128)(2,1)S(1)}, u32[]{:S(2)}, u32[]{:S(2)}) collective-permute-start(bf16[64,4096]{1,0:T(8,128)(2,1)S(1)} %dynamic-slice_bitcast_fusion.1), channel_id=1, source_target_pairs={{0,16},{16,0},{1,17},{17,1},{2,18},{18,2},{3,19},{19,3},{4,20},{20... | collective-permute-start | bytes 1572872 | tf_op jit(solution)/shard_map/ppermute | solution.py:17
  15.4 67.5 %copy-start.10 = (bf16[64,4096]{1,0:T(8,128)(2,1)}, bf16[64,4096]{1,0:T(8,128)(2,1)S(1)}, u32[]{:S(2)}) copy-start(bf16[64,4096]{1,0:T(8,128)(2,1)S(1)} %get-tuple-element.16.refs_0_) | copy-start | bytes 1572868
  15.4 14.7 %collective-permute-start.5 = (bf16[64,4096]{1,0:T(8,128)(2,1)S(1)}, bf16[64,4096]{1,0:T(8,128)(2,1)S(1)}, u32[]{:S(2)}, u32[]{:S(2)}) collective-permute-start(bf16[64,4096]{1,0:T(8,128)(2,1)S(1)} %get-tuple-element.15), channel_id=1, source_target_pairs={{0,8},{8,0},{1,9},{9,1},{2,10},{10,2},{3,11},{11,3},{4,12},{12,4},... | collective-permute-start | bytes 1572872 | tf_op jit(solution)/shard_map/ppermute | solution.py:21
  16.5 18.6 %collective-permute-start.2 = (bf16[64,4096]{1,0:T(8,128)(2,1)S(1)}, bf16[64,4096]{1,0:T(8,128)(2,1)S(1)}, u32[]{:S(2)}, u32[]{:S(2)}) collective-permute-start(bf16[64,4096]{1,0:T(8,128)(2,1)S(1)} %get-tuple-element.16.refs_0_), channel_id=1, source_target_pairs={{0,1},{1,2},{2,3},{3,4},{4,5},{5,6},{6,7},{7,0},{8,9},{9,10},{10,1... | collective-permute-start | bytes 1572872 | tf_op jit(solution)/shard_map/ppermute | solution.py:35
  18.1 17.1 %collective-permute-start.6 = (bf16[64,4096]{1,0:T(8,128)(2,1)S(1)}, bf16[64,4096]{1,0:T(8,128)(2,1)}, u32[]{:S(2)}, u32[]{:S(2)}) collective-permute-start(bf16[64,4096]{1,0:T(8,128)(2,1)S(1)} %get-tuple-element.16.refs_0_), channel_id=1, source_target_pairs={{0,7},{1,0},{2,1},{3,2},{4,3},{5,4},{6,5},{7,6},{8,15},{9,8},{10,9... | collective-permute-start | bytes 1572872 | tf_op jit(solution)/shard_map/ppermute | solution.py:35
  30.1 52.8 %copy-start.12 = (bf16[64,4096]{1,0:T(8,128)(2,1)}, bf16[64,4096]{1,0:T(8,128)(2,1)S(1)}, u32[]{:S(2)}) copy-start(bf16[64,4096]{1,0:T(8,128)(2,1)S(1)} %collective-permute-done.5.refs_1_) | copy-start | bytes 1572868
  30.1 14.5 %collective-permute-start.9 = (bf16[64,4096]{1,0:T(8,128)(2,1)S(1)}, bf16[64,4096]{1,0:T(8,128)(2,1)}, u32[]{:S(2)}, u32[]{:S(2)}) collective-permute-start(bf16[64,4096]{1,0:T(8,128)(2,1)S(1)} %collective-permute-done.5.refs_1_), channel_id=1, source_target_pairs={{0,7},{1,0},{2,1},{3,2},{4,3},{5,4},{6,5},{7,6},{8,15},{9,8},{10,9... | collective-permute-start | bytes 1572872 | tf_op jit(solution)/shard_map/ppermute | solution.py:35
  35.1 13.0 %collective-permute-start.8 = (bf16[64,4096]{1,0:T(8,128)(2,1)S(1)}, bf16[64,4096]{1,0:T(8,128)(2,1)}, u32[]{:S(2)}, u32[]{:S(2)}) collective-permute-start(bf16[64,4096]{1,0:T(8,128)(2,1)S(1)} %collective-permute-done.5.refs_1_), channel_id=1, source_target_pairs={{0,1},{1,2},{2,3},{3,4},{4,5},{5,6},{6,7},{7,0},{8,9},{9,10},{10,1... | collective-permute-start | bytes 1572872 | tf_op jit(solution)/shard_map/ppermute | solution.py:35
  35.1 47.8 %copy-start.13 = (bf16[64,4096]{1,0:T(8,128)(2,1)}, bf16[64,4096]{1,0:T(8,128)(2,1)S(1)}, u32[]{:S(2)}) copy-start(bf16[64,4096]{1,0:T(8,128)(2,1)S(1)} %collective-permute-done.2.refs_2_) | copy-start | bytes 1572868
  35.1 28.8 %collective-permute-start.3 = (bf16[64,4096]{1,0:T(8,128)(2,1)S(1)}, bf16[64,4096]{1,0:T(8,128)(2,1)}, u32[]{:S(2)}, u32[]{:S(2)}) collective-permute-start(bf16[64,4096]{1,0:T(8,128)(2,1)S(1)} %collective-permute-done.2.refs_2_), channel_id=1, source_target_pairs={{0,1},{1,2},{2,3},{3,4},{4,5},{5,6},{6,7},{7,0},{8,9},{9,10},{10,1... | collective-permute-start | bytes 1572872 | tf_op jit(solution)/shard_map/ppermute | solution.py:35
  35.2 28.8 %collective-permute-start.7 = (bf16[64,4096]{1,0:T(8,128)(2,1)}, bf16[64,4096]{1,0:T(8,128)(2,1)}, u32[]{:S(2)}, u32[]{:S(2)}) collective-permute-start(bf16[64,4096]{1,0:T(8,128)(2,1)} %collective-permute-done.6.refs_3_), channel_id=1, source_target_pairs={{0,7},{1,0},{2,1},{3,2},{4,3},{5,4},{6,5},{7,6},{8,15},{9,8},{10,9... | collective-permute-start | bytes 1572872 | tf_op jit(solution)/shard_map/ppermute | solution.py:35
  44.6 22.6 %collective-permute-start.11 = (bf16[64,4096]{1,0:T(8,128)(2,1)}, bf16[64,4096]{1,0:T(8,128)(2,1)}, u32[]{:S(2)}, u32[]{:S(2)}) collective-permute-start(bf16[64,4096]{1,0:T(8,128)(2,1)} %collective-permute-done.9.refs_7_), channel_id=1, source_target_pairs={{0,7},{1,0},{2,1},{3,2},{4,3},{5,4},{6,5},{7,6},{8,15},{9,8},{10,9... | collective-permute-start | bytes 1572872 | tf_op jit(solution)/shard_map/ppermute | solution.py:35
  48.1 22.5 %collective-permute-start.17 = (bf16[64,4096]{1,0:T(8,128)(2,1)}, bf16[64,4096]{1,0:T(8,128)(2,1)}, u32[]{:S(2)}, u32[]{:S(2)}) collective-permute-start(bf16[64,4096]{1,0:T(8,128)(2,1)} %collective-permute-done.8.refs_6_), channel_id=1, source_target_pairs={{0,1},{1,2},{2,3},{3,4},{4,5},{5,6},{6,7},{7,0},{8,9},{9,10},{10,1... | collective-permute-start | bytes 1572872 | tf_op jit(solution)/shard_map/ppermute | solution.py:35
  48.1 12.4 %collective-permute-start = (f32[2,2048]{1,0:T(2,128)S(1)}, f32[2,2048]{1,0:T(2,128)S(1)}, u32[]{:S(2)}, u32[]{:S(2)}) collective-permute-start(f32[2,2048]{1,0:T(2,128)S(1)} %bitcast.50), channel_id=1, source_target_pairs={{0,0},{8,16},{16,8},{24,24},{1,1},{9,17},{17,9},{25,25},{2,2},{10,... | collective-permute-start | bytes 49160 | tf_op jit(solution)/shard_map/ppermute | solution.py:25
  62.4 1.0 copy-start
  63.9 36.0 %collective-permute-start.4 = (bf16[64,4096]{1,0:T(8,128)(2,1)}, bf16[64,4096]{1,0:T(8,128)(2,1)S(1)}, u32[]{:S(2)}, u32[]{:S(2)}) collective-permute-start(bf16[64,4096]{1,0:T(8,128)(2,1)} %collective-permute-done.3.refs_4_), channel_id=1, source_target_pairs={{0,1},{1,2},{2,3},{3,4},{4,5},{5,6},{6,7},{7,0},{8,9},{9,10},{10,1... | collective-permute-start | bytes 1572872 | tf_op jit(solution)/shard_map/ppermute | solution.py:35
  64.0 36.7 %collective-permute-start.16 = (bf16[64,4096]{1,0:T(8,128)(2,1)}, bf16[64,4096]{1,0:T(8,128)(2,1)}, u32[]{:S(2)}, u32[]{:S(2)}) collective-permute-start(bf16[64,4096]{1,0:T(8,128)(2,1)} %collective-permute-done.7.refs_5_), channel_id=1, source_target_pairs={{0,7},{1,0},{2,1},{3,2},{4,3},{5,4},{6,5},{7,6},{8,15},{9,8},{10,9... | collective-permute-start | bytes 1572872 | tf_op jit(solution)/shard_map/ppermute | solution.py:35
  67.2 28.8 %collective-permute-start.12 = (bf16[64,4096]{1,0:T(8,128)(2,1)}, bf16[64,4096]{1,0:T(8,128)(2,1)S(1)}, u32[]{:S(2)}, u32[]{:S(2)}) collective-permute-start(bf16[64,4096]{1,0:T(8,128)(2,1)} %collective-permute-done.11.refs_3_), channel_id=1, source_target_pairs={{0,7},{1,0},{2,1},{3,2},{4,3},{5,4},{6,5},{7,6},{8,15},{9,8},{10,9... | collective-permute-start | bytes 1572872 | tf_op jit(solution)/shard_map/ppermute | solution.py:35
  70.6 30.1 %collective-permute-start.18 = (bf16[64,4096]{1,0:T(8,128)(2,1)}, bf16[64,4096]{1,0:T(8,128)(2,1)}, u32[]{:S(2)}, u32[]{:S(2)}) collective-permute-start(bf16[64,4096]{1,0:T(8,128)(2,1)} %collective-permute-done.17.refs_2_), channel_id=1, source_target_pairs={{0,1},{1,2},{2,3},{3,4},{4,5},{5,6},{6,7},{7,0},{8,9},{9,10},{10,1... | collective-permute-start | bytes 1572872 | tf_op jit(solution)/shard_map/ppermute | solution.py:35
  96.0 0.8 copy-start.9
  96.8 17.1 %collective-permute-start.13 = (bf16[64,4096]{1,0:T(8,128)(2,1)}, bf16[64,4096]{1,0:T(8,128)(2,1)S(1)}, u32[]{:S(2)}, u32[]{:S(2)}) collective-permute-start(bf16[64,4096]{1,0:T(8,128)(2,1)} %after.6.refs_5_), channel_id=1, source_target_pairs={{0,7},{1,0},{2,1},{3,2},{4,3},{5,4},{6,5},{7,6},{8,15},{9,8},{10,9... | collective-permute-start | bytes 1572872 | tf_op jit(solution)/shard_map/ppermute | solution.py:35
  99.9 0.8 copy-start.6
  100.7 14.4 %collective-permute-start.10 = (bf16[64,4096]{1,0:T(8,128)(2,1)}, bf16[64,4096]{1,0:T(8,128)(2,1)S(1)}, u32[]{:S(2)}, u32[]{:S(2)}) collective-permute-start(bf16[64,4096]{1,0:T(8,128)(2,1)} %after.5.refs_0_), channel_id=1, source_target_pairs={{0,1},{1,2},{2,3},{3,4},{4,5},{5,6},{6,7},{7,0},{8,9},{9,10},{10,1... | collective-permute-start | bytes 1572872 | tf_op jit(solution)/shard_map/ppermute | solution.py:35
  112.4 1.1 copy-start.11
  112.4 4.1 %collective-permute-start.19 = (bf16[8,64,768]{2,1,0:T(8,128)(2,1)}, bf16[8,64,768]{2,1,0:T(8,128)(2,1)S(1)}, u32[]{:S(2)}, u32[]{:S(2)}) collective-permute-start(bf16[8,64,768]{2,1,0:T(8,128)(2,1)} %after.7), channel_id=1, source_target_pairs={{0,16},{16,0},{1,17},{17,1},{2,18},{18,2},{3,19},{19,3},{4,20},{20... | collective-permute-start | bytes 2359304 | tf_op jit(solution)/shard_map/ppermute | solution.py:17
  113.4 3.0 %collective-permute-start.20 = (bf16[6,64,768]{2,1,0:T(8,128)(2,1)S(1)}, bf16[6,64,768]{2,1,0:T(8,128)(2,1)S(1)}, u32[]{:S(2)}, u32[]{:S(2)}) collective-permute-start(bf16[6,64,768]{2,1,0:T(8,128)(2,1)S(1)} %copy-done.11), channel_id=1, source_target_pairs={{0,16},{16,0},{1,17},{17,1},{2,18},{18,2},{3,19},{19,3},{4,20},{20... | collective-permute-start | bytes 1769480 | tf_op jit(solution)/shard_map/ppermute | solution.py:17
  114.0 4.0 %copy-start.4 = (bf16[64,4096]{1,0:T(8,128)(2,1)}, bf16[64,4096]{1,0:T(8,128)(2,1)S(1)}, u32[]{:S(2)}) copy-start(bf16[64,4096]{1,0:T(8,128)(2,1)S(1)} %collective-permute-done.13.two) | copy-start | bytes 1572868
  114.0 2.5 %collective-permute-start.15 = (bf16[64,4096]{1,0:T(8,128)(2,1)S(1)}, bf16[64,4096]{1,0:T(8,128)(2,1)S(1)}, u32[]{:S(2)}, u32[]{:S(2)}) collective-permute-start(bf16[64,4096]{1,0:T(8,128)(2,1)S(1)} %collective-permute-done.13.two), channel_id=1, source_target_pairs={{0,16},{16,0},{1,17},{17,1},{2,18},{18,2},{3,19},{19,3},{4,20},{20... | collective-permute-start | bytes 1572872 | tf_op jit(solution)/shard_map/ppermute | solution.py:17
  115.0 2.9 %copy-start.5 = (bf16[64,4096]{1,0:T(8,128)(2,1)}, bf16[64,4096]{1,0:T(8,128)(2,1)S(1)}, u32[]{:S(2)}) copy-start(bf16[64,4096]{1,0:T(8,128)(2,1)S(1)} %collective-permute-done.10.one) | copy-start | bytes 1572868
  115.0 2.9 %collective-permute-start.14 = (bf16[64,4096]{1,0:T(8,128)(2,1)S(1)}, bf16[64,4096]{1,0:T(8,128)(2,1)S(1)}, u32[]{:S(2)}, u32[]{:S(2)}) collective-permute-start(bf16[64,4096]{1,0:T(8,128)(2,1)S(1)} %collective-permute-done.10.one), channel_id=1, source_target_pairs={{0,16},{16,0},{1,17},{17,1},{2,18},{18,2},{3,19},{19,3},{4,20},{20... | collective-permute-start | bytes 1572872 | tf_op jit(solution)/shard_map/ppermute | solution.py:17
  116.4 1.5 copy-start.3
  116.4 1.5 copy-start.2
  116.5 1.5 copy-start.7
  118.0 0.8 copy-start.8
  168.4 4.5 %collective-permute-start.21 = (bf16[8,128,256]{2,1,0:T(8,128)(2,1)S(1)}, bf16[8,128,256]{2,1,0:T(8,128)(2,1)S(1)}, u32[]{:S(2)}, u32[]{:S(2)}) collective-permute-start(bf16[8,128,256]{2,1,0:T(8,128)(2,1)S(1)} %dynamic-slice_bitcast_fusion), channel_id=1, source_target_pairs={{0,16},{16,0},{1,17},{17,1},{2,18},{18,2},{3,19},{19,3},{4,20},{20... | collective-permute-start | bytes 1572872 | tf_op jit(solution)/shard_map/ppermute | solution.py:17
Sparse Core Ops, SparseCore 0:
  9.9 72.9 all-gather.2

commit v4 on v3

--- a/solution.py
+++ b/solution.py
@@ -66,7 +66,7 @@
     + [(0, 3), (0, 5), (1, 2), (1, 6), (1, 3), (1, 5)]
     + [(0, 4), (1, 4)]
 )
-BATCHES = ((0, 8), (8, 14), (14, 16))
+BATCHES = ((0, 5), (5, 14), (14, 16))
 
 
 def project_kernel(count, core_ref, *refs):

time: 183 us -> 181 us (0.989)
    all_gather x1, waiting for transfers between devices: 12.3 us -> 10.3 us  [gather_weight(): lax.all_gather(weight, ('y', 'xl', 'c', 'xh'), axis=0, tiled=False, axis_...]
  transfers between devices with their start and end apart: 23 -> 23, of which waited for: 9 -> 8; matrix products, arithmetic and copies ran while one was open for 3% -> 3% of each run, Pallas kernels for 14% -> 14%
where the time goes in v4:
time: 181 us; the launch traced here: 180 us
  starting transfers between devices  46.7 us (26%)
  Pallas kernels  41.4 us (23%)
  waiting for transfers between devices  34.2 us (19%)
  blocking collectives  33.5 us (19%)
  between operations  13.8 us (8%)
  local copies, waits for them, and re-layouts  5.69 us (3%)
  other arithmetic  5.17 us (3%)
    all_to_all x1, blocking collectives, shards(): lax.all_to_all(mixed, ('xh', 'z'), split_axis=0, concat_axis=0, tiled=True)  33.5 us
    ppermute x14, starting transfers between devices, ring_z(): return lax.ppermute(value, 'z', [(i, (i + step) % 8) for i in range(8)])  26.5 us
    pallas_call x2, Pallas kernels, project(): pl.pallas_call(functools.partial(project_kernel, len(pieces)), out_shape=...  24.8 us
    pallas_call x1, Pallas kernels, finish(): pl.pallas_call(finish_kernel, out_shape=jax.ShapeDtypeStruct((16, 128, 25...  16.1 us
    ppermute x1, starting transfers between devices, swap_roles(): return lax.ppermute(value, ('c', 'xh'), [(0, 0), (1, 2), (2, 1), (3, 3)])  10.6 us
    all_gather x1, waiting for transfers between devices, gather_weight(): lax.all_gather(weight, ('y', 'xl', 'c', 'xh'), axis=0, tiled=False, axis_...  10.3 us
    ppermute x14, waiting for transfers between devices, ring_z(): return lax.ppermute(value, 'z', [(i, (i + step) % 8) for i in range(8)])  8.88 us
    ppermute x6, starting transfers between devices, swap_core(): return lax.ppermute(value, 'c', [(0, 1), (1, 0)])  8.48 us
  transfers between devices with their start and end apart: 23, of which 8 were waited for; matrix products, arithmetic and copies ran while one was open for 3% of the time, Pallas kernels for 14%

profile of v4, /device:TPU:1, one launch (start us, length us, event | category | flops | bytes accessed | tf_op | source)
XLA Modules:
  0.0 180.4 jit_solution(9841493960615720185)
XLA Ops:
  6.5 1.9 %pad_maximum_fusion = bf16[256,768]{1,0:T(8,128)(2,1)} fusion(bf16[256,256]{1,0:T(8,128)(2,1)} %param.8, bf16[256,256]{1,0:T(8,128)(2,1)} %param.7, bf16[256,256]{1,0:T(8,128)(2,1)} %param.6), kind=kLoop, calls=%fused_computation.9 | loop fusion | flops 1179648 | bytes 786432 | tf_op jit(solution)/shard_map/concatenate | solution.py:238
  8.5 1.5 multiply_reduce_fusion
  10.0 0.1 rsqrt.12
  10.1 0.3 multiply_convert_fusion
  10.4 3.3 %collective-permute-start.1 = (bf16[64,4096]{1,0:T(8,128)(2,1)S(1)}, bf16[64,4096]{1,0:T(8,128)(2,1)S(1)}, u32[]{:S(2)}, u32[]{:S(2)}) collective-permute-start(bf16[64,4096]{1,0:T(8,128)(2,1)S(1)} %dynamic-slice_bitcast_fusion.1), channel_id=1, source_target_pairs={{0,16},{16,0},{1,17},{17,1},{2,18},{18,2},{3,19},{19,3},{4,20},{20... | collective-permute-start | bytes 1572872 | tf_op jit(solution)/shard_map/ppermute | solution.py:17
  13.7 1.5 collective-permute-done.1
  15.3 0.1 bitcast_select_fusion.2
  15.4 1.1 collective-permute-start.5
  16.4 1.6 collective-permute-start.2
  18.1 3.9 %collective-permute-start.6 = (bf16[64,4096]{1,0:T(8,128)(2,1)S(1)}, bf16[64,4096]{1,0:T(8,128)(2,1)S(1)}, u32[]{:S(2)}, u32[]{:S(2)}) collective-permute-start(bf16[64,4096]{1,0:T(8,128)(2,1)S(1)} %get-tuple-element.16.refs_0_), channel_id=1, source_target_pairs={{0,7},{1,0},{2,1},{3,2},{4,3},{5,4},{6,5},{7,6},{8,15},{9,8},{10,9... | collective-permute-start | bytes 1572872 | tf_op jit(solution)/shard_map/ppermute | solution.py:35
  22.0 8.1 %collective-permute-done.5.refs_1_ = bf16[64,4096]{1,0:T(8,128)(2,1)S(1)} collective-permute-done((bf16[64,4096]{1,0:T(8,128)(2,1)S(1)}, bf16[64,4096]{1,0:T(8,128)(2,1)S(1)}, u32[]{:S(2)}, u32[]{:S(2)}) %collective-permute-start.5) | collective-permute-done | bytes 524320 | tf_op jit(solution)/shard_map/ppermute | solution.py:21
  30.1 5.0 %collective-permute-start.8 = (bf16[64,4096]{1,0:T(8,128)(2,1)S(1)}, bf16[64,4096]{1,0:T(8,128)(2,1)S(1)}, u32[]{:S(2)}, u32[]{:S(2)}) collective-permute-start(bf16[64,4096]{1,0:T(8,128)(2,1)S(1)} %collective-permute-done.5.refs_1_), channel_id=1, source_target_pairs={{0,7},{1,0},{2,1},{3,2},{4,3},{5,4},{6,5},{7,6},{8,15},{9,8},{10,9... | collective-permute-start | bytes 1572872 | tf_op jit(solution)/shard_map/ppermute | solution.py:35
  35.1 0.1 collective-permute-start.3
  35.2 2.7 %collective-permute-start.14 = (bf16[64,4096]{1,0:T(8,128)(2,1)S(1)}, bf16[64,4096]{1,0:T(8,128)(2,1)}, u32[]{:S(2)}, u32[]{:S(2)}) collective-permute-start(bf16[64,4096]{1,0:T(8,128)(2,1)S(1)} %collective-permute-done.6.refs_3_), channel_id=1, source_target_pairs={{0,7},{1,0},{2,1},{3,2},{4,3},{5,4},{6,5},{7,6},{8,15},{9,8},{10,9... | collective-permute-start | bytes 1572872 | tf_op jit(solution)/shard_map/ppermute | solution.py:35
  37.9 6.8 %collective-permute-done.8.refs_2_ = bf16[64,4096]{1,0:T(8,128)(2,1)S(1)} collective-permute-done((bf16[64,4096]{1,0:T(8,128)(2,1)S(1)}, bf16[64,4096]{1,0:T(8,128)(2,1)S(1)}, u32[]{:S(2)}, u32[]{:S(2)}) %collective-permute-start.8) | collective-permute-done | bytes 524320 | tf_op jit(solution)/shard_map/ppermute | solution.py:35
  44.6 3.4 %collective-permute-start.9 = (bf16[64,4096]{1,0:T(8,128)(2,1)S(1)}, bf16[64,4096]{1,0:T(8,128)(2,1)}, u32[]{:S(2)}, u32[]{:S(2)}) collective-permute-start(bf16[64,4096]{1,0:T(8,128)(2,1)S(1)} %collective-permute-done.8.refs_2_), channel_id=1, source_target_pairs={{0,7},{1,0},{2,1},{3,2},{4,3},{5,4},{6,5},{7,6},{8,15},{9,8},{10,9... | collective-permute-start | bytes 1572872 | tf_op jit(solution)/shard_map/ppermute | solution.py:35
  48.0 10.6 %collective-permute-start = (f32[2,2048]{1,0:T(2,128)S(1)}, f32[2,2048]{1,0:T(2,128)S(1)}, u32[]{:S(2)}, u32[]{:S(2)}) collective-permute-start(f32[2,2048]{1,0:T(2,128)S(1)} %bitcast.50), channel_id=1, source_target_pairs={{0,0},{8,16},{16,8},{24,24},{1,1},{9,17},{17,9},{25,25},{2,2},{10,... | collective-permute-start | bytes 49160 | tf_op jit(solution)/shard_map/ppermute | solution.py:25
  58.8 0.6 stack.67.refs_1_.chunk_ref
  59.4 1.0 collective-permute-done
  60.5 1.2 reduce-window.6
  61.7 0.2 slice_reduce_fusion
  61.9 0.1 collective-permute-start.4
  62.0 3.0 %collective-permute-start.16 = (bf16[64,4096]{1,0:T(8,128)(2,1)}, bf16[64,4096]{1,0:T(8,128)(2,1)}, u32[]{:S(2)}, u32[]{:S(2)}) collective-permute-start(bf16[64,4096]{1,0:T(8,128)(2,1)} %collective-permute-done.14.refs_0_), channel_id=1, source_target_pairs={{0,7},{1,0},{2,1},{3,2},{4,3},{5,4},{6,5},{7,6},{8,15},{9,8},{10,9... | collective-permute-start | bytes 1572872 | tf_op jit(solution)/shard_map/ppermute | solution.py:35
  65.0 2.1 %collective-permute-done.9.refs_6_ = bf16[64,4096]{1,0:T(8,128)(2,1)} collective-permute-done((bf16[64,4096]{1,0:T(8,128)(2,1)S(1)}, bf16[64,4096]{1,0:T(8,128)(2,1)}, u32[]{:S(2)}, u32[]{:S(2)}) %collective-permute-start.9) | collective-permute-done | bytes 524320 | tf_op jit(solution)/shard_map/ppermute | solution.py:35
  67.1 3.5 %collective-permute-start.10 = (bf16[64,4096]{1,0:T(8,128)(2,1)}, bf16[64,4096]{1,0:T(8,128)(2,1)}, u32[]{:S(2)}, u32[]{:S(2)}) collective-permute-start(bf16[64,4096]{1,0:T(8,128)(2,1)} %collective-permute-done.9.refs_6_), channel_id=1, source_target_pairs={{0,7},{1,0},{2,1},{3,2},{4,3},{5,4},{6,5},{7,6},{8,15},{9,8},{10,9... | collective-permute-start | bytes 1572872 | tf_op jit(solution)/shard_map/ppermute | solution.py:35
  70.6 0.1 broadcast_add_fusion
  70.7 0.4 copy.19
  71.1 0.9 copy.20.refs_2_.refs_4_
  72.0 0.5 after.4.core_ref
  72.6 10.3 %all-gather.3.cloned.1.call-done = bf16[8192,768]{1,0:T(8,128)(2,1)} async-done(((bf16[256,768]{1,0:T(8,128)(2,1)}), bf16[8192,768]{1,0:T(8,128)(2,1)}) %all-gather.3.cloned.1.call-update) | async-done | bytes 12582928 | tf_op jit(solution)/shard_map/all_gather | solution.py:58
  82.9 11.0 %project.2 = (bf16[5,64,768]{2,1,0:T(8,128)(2,1)}, bf16[5,64,768]{2,1,0:T(8,128)(2,1)}) custom-call(s32[1]{0:T(128)} %after.4.core_ref, bf16[64,4096]{1,0:T(8,128)(2,1)} %copy-done.2, bf16[64,4096]{1,0:T(8,128)(2,1)} %copy-done.4, bf16[64,4096]{1,0:T(8,128)(2,1)} %copy-done.5, bf16[64,4096]{1,0:T(8,128)(2,1)} %copy-done.6, ...), custom_call_target="tpu_custom_call" | custom-call | flops 4026531840 | bytes 17825792 | tf_op jit(solution)/shard_map/project/pallas_call | solution.py:100
  93.9 3.1 %collective-permute-start.11 = (bf16[64,4096]{1,0:T(8,128)(2,1)}, bf16[64,4096]{1,0:T(8,128)(2,1)S(1)}, u32[]{:S(2)}, u32[]{:S(2)}) collective-permute-start(bf16[64,4096]{1,0:T(8,128)(2,1)} %after.6.refs_8_), channel_id=1, source_target_pairs={{0,7},{1,0},{2,1},{3,2},{4,3},{5,4},{6,5},{7,6},{8,15},{9,8},{10,9... | collective-permute-start | bytes 1572872 | tf_op jit(solution)/shard_map/ppermute | solution.py:35
  97.0 13.8 %project.3 = (bf16[9,64,768]{2,1,0:T(8,128)(2,1)}, bf16[9,64,768]{2,1,0:T(8,128)(2,1)}) custom-call(s32[1]{0:T(128)} %after.4.core_ref, bf16[64,4096]{1,0:T(8,128)(2,1)} %collective-permute-done.14.refs_0_, bf16[64,4096]{1,0:T(8,128)(2,1)} %collective-permute-done.15.refs_1_, bf16[64,4096]{1,0:T(8,128)(2,1)} %copy-done.12, bf16[64,4096]{1,0:T(8,128)(2,1)} %after.5.refs_3_, ...), custom_call_target="tpu_custom_call" | custom-call | flops 7247757312 | bytes 22020096 | tf_op jit(solution)/shard_map/project/pallas_call | solution.py:100
  110.8 0.5 collective-permute-start.20
  111.4 0.1 collective-permute-start.13
  111.5 1.3 collective-permute-start.12
  112.7 2.9 %collective-permute-done.19.refs_2_ = bf16[5,64,768]{2,1,0:T(8,128)(2,1)S(1)} collective-permute-done((bf16[5,64,768]{2,1,0:T(8,128)(2,1)}, bf16[5,64,768]{2,1,0:T(8,128)(2,1)S(1)}, u32[]{:S(2)}, u32[]{:S(2)}) %collective-permute-start.19) | collective-permute-done | bytes 491552 | tf_op jit(solution)/shard_map/ppermute | solution.py:17
  115.7 0.7 copy-done.11
  116.4 0.3 copy-done.3
  116.7 0.2 copy-done.9
  116.9 0.2 copy-done.10
  117.1 16.1 %finish.1 = bf16[16,128,256]{2,1,0:T(8,128)(2,1)} custom-call(s32[16]{0:T(128)} %stack.67.refs_1_.chunk_ref, s32[1]{0:T(128)} %after.4.core_ref, bf16[64,4096]{1,0:T(8,128)(2,1)} %copy-done.8, bf16[64,4096]{1,0:T(8,128)(2,1)} %copy-done.7, bf16[64,4096]{1,0:T(8,128)(2,1)} %copy-done.10, bf16[64,4096]{1,0:T(8,128)(2,1)} %copy-done.9, ...), custom_call_target="tpu_custom_call" | custom-call | flops 2415919104 | bytes 12582912 | tf_op jit(solution)/shard_map/finish/pallas_call | solution.py:208
  133.1 33.5 %all_to_all.5 = bf16[16,128,256]{2,1,0:T(8,128)(2,1)S(1)} all-to-all(bf16[16,128,256]{2,1,0:T(8,128)(2,1)} %finish.1), channel_id=1, replica_groups=mesh['y'=4,'xl'=2,'c'=2,'xh'=2,'z'=8] {'xh','z'}, dimensions={0} | all-to-all | bytes 2097152 | tf_op jit(solution)/shard_map/all_to_all | solution.py:275
  166.6 3.2 %collective-permute-start.21 = (bf16[8,128,256]{2,1,0:T(8,128)(2,1)S(1)}, bf16[8,128,256]{2,1,0:T(8,128)(2,1)S(1)}, u32[]{:S(2)}, u32[]{:S(2)}) collective-permute-start(bf16[8,128,256]{2,1,0:T(8,128)(2,1)S(1)} %dynamic-slice_bitcast_fusion), channel_id=1, source_target_pairs={{0,16},{16,0},{1,17},{17,1},{2,18},{18,2},{3,19},{19,3},{4,20},{20... | collective-permute-start | bytes 1572872 | tf_op jit(solution)/shard_map/ppermute | solution.py:17
  169.9 1.5 collective-permute-done.21
  171.5 0.1 maximum_bitcast_fusion
  171.6 0.7 copy.22
  172.3 1.3 copy.23
  (57 shorter events, 0.4 us)
Async XLA Ops:
  6.5 3.5 %copy-start.1 = (bf16[1,128,4096]{2,1,0:T(8,128)(2,1)S(1)}, bf16[1,128,4096]{2,1,0:T(8,128)(2,1)}, u32[]{:S(2)}) copy-start(bf16[1,128,4096]{2,1,0:T(8,128)(2,1)} %param.5) | copy-start | bytes 3145732
  6.5 76.3 %all-gather.3.cloned.1.call-start = ((), (), s32[]{:S(2)}) async-start(), calls=%async_computation.1 | async-start | bytes 12976128 | tf_op jit(solution)/shard_map/all_gather | solution.py:58
  10.3 37.7 %copy-start.13 = (f32[1,2,2048]{2,1,0:T(2,128)S(1)}, f32[1,2,2048]{2,1,0:T(2,128)}, u32[]{:S(2)}) copy-start(f32[1,2,2048]{2,1,0:T(2,128)} %param.9) | copy-start | bytes 49156
  10.4 4.9 %collective-permute-start.1 = (bf16[64,4096]{1,0:T(8,128)(2,1)S(1)}, bf16[64,4096]{1,0:T(8,128)(2,1)S(1)}, u32[]{:S(2)}, u32[]{:S(2)}) collective-permute-start(bf16[64,4096]{1,0:T(8,128)(2,1)S(1)} %dynamic-slice_bitcast_fusion.1), channel_id=1, source_target_pairs={{0,16},{16,0},{1,17},{17,1},{2,18},{18,2},{3,19},{19,3},{4,20},{20... | collective-permute-start | bytes 1572872 | tf_op jit(solution)/shard_map/ppermute | solution.py:17
  15.3 67.5 %copy-start.2 = (bf16[64,4096]{1,0:T(8,128)(2,1)}, bf16[64,4096]{1,0:T(8,128)(2,1)S(1)}, u32[]{:S(2)}) copy-start(bf16[64,4096]{1,0:T(8,128)(2,1)S(1)} %get-tuple-element.16.refs_0_) | copy-start | bytes 1572868
  15.4 14.7 %collective-permute-start.5 = (bf16[64,4096]{1,0:T(8,128)(2,1)S(1)}, bf16[64,4096]{1,0:T(8,128)(2,1)S(1)}, u32[]{:S(2)}, u32[]{:S(2)}) collective-permute-start(bf16[64,4096]{1,0:T(8,128)(2,1)S(1)} %get-tuple-element.15), channel_id=1, source_target_pairs={{0,8},{8,0},{1,9},{9,1},{2,10},{10,2},{3,11},{11,3},{4,12},{12,4},... | collective-permute-start | bytes 1572872 | tf_op jit(solution)/shard_map/ppermute | solution.py:21
  16.4 18.6 %collective-permute-start.2 = (bf16[64,4096]{1,0:T(8,128)(2,1)S(1)}, bf16[64,4096]{1,0:T(8,128)(2,1)S(1)}, u32[]{:S(2)}, u32[]{:S(2)}) collective-permute-start(bf16[64,4096]{1,0:T(8,128)(2,1)S(1)} %get-tuple-element.16.refs_0_), channel_id=1, source_target_pairs={{0,1},{1,2},{2,3},{3,4},{4,5},{5,6},{6,7},{7,0},{8,9},{9,10},{10,1... | collective-permute-start | bytes 1572872 | tf_op jit(solution)/shard_map/ppermute | solution.py:35
  18.1 17.1 %collective-permute-start.6 = (bf16[64,4096]{1,0:T(8,128)(2,1)S(1)}, bf16[64,4096]{1,0:T(8,128)(2,1)S(1)}, u32[]{:S(2)}, u32[]{:S(2)}) collective-permute-start(bf16[64,4096]{1,0:T(8,128)(2,1)S(1)} %get-tuple-element.16.refs_0_), channel_id=1, source_target_pairs={{0,7},{1,0},{2,1},{3,2},{4,3},{5,4},{6,5},{7,6},{8,15},{9,8},{10,9... | collective-permute-start | bytes 1572872 | tf_op jit(solution)/shard_map/ppermute | solution.py:35
  30.1 52.8 %copy-start.4 = (bf16[64,4096]{1,0:T(8,128)(2,1)}, bf16[64,4096]{1,0:T(8,128)(2,1)S(1)}, u32[]{:S(2)}) copy-start(bf16[64,4096]{1,0:T(8,128)(2,1)S(1)} %collective-permute-done.5.refs_1_) | copy-start | bytes 1572868
  30.1 14.5 %collective-permute-start.8 = (bf16[64,4096]{1,0:T(8,128)(2,1)S(1)}, bf16[64,4096]{1,0:T(8,128)(2,1)S(1)}, u32[]{:S(2)}, u32[]{:S(2)}) collective-permute-start(bf16[64,4096]{1,0:T(8,128)(2,1)S(1)} %collective-permute-done.5.refs_1_), channel_id=1, source_target_pairs={{0,7},{1,0},{2,1},{3,2},{4,3},{5,4},{6,5},{7,6},{8,15},{9,8},{10,9... | collective-permute-start | bytes 1572872 | tf_op jit(solution)/shard_map/ppermute | solution.py:35
  35.1 13.0 %collective-permute-start.15 = (bf16[64,4096]{1,0:T(8,128)(2,1)S(1)}, bf16[64,4096]{1,0:T(8,128)(2,1)}, u32[]{:S(2)}, u32[]{:S(2)}) collective-permute-start(bf16[64,4096]{1,0:T(8,128)(2,1)S(1)} %collective-permute-done.5.refs_1_), channel_id=1, source_target_pairs={{0,1},{1,2},{2,3},{3,4},{4,5},{5,6},{6,7},{7,0},{8,9},{9,10},{10,1... | collective-permute-start | bytes 1572872 | tf_op jit(solution)/shard_map/ppermute | solution.py:35
  35.1 47.8 %copy-start.5 = (bf16[64,4096]{1,0:T(8,128)(2,1)}, bf16[64,4096]{1,0:T(8,128)(2,1)S(1)}, u32[]{:S(2)}) copy-start(bf16[64,4096]{1,0:T(8,128)(2,1)S(1)} %collective-permute-done.2.refs_2_) | copy-start | bytes 1572868
  35.1 26.8 %collective-permute-start.3 = (bf16[64,4096]{1,0:T(8,128)(2,1)S(1)}, bf16[64,4096]{1,0:T(8,128)(2,1)}, u32[]{:S(2)}, u32[]{:S(2)}) collective-permute-start(bf16[64,4096]{1,0:T(8,128)(2,1)S(1)} %collective-permute-done.2.refs_2_), channel_id=1, source_target_pairs={{0,1},{1,2},{2,3},{3,4},{4,5},{5,6},{6,7},{7,0},{8,9},{9,10},{10,1... | collective-permute-start | bytes 1572872 | tf_op jit(solution)/shard_map/ppermute | solution.py:35
  35.2 47.7 %copy-start.6 = (bf16[64,4096]{1,0:T(8,128)(2,1)}, bf16[64,4096]{1,0:T(8,128)(2,1)S(1)}, u32[]{:S(2)}) copy-start(bf16[64,4096]{1,0:T(8,128)(2,1)S(1)} %collective-permute-done.6.refs_3_) | copy-start | bytes 1572868
  35.2 26.8 %collective-permute-start.14 = (bf16[64,4096]{1,0:T(8,128)(2,1)S(1)}, bf16[64,4096]{1,0:T(8,128)(2,1)}, u32[]{:S(2)}, u32[]{:S(2)}) collective-permute-start(bf16[64,4096]{1,0:T(8,128)(2,1)S(1)} %collective-permute-done.6.refs_3_), channel_id=1, source_target_pairs={{0,7},{1,0},{2,1},{3,2},{4,3},{5,4},{6,5},{7,6},{8,15},{9,8},{10,9... | collective-permute-start | bytes 1572872 | tf_op jit(solution)/shard_map/ppermute | solution.py:35
  44.6 26.0 %copy-start.12 = (bf16[64,4096]{1,0:T(8,128)(2,1)}, bf16[64,4096]{1,0:T(8,128)(2,1)S(1)}, u32[]{:S(2)}) copy-start(bf16[64,4096]{1,0:T(8,128)(2,1)S(1)} %collective-permute-done.8.refs_2_) | copy-start | bytes 1572868
  44.6 22.5 %collective-permute-start.9 = (bf16[64,4096]{1,0:T(8,128)(2,1)S(1)}, bf16[64,4096]{1,0:T(8,128)(2,1)}, u32[]{:S(2)}, u32[]{:S(2)}) collective-permute-start(bf16[64,4096]{1,0:T(8,128)(2,1)S(1)} %collective-permute-done.8.refs_2_), channel_id=1, source_target_pairs={{0,7},{1,0},{2,1},{3,2},{4,3},{5,4},{6,5},{7,6},{8,15},{9,8},{10,9... | collective-permute-start | bytes 1572872 | tf_op jit(solution)/shard_map/ppermute | solution.py:35
  48.0 22.6 %collective-permute-start.17 = (bf16[64,4096]{1,0:T(8,128)(2,1)}, bf16[64,4096]{1,0:T(8,128)(2,1)}, u32[]{:S(2)}, u32[]{:S(2)}) collective-permute-start(bf16[64,4096]{1,0:T(8,128)(2,1)} %collective-permute-done.15.refs_1_), channel_id=1, source_target_pairs={{0,1},{1,2},{2,3},{3,4},{4,5},{5,6},{6,7},{7,0},{8,9},{9,10},{10,1... | collective-permute-start | bytes 1572872 | tf_op jit(solution)/shard_map/ppermute | solution.py:35
  48.0 12.4 %collective-permute-start = (f32[2,2048]{1,0:T(2,128)S(1)}, f32[2,2048]{1,0:T(2,128)S(1)}, u32[]{:S(2)}, u32[]{:S(2)}) collective-permute-start(f32[2,2048]{1,0:T(2,128)S(1)} %bitcast.50), channel_id=1, source_target_pairs={{0,0},{8,16},{16,8},{24,24},{1,1},{9,17},{17,9},{25,25},{2,2},{10,... | collective-permute-start | bytes 49160 | tf_op jit(solution)/shard_map/ppermute | solution.py:25
  61.9 35.1 %collective-permute-start.4 = (bf16[64,4096]{1,0:T(8,128)(2,1)}, bf16[64,4096]{1,0:T(8,128)(2,1)}, u32[]{:S(2)}, u32[]{:S(2)}) collective-permute-start(bf16[64,4096]{1,0:T(8,128)(2,1)} %collective-permute-done.3.refs_4_), channel_id=1, source_target_pairs={{0,1},{1,2},{2,3},{3,4},{4,5},{5,6},{6,7},{7,0},{8,9},{9,10},{10,1... | collective-permute-start | bytes 1572872 | tf_op jit(solution)/shard_map/ppermute | solution.py:35
  62.0 35.0 %collective-permute-start.16 = (bf16[64,4096]{1,0:T(8,128)(2,1)}, bf16[64,4096]{1,0:T(8,128)(2,1)}, u32[]{:S(2)}, u32[]{:S(2)}) collective-permute-start(bf16[64,4096]{1,0:T(8,128)(2,1)} %collective-permute-done.14.refs_0_), channel_id=1, source_target_pairs={{0,7},{1,0},{2,1},{3,2},{4,3},{5,4},{6,5},{7,6},{8,15},{9,8},{10,9... | collective-permute-start | bytes 1572872 | tf_op jit(solution)/shard_map/ppermute | solution.py:35
  67.1 26.8 %collective-permute-start.10 = (bf16[64,4096]{1,0:T(8,128)(2,1)}, bf16[64,4096]{1,0:T(8,128)(2,1)}, u32[]{:S(2)}, u32[]{:S(2)}) collective-permute-start(bf16[64,4096]{1,0:T(8,128)(2,1)} %collective-permute-done.9.refs_6_), channel_id=1, source_target_pairs={{0,7},{1,0},{2,1},{3,2},{4,3},{5,4},{6,5},{7,6},{8,15},{9,8},{10,9... | collective-permute-start | bytes 1572872 | tf_op jit(solution)/shard_map/ppermute | solution.py:35
  70.6 26.4 %collective-permute-start.18 = (bf16[64,4096]{1,0:T(8,128)(2,1)}, bf16[64,4096]{1,0:T(8,128)(2,1)}, u32[]{:S(2)}, u32[]{:S(2)}) collective-permute-start(bf16[64,4096]{1,0:T(8,128)(2,1)} %collective-permute-done.17.refs_5_), channel_id=1, source_target_pairs={{0,1},{1,2},{2,3},{3,4},{4,5},{5,6},{6,7},{7,0},{8,9},{9,10},{10,1... | collective-permute-start | bytes 1572872 | tf_op jit(solution)/shard_map/ppermute | solution.py:35
  71.1 1.0 copy-start
  93.9 17.5 %collective-permute-start.11 = (bf16[64,4096]{1,0:T(8,128)(2,1)}, bf16[64,4096]{1,0:T(8,128)(2,1)S(1)}, u32[]{:S(2)}, u32[]{:S(2)}) collective-permute-start(bf16[64,4096]{1,0:T(8,128)(2,1)} %after.6.refs_8_), channel_id=1, source_target_pairs={{0,7},{1,0},{2,1},{3,2},{4,3},{5,4},{6,5},{7,6},{8,15},{9,8},{10,9... | collective-permute-start | bytes 1572872 | tf_op jit(solution)/shard_map/ppermute | solution.py:35
  97.0 14.5 %collective-permute-start.7 = (bf16[64,4096]{1,0:T(8,128)(2,1)}, bf16[64,4096]{1,0:T(8,128)(2,1)S(1)}, u32[]{:S(2)}, u32[]{:S(2)}) collective-permute-start(bf16[64,4096]{1,0:T(8,128)(2,1)} %after.5.refs_3_), channel_id=1, source_target_pairs={{0,1},{1,2},{2,3},{3,4},{4,5},{5,6},{6,7},{7,0},{8,9},{9,10},{10,1... | collective-permute-start | bytes 1572872 | tf_op jit(solution)/shard_map/ppermute | solution.py:35
  110.8 4.8 %collective-permute-start.20 = (bf16[9,64,768]{2,1,0:T(8,128)(2,1)}, bf16[9,64,768]{2,1,0:T(8,128)(2,1)S(1)}, u32[]{:S(2)}, u32[]{:S(2)}) collective-permute-start(bf16[9,64,768]{2,1,0:T(8,128)(2,1)} %get-tuple-element.12), channel_id=1, source_target_pairs={{0,16},{16,0},{1,17},{17,1},{2,18},{18,2},{3,19},{19,3},{4,20},{20... | collective-permute-start | bytes 2654216 | tf_op jit(solution)/shard_map/ppermute | solution.py:17
  111.3 4.3 %copy-start.7 = (bf16[64,4096]{1,0:T(8,128)(2,1)}, bf16[64,4096]{1,0:T(8,128)(2,1)S(1)}, u32[]{:S(2)}) copy-start(bf16[64,4096]{1,0:T(8,128)(2,1)S(1)} %collective-permute-done.11.two) | copy-start | bytes 1572868
  111.4 4.3 %collective-permute-start.13 = (bf16[64,4096]{1,0:T(8,128)(2,1)S(1)}, bf16[64,4096]{1,0:T(8,128)(2,1)S(1)}, u32[]{:S(2)}, u32[]{:S(2)}) collective-permute-start(bf16[64,4096]{1,0:T(8,128)(2,1)S(1)} %collective-permute-done.11.two), channel_id=1, source_target_pairs={{0,16},{16,0},{1,17},{17,1},{2,18},{18,2},{3,19},{19,3},{4,20},{20... | collective-permute-start | bytes 1572872 | tf_op jit(solution)/shard_map/ppermute | solution.py:17
  111.5 4.2 %copy-start.8 = (bf16[64,4096]{1,0:T(8,128)(2,1)}, bf16[64,4096]{1,0:T(8,128)(2,1)S(1)}, u32[]{:S(2)}) copy-start(bf16[64,4096]{1,0:T(8,128)(2,1)S(1)} %collective-permute-done.7.one) | copy-start | bytes 1572868
  111.5 4.2 %collective-permute-start.12 = (bf16[64,4096]{1,0:T(8,128)(2,1)S(1)}, bf16[64,4096]{1,0:T(8,128)(2,1)S(1)}, u32[]{:S(2)}, u32[]{:S(2)}) collective-permute-start(bf16[64,4096]{1,0:T(8,128)(2,1)S(1)} %collective-permute-done.7.one), channel_id=1, source_target_pairs={{0,16},{16,0},{1,17},{17,1},{2,18},{18,2},{3,19},{19,3},{4,20},{20... | collective-permute-start | bytes 1572872 | tf_op jit(solution)/shard_map/ppermute | solution.py:17
  112.7 2.9 %collective-permute-start.19 = (bf16[5,64,768]{2,1,0:T(8,128)(2,1)}, bf16[5,64,768]{2,1,0:T(8,128)(2,1)S(1)}, u32[]{:S(2)}, u32[]{:S(2)}) collective-permute-start(bf16[5,64,768]{2,1,0:T(8,128)(2,1)} %after.7), channel_id=1, source_target_pairs={{0,16},{16,0},{1,17},{17,1},{2,18},{18,2},{3,19},{19,3},{4,20},{20... | collective-permute-start | bytes 1474568 | tf_op jit(solution)/shard_map/ppermute | solution.py:17
  115.6 0.8 copy-start.11
  115.6 1.1 copy-start.3
  115.6 1.2 copy-start.9
  115.7 1.4 copy-start.10
  166.6 4.8 %collective-permute-start.21 = (bf16[8,128,256]{2,1,0:T(8,128)(2,1)S(1)}, bf16[8,128,256]{2,1,0:T(8,128)(2,1)S(1)}, u32[]{:S(2)}, u32[]{:S(2)}) collective-permute-start(bf16[8,128,256]{2,1,0:T(8,128)(2,1)S(1)} %dynamic-slice_bitcast_fusion), channel_id=1, source_target_pairs={{0,16},{16,0},{1,17},{17,1},{2,18},{18,2},{3,19},{19,3},{4,20},{20... | collective-permute-start | bytes 1572872 | tf_op jit(solution)/shard_map/ppermute | solution.py:17
Sparse Core Ops, SparseCore 0:
  9.9 72.9 all-gather.2

commit v5 on v4

--- a/solution.py
+++ b/solution.py
@@ -169,7 +169,7 @@
     states = [jnp.zeros((DH, DH), jnp.float32)] * 2
     for step in range(8):
         rows = all_ref[2 * step : 2 * step + 2].reshape(BLOCK, 768)
-        results = []
+        results, queries, locals_, updates = [], [], [], []
         for head in range(2):
             query = rows[:, head * DH : (head + 1) * DH]
             keys = rows[:, 256 + head * DH : 256 + (head + 1) * DH]
@@ -183,15 +183,28 @@
             weights = jnp.exp(jnp.where(causal, g_column - g_row, -jnp.inf))
             weighted = (scores * weights).astype(jnp.bfloat16)
             scaled_query = (query.astype(jnp.float32) * jnp.exp(g_column)).astype(jnp.bfloat16)
-            state = states[head]
-            attended = jnp.dot(weighted, values, preferred_element_type=jnp.float32) + jnp.dot(
-                scaled_query, state.astype(jnp.bfloat16), preferred_element_type=jnp.float32
-            )
+            queries.append(scaled_query)
+            local = jnp.dot(weighted, values, preferred_element_type=jnp.float32)
             faded_keys = (keys.astype(jnp.float32) * jnp.exp(total - g_column)).astype(jnp.bfloat16)
             update = lax.dot_general(
                 faded_keys, values, (((0,), (0,)), ((), ())), preferred_element_type=jnp.float32
             )
-            states[head] = jnp.exp(total) * state + update
+            locals_.append(local)
+            updates.append(jnp.exp(total) * states[head] + update)
+        zero = jnp.zeros((DH, DH), jnp.bfloat16)
+        both = jnp.concatenate(
+            (
+                jnp.concatenate((states[0].astype(jnp.bfloat16), zero), axis=1),
+                jnp.concatenate((zero, states[1].astype(jnp.bfloat16)), axis=1),
+            ),
+            axis=0,
+        )
+        carried = jnp.dot(
+            jnp.concatenate(queries, axis=1), both, preferred_element_type=jnp.float32
+        )
+        states = updates
+        for head in range(2):
+            attended = locals_[head] + carried[:, head * DH : (head + 1) * DH]
             inverse_rms = lax.rsqrt(jnp.mean(attended * attended, axis=-1, keepdims=True) + 1e-06)
             results.append((attended * inverse_rms).astype(jnp.bfloat16))
         mixed = jnp.concatenate(results, axis=1).reshape(2, BLOCK // 2, 2 * DH)

time: 181 us -> 181 us (level)
  no operation moved by 1% of the time
where the time goes in v5:
time: 181 us; the launch traced here: 180 us
  starting transfers between devices  46.4 us (26%)
  Pallas kernels  41.3 us (23%)
  waiting for transfers between devices  34.2 us (19%)
  blocking collectives  33.8 us (19%)
  between operations  13.8 us (8%)
  local copies, waits for them, and re-layouts  5.69 us (3%)
  other arithmetic  5.17 us (3%)
    all_to_all x1, blocking collectives, shards(): lax.all_to_all(mixed, ('xh', 'z'), split_axis=0, concat_axis=0, tiled=True)  33.8 us
    ppermute x14, starting transfers between devices, ring_z(): return lax.ppermute(value, 'z', [(i, (i + step) % 8) for i in range(8)])  26.5 us
    pallas_call x2, Pallas kernels, project(): pl.pallas_call(functools.partial(project_kernel, len(pieces)), out_shape=...  24.8 us
    pallas_call x1, Pallas kernels, finish(): pl.pallas_call(finish_kernel, out_shape=jax.ShapeDtypeStruct((16, 128, 25...  16 us
    ppermute x1, starting transfers between devices, swap_roles(): return lax.ppermute(value, ('c', 'xh'), [(0, 0), (1, 2), (2, 1), (3, 3)])  10.6 us
    all_gather x1, waiting for transfers between devices, gather_weight(): lax.all_gather(weight, ('y', 'xl', 'c', 'xh'), axis=0, tiled=False, axis_...  10.3 us
    ppermute x14, waiting for transfers between devices, ring_z(): return lax.ppermute(value, 'z', [(i, (i + step) % 8) for i in range(8)])  8.88 us
    ppermute x6, starting transfers between devices, swap_core(): return lax.ppermute(value, 'c', [(0, 1), (1, 0)])  8.18 us
  transfers between devices with their start and end apart: 23, of which 8 were waited for; matrix products, arithmetic and copies ran while one was open for 3% of the time, Pallas kernels for 14%

profile of v5, /device:TPU:1, one launch (start us, length us, event | category | flops | bytes accessed | tf_op | source)
XLA Modules:
  0.0 180.4 jit_solution(248644507219383551)
XLA Ops:
  6.5 1.9 %pad_maximum_fusion = bf16[256,768]{1,0:T(8,128)(2,1)} fusion(bf16[256,256]{1,0:T(8,128)(2,1)} %param.8, bf16[256,256]{1,0:T(8,128)(2,1)} %param.7, bf16[256,256]{1,0:T(8,128)(2,1)} %param.6), kind=kLoop, calls=%fused_computation.9 | loop fusion | flops 1179648 | bytes 786432 | tf_op jit(solution)/shard_map/concatenate | solution.py:251
  8.5 1.5 multiply_reduce_fusion
  10.0 0.1 rsqrt.12
  10.1 0.3 multiply_convert_fusion
  10.4 3.3 %collective-permute-start.1 = (bf16[64,4096]{1,0:T(8,128)(2,1)S(1)}, bf16[64,4096]{1,0:T(8,128)(2,1)S(1)}, u32[]{:S(2)}, u32[]{:S(2)}) collective-permute-start(bf16[64,4096]{1,0:T(8,128)(2,1)S(1)} %dynamic-slice_bitcast_fusion.1), channel_id=1, source_target_pairs={{0,16},{16,0},{1,17},{17,1},{2,18},{18,2},{3,19},{19,3},{4,20},{20... | collective-permute-start | bytes 1572872 | tf_op jit(solution)/shard_map/ppermute | solution.py:17
  13.7 1.5 collective-permute-done.1
  15.3 0.1 bitcast_select_fusion.2
  15.4 1.1 collective-permute-start.5
  16.4 1.6 collective-permute-start.2
  18.1 3.9 %collective-permute-start.6 = (bf16[64,4096]{1,0:T(8,128)(2,1)S(1)}, bf16[64,4096]{1,0:T(8,128)(2,1)S(1)}, u32[]{:S(2)}, u32[]{:S(2)}) collective-permute-start(bf16[64,4096]{1,0:T(8,128)(2,1)S(1)} %get-tuple-element.16.refs_0_), channel_id=1, source_target_pairs={{0,7},{1,0},{2,1},{3,2},{4,3},{5,4},{6,5},{7,6},{8,15},{9,8},{10,9... | collective-permute-start | bytes 1572872 | tf_op jit(solution)/shard_map/ppermute | solution.py:35
  22.0 8.1 %collective-permute-done.5.refs_1_ = bf16[64,4096]{1,0:T(8,128)(2,1)S(1)} collective-permute-done((bf16[64,4096]{1,0:T(8,128)(2,1)S(1)}, bf16[64,4096]{1,0:T(8,128)(2,1)S(1)}, u32[]{:S(2)}, u32[]{:S(2)}) %collective-permute-start.5) | collective-permute-done | bytes 524320 | tf_op jit(solution)/shard_map/ppermute | solution.py:21
  30.1 5.0 %collective-permute-start.8 = (bf16[64,4096]{1,0:T(8,128)(2,1)S(1)}, bf16[64,4096]{1,0:T(8,128)(2,1)S(1)}, u32[]{:S(2)}, u32[]{:S(2)}) collective-permute-start(bf16[64,4096]{1,0:T(8,128)(2,1)S(1)} %collective-permute-done.5.refs_1_), channel_id=1, source_target_pairs={{0,7},{1,0},{2,1},{3,2},{4,3},{5,4},{6,5},{7,6},{8,15},{9,8},{10,9... | collective-permute-start | bytes 1572872 | tf_op jit(solution)/shard_map/ppermute | solution.py:35
  35.1 0.1 collective-permute-start.3
  35.2 2.7 %collective-permute-start.14 = (bf16[64,4096]{1,0:T(8,128)(2,1)S(1)}, bf16[64,4096]{1,0:T(8,128)(2,1)}, u32[]{:S(2)}, u32[]{:S(2)}) collective-permute-start(bf16[64,4096]{1,0:T(8,128)(2,1)S(1)} %collective-permute-done.6.refs_3_), channel_id=1, source_target_pairs={{0,7},{1,0},{2,1},{3,2},{4,3},{5,4},{6,5},{7,6},{8,15},{9,8},{10,9... | collective-permute-start | bytes 1572872 | tf_op jit(solution)/shard_map/ppermute | solution.py:35
  37.9 6.8 %collective-permute-done.8.refs_2_ = bf16[64,4096]{1,0:T(8,128)(2,1)S(1)} collective-permute-done((bf16[64,4096]{1,0:T(8,128)(2,1)S(1)}, bf16[64,4096]{1,0:T(8,128)(2,1)S(1)}, u32[]{:S(2)}, u32[]{:S(2)}) %collective-permute-start.8) | collective-permute-done | bytes 524320 | tf_op jit(solution)/shard_map/ppermute | solution.py:35
  44.6 3.4 %collective-permute-start.9 = (bf16[64,4096]{1,0:T(8,128)(2,1)S(1)}, bf16[64,4096]{1,0:T(8,128)(2,1)}, u32[]{:S(2)}, u32[]{:S(2)}) collective-permute-start(bf16[64,4096]{1,0:T(8,128)(2,1)S(1)} %collective-permute-done.8.refs_2_), channel_id=1, source_target_pairs={{0,7},{1,0},{2,1},{3,2},{4,3},{5,4},{6,5},{7,6},{8,15},{9,8},{10,9... | collective-permute-start | bytes 1572872 | tf_op jit(solution)/shard_map/ppermute | solution.py:35
  48.0 10.6 %collective-permute-start = (f32[2,2048]{1,0:T(2,128)S(1)}, f32[2,2048]{1,0:T(2,128)S(1)}, u32[]{:S(2)}, u32[]{:S(2)}) collective-permute-start(f32[2,2048]{1,0:T(2,128)S(1)} %bitcast.50), channel_id=1, source_target_pairs={{0,0},{8,16},{16,8},{24,24},{1,1},{9,17},{17,9},{25,25},{2,2},{10,... | collective-permute-start | bytes 49160 | tf_op jit(solution)/shard_map/ppermute | solution.py:25
  58.8 0.6 stack.67.refs_1_.chunk_ref
  59.4 1.0 collective-permute-done
  60.5 1.2 reduce-window.6
  61.7 0.2 slice_reduce_fusion
  61.9 0.1 collective-permute-start.4
  62.0 3.0 %collective-permute-start.16 = (bf16[64,4096]{1,0:T(8,128)(2,1)}, bf16[64,4096]{1,0:T(8,128)(2,1)}, u32[]{:S(2)}, u32[]{:S(2)}) collective-permute-start(bf16[64,4096]{1,0:T(8,128)(2,1)} %collective-permute-done.14.refs_0_), channel_id=1, source_target_pairs={{0,7},{1,0},{2,1},{3,2},{4,3},{5,4},{6,5},{7,6},{8,15},{9,8},{10,9... | collective-permute-start | bytes 1572872 | tf_op jit(solution)/shard_map/ppermute | solution.py:35
  65.0 2.1 %collective-permute-done.9.refs_6_ = bf16[64,4096]{1,0:T(8,128)(2,1)} collective-permute-done((bf16[64,4096]{1,0:T(8,128)(2,1)S(1)}, bf16[64,4096]{1,0:T(8,128)(2,1)}, u32[]{:S(2)}, u32[]{:S(2)}) %collective-permute-start.9) | collective-permute-done | bytes 524320 | tf_op jit(solution)/shard_map/ppermute | solution.py:35
  67.1 3.5 %collective-permute-start.10 = (bf16[64,4096]{1,0:T(8,128)(2,1)}, bf16[64,4096]{1,0:T(8,128)(2,1)}, u32[]{:S(2)}, u32[]{:S(2)}) collective-permute-start(bf16[64,4096]{1,0:T(8,128)(2,1)} %collective-permute-done.9.refs_6_), channel_id=1, source_target_pairs={{0,7},{1,0},{2,1},{3,2},{4,3},{5,4},{6,5},{7,6},{8,15},{9,8},{10,9... | collective-permute-start | bytes 1572872 | tf_op jit(solution)/shard_map/ppermute | solution.py:35
  70.6 0.1 broadcast_add_fusion
  70.7 0.4 copy.19
  71.1 0.9 copy.20.refs_2_.refs_4_
  72.0 0.5 after.4.core_ref
  72.6 10.3 %all-gather.3.cloned.1.call-done = bf16[8192,768]{1,0:T(8,128)(2,1)} async-done(((bf16[256,768]{1,0:T(8,128)(2,1)}), bf16[8192,768]{1,0:T(8,128)(2,1)}) %all-gather.3.cloned.1.call-update) | async-done | bytes 12582928 | tf_op jit(solution)/shard_map/all_gather | solution.py:58
  82.9 11.0 %project.2 = (bf16[5,64,768]{2,1,0:T(8,128)(2,1)}, bf16[5,64,768]{2,1,0:T(8,128)(2,1)}) custom-call(s32[1]{0:T(128)} %after.4.core_ref, bf16[64,4096]{1,0:T(8,128)(2,1)} %copy-done.2, bf16[64,4096]{1,0:T(8,128)(2,1)} %copy-done.4, bf16[64,4096]{1,0:T(8,128)(2,1)} %copy-done.5, bf16[64,4096]{1,0:T(8,128)(2,1)} %copy-done.6, ...), custom_call_target="tpu_custom_call" | custom-call | flops 4026531840 | bytes 17825792 | tf_op jit(solution)/shard_map/project/pallas_call | solution.py:100
  93.9 3.1 %collective-permute-start.11 = (bf16[64,4096]{1,0:T(8,128)(2,1)}, bf16[64,4096]{1,0:T(8,128)(2,1)S(1)}, u32[]{:S(2)}, u32[]{:S(2)}) collective-permute-start(bf16[64,4096]{1,0:T(8,128)(2,1)} %after.6.refs_8_), channel_id=1, source_target_pairs={{0,7},{1,0},{2,1},{3,2},{4,3},{5,4},{6,5},{7,6},{8,15},{9,8},{10,9... | collective-permute-start | bytes 1572872 | tf_op jit(solution)/shard_map/ppermute | solution.py:35
  97.0 13.8 %project.3 = (bf16[9,64,768]{2,1,0:T(8,128)(2,1)}, bf16[9,64,768]{2,1,0:T(8,128)(2,1)}) custom-call(s32[1]{0:T(128)} %after.4.core_ref, bf16[64,4096]{1,0:T(8,128)(2,1)} %collective-permute-done.14.refs_0_, bf16[64,4096]{1,0:T(8,128)(2,1)} %collective-permute-done.15.refs_1_, bf16[64,4096]{1,0:T(8,128)(2,1)} %copy-done.12, bf16[64,4096]{1,0:T(8,128)(2,1)} %after.5.refs_3_, ...), custom_call_target="tpu_custom_call" | custom-call | flops 7247757312 | bytes 22020096 | tf_op jit(solution)/shard_map/project/pallas_call | solution.py:100
  110.8 0.5 collective-permute-start.20
  111.4 0.1 collective-permute-start.13
  111.5 1.3 collective-permute-start.12
  112.7 2.9 %collective-permute-done.19.refs_2_ = bf16[5,64,768]{2,1,0:T(8,128)(2,1)S(1)} collective-permute-done((bf16[5,64,768]{2,1,0:T(8,128)(2,1)}, bf16[5,64,768]{2,1,0:T(8,128)(2,1)S(1)}, u32[]{:S(2)}, u32[]{:S(2)}) %collective-permute-start.19) | collective-permute-done | bytes 491552 | tf_op jit(solution)/shard_map/ppermute | solution.py:17
  115.7 0.7 copy-done.11
  116.4 0.3 copy-done.3
  116.7 0.2 copy-done.9
  116.9 0.2 copy-done.10
  117.1 16.0 %finish.1 = bf16[16,128,256]{2,1,0:T(8,128)(2,1)} custom-call(s32[16]{0:T(128)} %stack.67.refs_1_.chunk_ref, s32[1]{0:T(128)} %after.4.core_ref, bf16[64,4096]{1,0:T(8,128)(2,1)} %copy-done.8, bf16[64,4096]{1,0:T(8,128)(2,1)} %copy-done.7, bf16[64,4096]{1,0:T(8,128)(2,1)} %copy-done.10, bf16[64,4096]{1,0:T(8,128)(2,1)} %copy-done.9, ...), custom_call_target="tpu_custom_call" | custom-call | flops 2415919104 | bytes 12582912 | tf_op jit(solution)/shard_map/finish/pallas_call | solution.py:221
  133.1 33.8 %all_to_all.5 = bf16[16,128,256]{2,1,0:T(8,128)(2,1)S(1)} all-to-all(bf16[16,128,256]{2,1,0:T(8,128)(2,1)} %finish.1), channel_id=1, replica_groups=mesh['y'=4,'xl'=2,'c'=2,'xh'=2,'z'=8] {'xh','z'}, dimensions={0} | all-to-all | bytes 2097152 | tf_op jit(solution)/shard_map/all_to_all | solution.py:288
  166.9 2.9 %collective-permute-start.21 = (bf16[8,128,256]{2,1,0:T(8,128)(2,1)S(1)}, bf16[8,128,256]{2,1,0:T(8,128)(2,1)S(1)}, u32[]{:S(2)}, u32[]{:S(2)}) collective-permute-start(bf16[8,128,256]{2,1,0:T(8,128)(2,1)S(1)} %dynamic-slice_bitcast_fusion), channel_id=1, source_target_pairs={{0,16},{16,0},{1,17},{17,1},{2,18},{18,2},{3,19},{19,3},{4,20},{20... | collective-permute-start | bytes 1572872 | tf_op jit(solution)/shard_map/ppermute | solution.py:17
  169.8 1.5 collective-permute-done.21
  171.5 0.1 maximum_bitcast_fusion
  171.6 0.7 copy.22
  172.2 1.3 copy.23
  (57 shorter events, 0.4 us)
Async XLA Ops:
  6.5 3.5 %copy-start.1 = (bf16[1,128,4096]{2,1,0:T(8,128)(2,1)S(1)}, bf16[1,128,4096]{2,1,0:T(8,128)(2,1)}, u32[]{:S(2)}) copy-start(bf16[1,128,4096]{2,1,0:T(8,128)(2,1)} %param.5) | copy-start | bytes 3145732
  6.5 76.3 %all-gather.3.cloned.1.call-start = ((), (), s32[]{:S(2)}) async-start(), calls=%async_computation.1 | async-start | bytes 12976128 | tf_op jit(solution)/shard_map/all_gather | solution.py:58
  10.3 37.7 %copy-start.13 = (f32[1,2,2048]{2,1,0:T(2,128)S(1)}, f32[1,2,2048]{2,1,0:T(2,128)}, u32[]{:S(2)}) copy-start(f32[1,2,2048]{2,1,0:T(2,128)} %param.9) | copy-start | bytes 49156
  10.4 4.9 %collective-permute-start.1 = (bf16[64,4096]{1,0:T(8,128)(2,1)S(1)}, bf16[64,4096]{1,0:T(8,128)(2,1)S(1)}, u32[]{:S(2)}, u32[]{:S(2)}) collective-permute-start(bf16[64,4096]{1,0:T(8,128)(2,1)S(1)} %dynamic-slice_bitcast_fusion.1), channel_id=1, source_target_pairs={{0,16},{16,0},{1,17},{17,1},{2,18},{18,2},{3,19},{19,3},{4,20},{20... | collective-permute-start | bytes 1572872 | tf_op jit(solution)/shard_map/ppermute | solution.py:17
  15.3 67.5 %copy-start.2 = (bf16[64,4096]{1,0:T(8,128)(2,1)}, bf16[64,4096]{1,0:T(8,128)(2,1)S(1)}, u32[]{:S(2)}) copy-start(bf16[64,4096]{1,0:T(8,128)(2,1)S(1)} %get-tuple-element.16.refs_0_) | copy-start | bytes 1572868
  15.4 14.7 %collective-permute-start.5 = (bf16[64,4096]{1,0:T(8,128)(2,1)S(1)}, bf16[64,4096]{1,0:T(8,128)(2,1)S(1)}, u32[]{:S(2)}, u32[]{:S(2)}) collective-permute-start(bf16[64,4096]{1,0:T(8,128)(2,1)S(1)} %get-tuple-element.15), channel_id=1, source_target_pairs={{0,8},{8,0},{1,9},{9,1},{2,10},{10,2},{3,11},{11,3},{4,12},{12,4},... | collective-permute-start | bytes 1572872 | tf_op jit(solution)/shard_map/ppermute | solution.py:21
  16.4 18.6 %collective-permute-start.2 = (bf16[64,4096]{1,0:T(8,128)(2,1)S(1)}, bf16[64,4096]{1,0:T(8,128)(2,1)S(1)}, u32[]{:S(2)}, u32[]{:S(2)}) collective-permute-start(bf16[64,4096]{1,0:T(8,128)(2,1)S(1)} %get-tuple-element.16.refs_0_), channel_id=1, source_target_pairs={{0,1},{1,2},{2,3},{3,4},{4,5},{5,6},{6,7},{7,0},{8,9},{9,10},{10,1... | collective-permute-start | bytes 1572872 | tf_op jit(solution)/shard_map/ppermute | solution.py:35
  18.1 17.1 %collective-permute-start.6 = (bf16[64,4096]{1,0:T(8,128)(2,1)S(1)}, bf16[64,4096]{1,0:T(8,128)(2,1)S(1)}, u32[]{:S(2)}, u32[]{:S(2)}) collective-permute-start(bf16[64,4096]{1,0:T(8,128)(2,1)S(1)} %get-tuple-element.16.refs_0_), channel_id=1, source_target_pairs={{0,7},{1,0},{2,1},{3,2},{4,3},{5,4},{6,5},{7,6},{8,15},{9,8},{10,9... | collective-permute-start | bytes 1572872 | tf_op jit(solution)/shard_map/ppermute | solution.py:35
  30.1 52.8 %copy-start.4 = (bf16[64,4096]{1,0:T(8,128)(2,1)}, bf16[64,4096]{1,0:T(8,128)(2,1)S(1)}, u32[]{:S(2)}) copy-start(bf16[64,4096]{1,0:T(8,128)(2,1)S(1)} %collective-permute-done.5.refs_1_) | copy-start | bytes 1572868
  30.1 14.5 %collective-permute-start.8 = (bf16[64,4096]{1,0:T(8,128)(2,1)S(1)}, bf16[64,4096]{1,0:T(8,128)(2,1)S(1)}, u32[]{:S(2)}, u32[]{:S(2)}) collective-permute-start(bf16[64,4096]{1,0:T(8,128)(2,1)S(1)} %collective-permute-done.5.refs_1_), channel_id=1, source_target_pairs={{0,7},{1,0},{2,1},{3,2},{4,3},{5,4},{6,5},{7,6},{8,15},{9,8},{10,9... | collective-permute-start | bytes 1572872 | tf_op jit(solution)/shard_map/ppermute | solution.py:35
  35.1 13.0 %collective-permute-start.15 = (bf16[64,4096]{1,0:T(8,128)(2,1)S(1)}, bf16[64,4096]{1,0:T(8,128)(2,1)}, u32[]{:S(2)}, u32[]{:S(2)}) collective-permute-start(bf16[64,4096]{1,0:T(8,128)(2,1)S(1)} %collective-permute-done.5.refs_1_), channel_id=1, source_target_pairs={{0,1},{1,2},{2,3},{3,4},{4,5},{5,6},{6,7},{7,0},{8,9},{9,10},{10,1... | collective-permute-start | bytes 1572872 | tf_op jit(solution)/shard_map/ppermute | solution.py:35
  35.1 47.8 %copy-start.5 = (bf16[64,4096]{1,0:T(8,128)(2,1)}, bf16[64,4096]{1,0:T(8,128)(2,1)S(1)}, u32[]{:S(2)}) copy-start(bf16[64,4096]{1,0:T(8,128)(2,1)S(1)} %collective-permute-done.2.refs_2_) | copy-start | bytes 1572868
  35.1 26.8 %collective-permute-start.3 = (bf16[64,4096]{1,0:T(8,128)(2,1)S(1)}, bf16[64,4096]{1,0:T(8,128)(2,1)}, u32[]{:S(2)}, u32[]{:S(2)}) collective-permute-start(bf16[64,4096]{1,0:T(8,128)(2,1)S(1)} %collective-permute-done.2.refs_2_), channel_id=1, source_target_pairs={{0,1},{1,2},{2,3},{3,4},{4,5},{5,6},{6,7},{7,0},{8,9},{9,10},{10,1... | collective-permute-start | bytes 1572872 | tf_op jit(solution)/shard_map/ppermute | solution.py:35
  35.2 47.7 %copy-start.6 = (bf16[64,4096]{1,0:T(8,128)(2,1)}, bf16[64,4096]{1,0:T(8,128)(2,1)S(1)}, u32[]{:S(2)}) copy-start(bf16[64,4096]{1,0:T(8,128)(2,1)S(1)} %collective-permute-done.6.refs_3_) | copy-start | bytes 1572868
  35.2 26.8 %collective-permute-start.14 = (bf16[64,4096]{1,0:T(8,128)(2,1)S(1)}, bf16[64,4096]{1,0:T(8,128)(2,1)}, u32[]{:S(2)}, u32[]{:S(2)}) collective-permute-start(bf16[64,4096]{1,0:T(8,128)(2,1)S(1)} %collective-permute-done.6.refs_3_), channel_id=1, source_target_pairs={{0,7},{1,0},{2,1},{3,2},{4,3},{5,4},{6,5},{7,6},{8,15},{9,8},{10,9... | collective-permute-start | bytes 1572872 | tf_op jit(solution)/shard_map/ppermute | solution.py:35
  44.6 26.0 %copy-start.12 = (bf16[64,4096]{1,0:T(8,128)(2,1)}, bf16[64,4096]{1,0:T(8,128)(2,1)S(1)}, u32[]{:S(2)}) copy-start(bf16[64,4096]{1,0:T(8,128)(2,1)S(1)} %collective-permute-done.8.refs_2_) | copy-start | bytes 1572868
  44.6 22.5 %collective-permute-start.9 = (bf16[64,4096]{1,0:T(8,128)(2,1)S(1)}, bf16[64,4096]{1,0:T(8,128)(2,1)}, u32[]{:S(2)}, u32[]{:S(2)}) collective-permute-start(bf16[64,4096]{1,0:T(8,128)(2,1)S(1)} %collective-permute-done.8.refs_2_), channel_id=1, source_target_pairs={{0,7},{1,0},{2,1},{3,2},{4,3},{5,4},{6,5},{7,6},{8,15},{9,8},{10,9... | collective-permute-start | bytes 1572872 | tf_op jit(solution)/shard_map/ppermute | solution.py:35
  48.0 22.6 %collective-permute-start.17 = (bf16[64,4096]{1,0:T(8,128)(2,1)}, bf16[64,4096]{1,0:T(8,128)(2,1)}, u32[]{:S(2)}, u32[]{:S(2)}) collective-permute-start(bf16[64,4096]{1,0:T(8,128)(2,1)} %collective-permute-done.15.refs_1_), channel_id=1, source_target_pairs={{0,1},{1,2},{2,3},{3,4},{4,5},{5,6},{6,7},{7,0},{8,9},{9,10},{10,1... | collective-permute-start | bytes 1572872 | tf_op jit(solution)/shard_map/ppermute | solution.py:35
  48.0 12.4 %collective-permute-start = (f32[2,2048]{1,0:T(2,128)S(1)}, f32[2,2048]{1,0:T(2,128)S(1)}, u32[]{:S(2)}, u32[]{:S(2)}) collective-permute-start(f32[2,2048]{1,0:T(2,128)S(1)} %bitcast.50), channel_id=1, source_target_pairs={{0,0},{8,16},{16,8},{24,24},{1,1},{9,17},{17,9},{25,25},{2,2},{10,... | collective-permute-start | bytes 49160 | tf_op jit(solution)/shard_map/ppermute | solution.py:25
  61.9 35.1 %collective-permute-start.4 = (bf16[64,4096]{1,0:T(8,128)(2,1)}, bf16[64,4096]{1,0:T(8,128)(2,1)}, u32[]{:S(2)}, u32[]{:S(2)}) collective-permute-start(bf16[64,4096]{1,0:T(8,128)(2,1)} %collective-permute-done.3.refs_4_), channel_id=1, source_target_pairs={{0,1},{1,2},{2,3},{3,4},{4,5},{5,6},{6,7},{7,0},{8,9},{9,10},{10,1... | collective-permute-start | bytes 1572872 | tf_op jit(solution)/shard_map/ppermute | solution.py:35
  62.0 35.0 %collective-permute-start.16 = (bf16[64,4096]{1,0:T(8,128)(2,1)}, bf16[64,4096]{1,0:T(8,128)(2,1)}, u32[]{:S(2)}, u32[]{:S(2)}) collective-permute-start(bf16[64,4096]{1,0:T(8,128)(2,1)} %collective-permute-done.14.refs_0_), channel_id=1, source_target_pairs={{0,7},{1,0},{2,1},{3,2},{4,3},{5,4},{6,5},{7,6},{8,15},{9,8},{10,9... | collective-permute-start | bytes 1572872 | tf_op jit(solution)/shard_map/ppermute | solution.py:35
  67.1 26.8 %collective-permute-start.10 = (bf16[64,4096]{1,0:T(8,128)(2,1)}, bf16[64,4096]{1,0:T(8,128)(2,1)}, u32[]{:S(2)}, u32[]{:S(2)}) collective-permute-start(bf16[64,4096]{1,0:T(8,128)(2,1)} %collective-permute-done.9.refs_6_), channel_id=1, source_target_pairs={{0,7},{1,0},{2,1},{3,2},{4,3},{5,4},{6,5},{7,6},{8,15},{9,8},{10,9... | collective-permute-start | bytes 1572872 | tf_op jit(solution)/shard_map/ppermute | solution.py:35
  70.6 26.4 %collective-permute-start.18 = (bf16[64,4096]{1,0:T(8,128)(2,1)}, bf16[64,4096]{1,0:T(8,128)(2,1)}, u32[]{:S(2)}, u32[]{:S(2)}) collective-permute-start(bf16[64,4096]{1,0:T(8,128)(2,1)} %collective-permute-done.17.refs_5_), channel_id=1, source_target_pairs={{0,1},{1,2},{2,3},{3,4},{4,5},{5,6},{6,7},{7,0},{8,9},{9,10},{10,1... | collective-permute-start | bytes 1572872 | tf_op jit(solution)/shard_map/ppermute | solution.py:35
  71.1 1.0 copy-start
  93.9 17.5 %collective-permute-start.11 = (bf16[64,4096]{1,0:T(8,128)(2,1)}, bf16[64,4096]{1,0:T(8,128)(2,1)S(1)}, u32[]{:S(2)}, u32[]{:S(2)}) collective-permute-start(bf16[64,4096]{1,0:T(8,128)(2,1)} %after.6.refs_8_), channel_id=1, source_target_pairs={{0,7},{1,0},{2,1},{3,2},{4,3},{5,4},{6,5},{7,6},{8,15},{9,8},{10,9... | collective-permute-start | bytes 1572872 | tf_op jit(solution)/shard_map/ppermute | solution.py:35
  97.0 14.5 %collective-permute-start.7 = (bf16[64,4096]{1,0:T(8,128)(2,1)}, bf16[64,4096]{1,0:T(8,128)(2,1)S(1)}, u32[]{:S(2)}, u32[]{:S(2)}) collective-permute-start(bf16[64,4096]{1,0:T(8,128)(2,1)} %after.5.refs_3_), channel_id=1, source_target_pairs={{0,1},{1,2},{2,3},{3,4},{4,5},{5,6},{6,7},{7,0},{8,9},{9,10},{10,1... | collective-permute-start | bytes 1572872 | tf_op jit(solution)/shard_map/ppermute | solution.py:35
  110.8 4.8 %collective-permute-start.20 = (bf16[9,64,768]{2,1,0:T(8,128)(2,1)}, bf16[9,64,768]{2,1,0:T(8,128)(2,1)S(1)}, u32[]{:S(2)}, u32[]{:S(2)}) collective-permute-start(bf16[9,64,768]{2,1,0:T(8,128)(2,1)} %get-tuple-element.12), channel_id=1, source_target_pairs={{0,16},{16,0},{1,17},{17,1},{2,18},{18,2},{3,19},{19,3},{4,20},{20... | collective-permute-start | bytes 2654216 | tf_op jit(solution)/shard_map/ppermute | solution.py:17
  111.3 4.3 %copy-start.7 = (bf16[64,4096]{1,0:T(8,128)(2,1)}, bf16[64,4096]{1,0:T(8,128)(2,1)S(1)}, u32[]{:S(2)}) copy-start(bf16[64,4096]{1,0:T(8,128)(2,1)S(1)} %collective-permute-done.11.two) | copy-start | bytes 1572868
  111.4 4.3 %collective-permute-start.13 = (bf16[64,4096]{1,0:T(8,128)(2,1)S(1)}, bf16[64,4096]{1,0:T(8,128)(2,1)S(1)}, u32[]{:S(2)}, u32[]{:S(2)}) collective-permute-start(bf16[64,4096]{1,0:T(8,128)(2,1)S(1)} %collective-permute-done.11.two), channel_id=1, source_target_pairs={{0,16},{16,0},{1,17},{17,1},{2,18},{18,2},{3,19},{19,3},{4,20},{20... | collective-permute-start | bytes 1572872 | tf_op jit(solution)/shard_map/ppermute | solution.py:17
  111.5 4.2 %copy-start.8 = (bf16[64,4096]{1,0:T(8,128)(2,1)}, bf16[64,4096]{1,0:T(8,128)(2,1)S(1)}, u32[]{:S(2)}) copy-start(bf16[64,4096]{1,0:T(8,128)(2,1)S(1)} %collective-permute-done.7.one) | copy-start | bytes 1572868
  111.5 4.2 %collective-permute-start.12 = (bf16[64,4096]{1,0:T(8,128)(2,1)S(1)}, bf16[64,4096]{1,0:T(8,128)(2,1)S(1)}, u32[]{:S(2)}, u32[]{:S(2)}) collective-permute-start(bf16[64,4096]{1,0:T(8,128)(2,1)S(1)} %collective-permute-done.7.one), channel_id=1, source_target_pairs={{0,16},{16,0},{1,17},{17,1},{2,18},{18,2},{3,19},{19,3},{4,20},{20... | collective-permute-start | bytes 1572872 | tf_op jit(solution)/shard_map/ppermute | solution.py:17
  112.7 2.9 %collective-permute-start.19 = (bf16[5,64,768]{2,1,0:T(8,128)(2,1)}, bf16[5,64,768]{2,1,0:T(8,128)(2,1)S(1)}, u32[]{:S(2)}, u32[]{:S(2)}) collective-permute-start(bf16[5,64,768]{2,1,0:T(8,128)(2,1)} %after.7), channel_id=1, source_target_pairs={{0,16},{16,0},{1,17},{17,1},{2,18},{18,2},{3,19},{19,3},{4,20},{20... | collective-permute-start | bytes 1474568 | tf_op jit(solution)/shard_map/ppermute | solution.py:17
  115.6 0.8 copy-start.11
  115.6 1.1 copy-start.3
  115.6 1.2 copy-start.9
  115.7 1.4 copy-start.10
  166.9 4.5 %collective-permute-start.21 = (bf16[8,128,256]{2,1,0:T(8,128)(2,1)S(1)}, bf16[8,128,256]{2,1,0:T(8,128)(2,1)S(1)}, u32[]{:S(2)}, u32[]{:S(2)}) collective-permute-start(bf16[8,128,256]{2,1,0:T(8,128)(2,1)S(1)} %dynamic-slice_bitcast_fusion), channel_id=1, source_target_pairs={{0,16},{16,0},{1,17},{17,1},{2,18},{18,2},{3,19},{19,3},{4,20},{20... | collective-permute-start | bytes 1572872 | tf_op jit(solution)/shard_map/ppermute | solution.py:17
Sparse Core Ops, SparseCore 0:
  9.9 72.9 all-gather.2
